TPU v7x, 32 devices: a whole 2x2x4 slice. The times are simulated.
32 devices in a mesh: grp: 8 (over y, x, core), dp: 4 (over z).
Axes of the slice: x: 2, y: 2, z: 4, core: 2. Of those that a mesh axis runs over, the one named last changes fastest.
Arguments:
- latents: bfloat16 [64, 256, 1152], P(('grp', 'dp')), may hold values from -6 to 6
- cotangent: bfloat16 [64, 256, 1152], P(('grp', 'dp')), may hold values from -6 to 6
- bands: int32 [64], P(('grp', 'dp')), may hold values from 0 to 15
- labels: int32 [64], P(('grp', 'dp')), may hold values from 0 to 999
- kept: int32 [64, 128], P(('grp', 'dp')), may hold values from 0 to 255, as said below
- band_counts: int32 [8], P('grp'), may hold values from 1 to 8, as said below
- time_table: bfloat16 [16, 1152], P(None, 'grp'), may hold values from -6 to 6
- class_table: bfloat16 [1000, 1152], P(None, 'grp'), may hold values from -6 to 6
- w_ada: bfloat16 [1152, 6912], P(None, 'grp'), may hold values from -0.1875 to 0.1875
- b_ada: bfloat16 [6912], P('grp'), may hold values from -3 to 3
- w_qkv: bfloat16 [1152, 3456], P(None, 'grp'), may hold values from -0.1875 to 0.1875
- qv_bias: bfloat16 [2304], P('grp'), may hold values from -2 to 2
- w_proj: bfloat16 [1152, 1152], P('grp'), may hold values from -0.75 to 0.75
- b_proj: bfloat16 [1152], P('grp'), may hold values from -2 to 2
- w_fc1: bfloat16 [1152, 4608], P(None, 'grp'), may hold values from -0.1875 to 0.1875
- b_fc1: bfloat16 [4608], P('grp'), may hold values from -2 to 2
- w_fc2: bfloat16 [4608, 1152], P('grp'), may hold values from -0.1875 to 0.1875
- b_fc2: bfloat16 [1152], P('grp'), may hold values from -2 to 2
Outputs:
- block_out: bfloat16 [64, 256, 1152], P(('grp', 'dp'))
- latents_grad: bfloat16 [64, 256, 1152], P(('grp', 'dp'))
- time_table_grad: float32 [16, 1152], P(None, 'grp')
- class_table_grad: float32 [1000, 1152], P(None, 'grp')
- w_ada_grad: float32 [1152, 6912], P(None, 'grp')
- b_ada_grad: float32 [6912], P('grp')
- w_qkv_grad: float32 [1152, 3456], P(None, 'grp')
- qv_bias_grad: float32 [2304], P('grp')
- w_proj_grad: float32 [1152, 1152], P('grp')
- b_proj_grad: float32 [1152], P('grp')
- w_fc1_grad: float32 [1152, 4608], P(None, 'grp')
- b_fc1_grad: float32 [4608], P('grp')
- w_fc2_grad: float32 [4608, 1152], P('grp')
- b_fc2_grad: float32 [1152], P('grp')
Inputs may be any that keep to these rules, and one draw needn't show every extreme that they name: `kept`: each row holds 128 different token positions in rising order. `band_counts`: some group has all 8 slots in use; slots below a group's count are in use.
All inputs are finite; a program needn't handle non-finite values.
Results may differ from a plain program's by a relative error of at most 0.018.
The roundings to bfloat16 on the way count: a program that leaves them out, or rounds other values in their place, can miss the bound.
Values may be sent and summed in bfloat16 or wider, within the bound.
A program may use at most 320 MiB of HBM per device.

v0:
```python
import jax
import jax.numpy as jnp
from jax import lax
from jax.sharding import PartitionSpec as P

HEADS = 16
HEAD_DIM = 72


EPS = 1e-06
HIGH = lax.Precision.HIGHEST


def modulate(values, shift, scale):
    mean = jnp.mean(values, -1, keepdims=True)
    cent = values - mean
    var = jnp.mean(cent * cent, -1, keepdims=True)
    return cent * lax.rsqrt(var + EPS) * (1.0 + scale[:, None, :]) + shift[:, None, :]


def product(left, right):
    return jnp.einsum("btd,de->bte", left, right, preferred_element_type=jnp.float32)


def weight_term(left, right):
    return jnp.einsum("btd,bte->de", left, right, preferred_element_type=jnp.float32)


def core(weights, tokens, mod):
    w_qkv, qv_bias, w_proj, b_proj, w_fc1, b_fc1, w_fc2, b_fc2 = weights
    count, length, width = tokens.shape
    shift1, scale1, gate1, shift2, scale2, gate2 = jnp.split(mod, 6, -1)
    h1 = modulate(tokens, shift1, scale1).astype(jnp.bfloat16)
    bias = jnp.concatenate(
        [
            qv_bias[:width].astype(jnp.float32),
            jnp.zeros((width,), jnp.float32),
            qv_bias[width:].astype(jnp.float32),
        ]
    )
    qkv = (product(h1, w_qkv) + bias).astype(jnp.bfloat16)
    query = qkv[..., :width].reshape(count, length, HEADS, HEAD_DIM)
    keys = qkv[..., width : 2 * width].reshape(count, length, HEADS, HEAD_DIM)
    values = qkv[..., 2 * width :].reshape(count, length, HEADS, HEAD_DIM)
    scores = jnp.einsum(
        "bqhd,bkhd->bhqk", query, keys, preferred_element_type=jnp.float32
    ) * HEAD_DIM ** (-0.5)
    total = jax.scipy.special.logsumexp(scores, axis=-1, keepdims=True)
    probs_full = jnp.exp(scores - total)
    probs = probs_full.astype(jnp.bfloat16)
    att = (
        jnp.einsum("bhqk,bkhd->bqhd", probs, values, preferred_element_type=jnp.float32)
        .reshape(count, length, width)
        .astype(jnp.bfloat16)
    )
    proj = product(att, w_proj) + b_proj.astype(jnp.float32)
    mixed = tokens + gate1[:, None, :] * proj
    h2 = modulate(mixed, shift2, scale2).astype(jnp.bfloat16)
    pre = product(h2, w_fc1) + b_fc1.astype(jnp.float32)
    act = jax.nn.gelu(pre, approximate=True).astype(jnp.bfloat16)
    mlp = product(act, w_fc2) + b_fc2.astype(jnp.float32)
    result = mixed + gate2[:, None, :] * mlp
    saved = (h1, query, keys, values, probs_full, probs, att, proj, mixed, h2, pre, act, mlp)
    return (result, saved)


def body(
    latents,
    cotangent,
    bands,
    labels,
    kept,
    band_counts,
    time_table,
    class_table,
    w_ada,
    b_ada,
    w_qkv,
    qv_bias,
    w_proj,
    b_proj,
    w_fc1,
    b_fc1,
    w_fc2,
    b_fc2,
):
    gathered = (
        lax.all_gather(time_table, "grp", axis=1, tiled=True),
        lax.all_gather(class_table, "grp", axis=1, tiled=True),
        lax.all_gather(w_ada, "grp", axis=1, tiled=True),
        lax.all_gather(b_ada, "grp", axis=0, tiled=True),
        lax.all_gather(w_qkv, "grp", axis=1, tiled=True),
        lax.all_gather(qv_bias, "grp", axis=0, tiled=True),
        lax.all_gather(w_proj, "grp", axis=0, tiled=True),
        lax.all_gather(b_proj, "grp", axis=0, tiled=True),
        lax.all_gather(w_fc1, "grp", axis=1, tiled=True),
        lax.all_gather(b_fc1, "grp", axis=0, tiled=True),
        lax.all_gather(w_fc2, "grp", axis=0, tiled=True),
        lax.all_gather(b_fc2, "grp", axis=0, tiled=True),
    )
    time_full, class_full, ada_full, ada_bias = (gathered[0], gathered[1], gathered[2], gathered[3])
    samples = latents.shape[0]
    width = latents.shape[2]
    slot = lax.axis_index("dp") * samples + jnp.arange(samples, dtype=jnp.int32)
    group_count = band_counts[0]
    weight = jnp.where(slot < group_count, 1.0, 0.0).astype(jnp.float32) / group_count.astype(
        jnp.float32
    )
    band_hot = (bands[:, None] == jnp.arange(time_full.shape[0], dtype=jnp.int32)[None, :]).astype(
        jnp.float32
    )
    class_hot = (
        labels[:, None] == jnp.arange(class_full.shape[0], dtype=jnp.int32)[None, :]
    ).astype(jnp.float32)
    cond = jnp.dot(band_hot, time_full.astype(jnp.float32), precision=HIGH) + jnp.dot(
        class_hot, class_full.astype(jnp.float32), precision=HIGH
    )
    cvec = jax.nn.silu(cond).astype(jnp.bfloat16)
    mod = jnp.dot(cvec, ada_full, preferred_element_type=jnp.float32) + ada_bias.astype(jnp.float32)
    rows = jnp.arange(samples, dtype=jnp.int32)[:, None]
    tokens = jnp.take_along_axis(latents, kept[:, :, None], 1).astype(jnp.float32)
    result, unused = core(tuple(gathered[4:]), tokens, mod)
    block_out = latents.at[rows, kept].set(result.astype(jnp.bfloat16))
    fetched = (
        lax.all_gather(w_ada, "grp", axis=1, tiled=True),
        lax.all_gather(w_qkv, "grp", axis=1, tiled=True),
        lax.all_gather(qv_bias, "grp", axis=0, tiled=True),
        lax.all_gather(w_proj, "grp", axis=0, tiled=True),
        lax.all_gather(b_proj, "grp", axis=0, tiled=True),
        lax.all_gather(w_fc1, "grp", axis=1, tiled=True),
        lax.all_gather(b_fc1, "grp", axis=0, tiled=True),
        lax.all_gather(w_fc2, "grp", axis=0, tiled=True),
        lax.all_gather(b_fc2, "grp", axis=0, tiled=True),
    )
    ada_full = fetched[0]
    back = tuple(fetched[1:])
    qkv_full, unused_bias, proj_full, unused_pbias, fc1_full, unused_b1, fc2_full, unused_b2 = back
    result, saved = core(back, tokens, mod)
    h1, query, keys, values, probs_full, probs, att, proj, mixed, h2, pre, act, mlp = saved
    shift1, scale1, gate1, shift2, scale2, gate2 = jnp.split(mod, 6, -1)
    weighted = cotangent.astype(jnp.float32) * weight[:, None, None]
    grad_out = jnp.take_along_axis(weighted, kept[:, :, None], 1)
    grad_mlp = (gate2[:, None, :] * grad_out).astype(jnp.bfloat16)
    grad_gate2 = jnp.sum(grad_out * mlp, 1)
    fc2_grad = weight_term(act, grad_mlp)
    fc2_bias_grad = jnp.sum(grad_mlp.astype(jnp.float32), (0, 1))
    grad_act = jnp.einsum("bte,de->btd", grad_mlp, fc2_full, preferred_element_type=jnp.float32)
    unused_pre, gelu_back = jax.vjp(lambda value: jax.nn.gelu(value, approximate=True), pre)
    grad_pre = gelu_back(grad_act)[0].astype(jnp.bfloat16)
    fc1_grad = weight_term(h2, grad_pre)
    fc1_bias_grad = jnp.sum(grad_pre.astype(jnp.float32), (0, 1))
    grad_h2 = jnp.einsum("bte,de->btd", grad_pre, fc1_full, preferred_element_type=jnp.float32)
    unused_h2, norm_back = jax.vjp(modulate, mixed, shift2, scale2)
    grad_mixed, grad_shift2, grad_scale2 = norm_back(grad_h2)
    grad_mixed = grad_mixed + grad_out
    grad_proj = (gate1[:, None, :] * grad_mixed).astype(jnp.bfloat16)
    grad_gate1 = jnp.sum(grad_mixed * proj, 1)
    proj_grad = weight_term(att, grad_proj)
    proj_bias_grad = jnp.sum(grad_proj.astype(jnp.float32), (0, 1))
    grad_att = jnp.einsum(
        "bte,de->btd", grad_proj, proj_full, preferred_element_type=jnp.float32
    ).astype(jnp.bfloat16)
    grad_heads = grad_att.reshape(query.shape)
    grad_values = jnp.einsum(
        "bhqk,bqhd->bkhd", probs, grad_heads, preferred_element_type=jnp.float32
    )
    grad_probs = jnp.einsum(
        "bqhd,bkhd->bhqk", grad_heads, values, preferred_element_type=jnp.float32
    )
    grad_scores = probs_full * (grad_probs - jnp.sum(grad_probs * probs_full, -1, keepdims=True))
    grad_scores = grad_scores.astype(jnp.bfloat16)
    grad_query = jnp.einsum(
        "bhqk,bkhd->bqhd", grad_scores, keys, preferred_element_type=jnp.float32
    ) * HEAD_DIM ** (-0.5)
    grad_keys = jnp.einsum(
        "bhqk,bqhd->bkhd", grad_scores, query, preferred_element_type=jnp.float32
    ) * HEAD_DIM ** (-0.5)
    count, length = (tokens.shape[0], tokens.shape[1])
    grad_qkv = jnp.concatenate(
        [
            grad_query.reshape(count, length, width),
            grad_keys.reshape(count, length, width),
            grad_values.reshape(count, length, width),
        ],
        -1,
    ).astype(jnp.bfloat16)
    qkv_grad = weight_term(h1, grad_qkv)
    qkv_sums = jnp.sum(grad_qkv.astype(jnp.float32), (0, 1))
    qv_bias_grad = jnp.concatenate([qkv_sums[:width], qkv_sums[2 * width :]])
    grad_h1 = jnp.einsum("bte,de->btd", grad_qkv, qkv_full, preferred_element_type=jnp.float32)
    unused_h1, first_back = jax.vjp(modulate, tokens, shift1, scale1)
    grad_tokens, grad_shift1, grad_scale1 = first_back(grad_h1)
    grad_tokens = grad_tokens + grad_mixed
    latents_grad = weighted.at[rows, kept].set(grad_tokens).astype(jnp.bfloat16)
    grad_mod = jnp.concatenate(
        [grad_shift1, grad_scale1, grad_gate1, grad_shift2, grad_scale2, grad_gate2], -1
    ).astype(jnp.bfloat16)
    ada_grad = jnp.dot(cvec.T, grad_mod, preferred_element_type=jnp.float32)
    ada_bias_grad = jnp.sum(grad_mod.astype(jnp.float32), 0)
    grad_cvec = jnp.dot(grad_mod, ada_full.T, preferred_element_type=jnp.float32)
    unused_cond, silu_back = jax.vjp(jax.nn.silu, cond)
    grad_cond = silu_back(grad_cvec)[0]
    time_grad = jnp.dot(band_hot.T, grad_cond, precision=HIGH)
    class_grad = jnp.dot(class_hot.T, grad_cond, precision=HIGH)
    shares = (
        lax.psum_scatter(time_grad, "grp", scatter_dimension=1, tiled=True),
        lax.psum_scatter(class_grad, "grp", scatter_dimension=1, tiled=True),
        lax.psum_scatter(ada_grad, "grp", scatter_dimension=1, tiled=True),
        lax.psum_scatter(ada_bias_grad, "grp", scatter_dimension=0, tiled=True),
        lax.psum_scatter(qkv_grad, "grp", scatter_dimension=1, tiled=True),
        lax.psum_scatter(qv_bias_grad, "grp", scatter_dimension=0, tiled=True),
        lax.psum_scatter(proj_grad, "grp", scatter_dimension=0, tiled=True),
        lax.psum_scatter(proj_bias_grad, "grp", scatter_dimension=0, tiled=True),
        lax.psum_scatter(fc1_grad, "grp", scatter_dimension=1, tiled=True),
        lax.psum_scatter(fc1_bias_grad, "grp", scatter_dimension=0, tiled=True),
        lax.psum_scatter(fc2_grad, "grp", scatter_dimension=0, tiled=True),
        lax.psum_scatter(fc2_bias_grad, "grp", scatter_dimension=0, tiled=True),
    )
    totals = (
        lax.psum(shares[0].astype(jnp.bfloat16), "dp").astype(jnp.float32),
        lax.psum(shares[1].astype(jnp.bfloat16), "dp").astype(jnp.float32),
        lax.psum(shares[2].astype(jnp.bfloat16), "dp").astype(jnp.float32),
        lax.psum(shares[3].astype(jnp.bfloat16), "dp").astype(jnp.float32),
        lax.psum(shares[4].astype(jnp.bfloat16), "dp").astype(jnp.float32),
        lax.psum(shares[5].astype(jnp.bfloat16), "dp").astype(jnp.float32),
        lax.psum(shares[6].astype(jnp.bfloat16), "dp").astype(jnp.float32),
        lax.psum(shares[7].astype(jnp.bfloat16), "dp").astype(jnp.float32),
        lax.psum(shares[8].astype(jnp.bfloat16), "dp").astype(jnp.float32),
        lax.psum(shares[9].astype(jnp.bfloat16), "dp").astype(jnp.float32),
        lax.psum(shares[10].astype(jnp.bfloat16), "dp").astype(jnp.float32),
        lax.psum(shares[11].astype(jnp.bfloat16), "dp").astype(jnp.float32),
    )
    return (
        block_out,
        latents_grad,
        totals[0],
        totals[1],
        totals[2],
        totals[3],
        totals[4],
        totals[5],
        totals[6],
        totals[7],
        totals[8],
        totals[9],
        totals[10],
        totals[11],
    )


def solution(mesh):
    return jax.shard_map(
        body,
        mesh=mesh,
        in_specs=(
            P(("grp", "dp"), None, None),
            P(("grp", "dp"), None, None),
            P(("grp", "dp")),
            P(("grp", "dp")),
            P(("grp", "dp"), None),
            P("grp"),
            P(None, "grp"),
            P(None, "grp"),
            P(None, "grp"),
            P("grp"),
            P(None, "grp"),
            P("grp"),
            P("grp", None),
            P("grp"),
            P(None, "grp"),
            P("grp"),
            P("grp", None),
            P("grp"),
        ),
        out_specs=(
            P(("grp", "dp"), None, None),
            P(("grp", "dp"), None, None),
            P(None, "grp"),
            P(None, "grp"),
            P(None, "grp"),
            P("grp"),
            P(None, "grp"),
            P("grp"),
            P("grp", None),
            P("grp"),
            P(None, "grp"),
            P("grp"),
            P("grp", None),
            P("grp"),
        ),
        check_vma=False,
    )
```

profile of v0, /device:TPU:0, one launch (start us, length us, event | category | flops | bytes accessed | tf_op | source)
XLA Modules:
  0.0 1405.1 jit_solution(3680828312680723182)
XLA Ops:
  17.0 27.0 %all-reduce.11 = (bf16[2304]{0:T(1024)(128)(2,1)S(1)}, bf16[6912]{0:T(1024)(128)(2,1)S(1)}, bf16[1152]{0:T(1024)(128)(2,1)}, bf16[1152]{0:T(1024)(128)(2,1)S(1)}, bf16[4608]{0:T(1024)(128)(2,1)}) all-reduce(bf16[2304]{0:T(1024)(128)(2,1)S(1)} %dynamic-update-slice.1, ...), channel_id=1, replica_groups=mesh['grp'=8,'dp'=4] {'grp'}, use_global_device_ids=true, to_apply=%add.1 | all-reduce | flops 16128 | bytes 64512
  44.7 8.5 all-gather
  59.8 3.8 gather_fusion
  73.0 57.4 %all-gather.10.cloned.1.call-done = bf16[1152,6912]{0,1:T(8,128)(2,1)} async-done(((bf16[1152,864]{0,1:T(8,128)(2,1)}), bf16[1152,6912]{0,1:T(8,128)(2,1)}) %all-gather.10.cloned.1.call-update) | async-done | bytes 15925264 | tf_op jit(solution)/shard_map/all_gather | solution.py:90
  130.4 9.7 convolution_add_fusion
  140.2 44.7 %all-gather.12.cloned.1.call-done = bf16[1152,3456]{0,1:T(8,128)(2,1)} async-done(((bf16[1152,432]{0,1:T(8,128)(2,1)}), bf16[1152,3456]{0,1:T(8,128)(2,1)}) %all-gather.12.cloned.1.call-update) | async-done | bytes 7962640 | tf_op jit(solution)/shard_map/all_gather | solution.py:92
  184.9 6.0 fusion.18
  198.9 18.1 %all-gather.14.cloned.1.call-done = bf16[1152,1152]{1,0:T(8,128)(2,1)} async-done(((bf16[144,1152]{1,0:T(8,128)(2,1)}), bf16[1152,1152]{1,0:T(8,128)(2,1)}) %all-gather.14.cloned.1.call-update) | async-done | bytes 2654224 | tf_op jit(solution)/shard_map/all_gather | solution.py:94
  216.9 5.6 convert_reduce_fusion.3
  225.6 57.0 %all-gather.16.cloned.1.call-done = bf16[1152,4608]{0,1:T(8,128)(2,1)} async-done(((bf16[1152,576]{0,1:T(8,128)(2,1)}), bf16[1152,4608]{0,1:T(8,128)(2,1)}) %all-gather.16.cloned.1.call-update) | async-done | bytes 10616848 | tf_op jit(solution)/shard_map/all_gather | solution.py:96
  282.5 10.0 fusion.12
  292.5 55.6 %all-gather.18.cloned.1.call-done = bf16[4608,1152]{1,0:T(8,128)(2,1)} async-done(((bf16[576,1152]{1,0:T(8,128)(2,1)}), bf16[4608,1152]{1,0:T(8,128)(2,1)}) %all-gather.18.cloned.1.call-update) | async-done | bytes 10616848 | tf_op jit(solution)/shard_map/all_gather | solution.py:98
  348.1 9.6 convert_reduce_fusion
  378.1 6.3 fusion.8
  384.5 10.3 multiply_reduce_fusion.2
  400.4 4.3 fusion.61
  405.8 4.4 convolution_bitcast_fusion.3
  411.2 10.2 convolution_bitcast_fusion.2
  422.2 12.5 convolution_bitcast_fusion.1
  435.7 14.0 convolution_bitcast_fusion
  450.5 12.8 fusion.78
  467.6 51.9 %reduce-scatter.16.cloned.1.call-done = f32[144,1152]{1,0:T(8,128)} async-done(((f32[1152,1152]{1,0:T(8,128)}), f32[144,1152]{1,0:T(8,128)}) %reduce-scatter.16.cloned.1.call-update) | async-done | bytes 663568 | tf_op jit(solution)/shard_map/reduce_scatter | solution.py:212
  521.4 114.7 %reduce-scatter.14.cloned.1.call-done = f32[1152,432]{0,1:T(8,128)} async-done(((f32[1152,3456]{0,1:T(8,128)}), f32[1152,432]{0,1:T(8,128)}) %reduce-scatter.14.cloned.1.call-update) | async-done | bytes 1990672 | tf_op jit(solution)/shard_map/reduce_scatter | solution.py:210
  638.7 138.4 %reduce-scatter.18.cloned.1.call-done = f32[1152,576]{0,1:T(8,128)} async-done(((f32[1152,4608]{0,1:T(8,128)}), f32[1152,576]{0,1:T(8,128)}) %reduce-scatter.18.cloned.1.call-update) | async-done | bytes 2654224 | tf_op jit(solution)/shard_map/reduce_scatter | solution.py:214
  780.1 138.3 %reduce-scatter.20.cloned.1.call-done = f32[576,1152]{1,0:T(8,128)} async-done(((f32[4608,1152]{1,0:T(8,128)}), f32[576,1152]{1,0:T(8,128)}) %reduce-scatter.20.cloned.1.call-update) | async-done | bytes 2654224 | tf_op jit(solution)/shard_map/reduce_scatter | solution.py:216
  921.3 199.6 %reduce-scatter.12.cloned.1.call-done = f32[1152,864]{0,1:T(8,128)} async-done(((f32[1152,6912]{0,1:T(8,128)}), f32[1152,864]{0,1:T(8,128)}) %reduce-scatter.12.cloned.1.call-update) | async-done | bytes 3981328 | tf_op jit(solution)/shard_map/reduce_scatter | solution.py:208
  1126.8 26.9 %scatter_fusion = bf16[2,256,1152]{2,1,0:T(8,128)(2,1)S(1)} fusion(bf16[2,256,1152]{2,1,0:T(8,128)(2,1)S(1)} %copy.129, s32[256]{0:T(256)S(1)} %copy-done.3, bf16[256,1152]{1,0:T(8,128)(2,1)} %bitcast.150), kind=kCustom, calls=%fused_computation.2 | custom fusion | bytes 1771520 | tf_op jit(solution)/shard_map/scatter | solution.py:123
  1153.8 26.3 %scatter_fusion.1 = f32[2,256,1152]{2,1,0:T(8,128)S(1)} fusion(f32[2,256,1152]{2,1,0:T(8,128)S(1)} %copy-done.1, s32[256]{0:T(256)S(1)} %copy-done.3, f32[256,1152]{1,0:T(8,128)} %bitcast.146), kind=kCustom, calls=%fused_computation.3 | custom fusion | bytes 3540992 | tf_op jit(solution)/shard_map/scatter | solution.py:194
  1182.9 25.6 %all-reduce.10 = (bf16[6912]{0:T(1024)(128)(2,1)S(1)}, bf16[2304]{0:T(1024)(128)(2,1)S(1)}, bf16[1152]{0:T(1024)(128)(2,1)S(1)}, bf16[4608]{0:T(1024)(128)(2,1)S(1)}, bf16[1152]{0:T(1024)(128)(2,1)S(1)}) all-reduce(f32[6912]{0:T(1024)S(1)} %convert_reduce_fusion.5, ...), channel_id=5, replica_groups=mesh['grp'=8,'dp'=4] {'grp'}, use_global_device_ids=true, to_apply=%region_26.27.clone | all-reduce | flops 16128 | bytes 96768
  1209.8 24.3 %all-reduce.12 = (bf16[16,144]{1,0:T(8,128)(2,1)S(1)}, bf16[864]{0:T(1024)(128)(2,1)S(1)}, bf16[288]{0:T(512)(128)(2,1)S(1)}, bf16[144]{0:T(256)(128)(2,1)S(1)},...) all-reduce(bf16[16,144]{1,0:T(8,128)(2,1)S(1)} %copy.108, ...), channel_id=1, replica_groups=mesh['grp'=8,'dp'=4] {'dp'}, use_global_device_ids=true, to_apply=%region_20.21 | all-reduce | flops 4320 | bytes 17280 | tf_op jit(solution)/shard_map/psum | solution.py:220
  1237.6 149.2 %all-reduce.16.cloned.1.call-done = (bf16[1000,144]{0,1:T(8,128)(2,1)}, bf16[1152,864]{0,1:T(8,128)(2,1)}, bf16[1152,432]{0,1:T(8,128)(2,1)}, bf16[144,1152]{1,0...) async-done(((bf16[1000,144]{0,1:T(8,128)(2,1)}, bf16[1152,864]{0,1:T(8,128)(2,1)}, bf16[1152,432]{0,1:T(8,128)(2,1)}, bf16[144,1152]{1,0:T(8,128)(2,1)}, ...) | async-done | bytes 6259984 | tf_op jit(solution)/shard_map/psum | solution.py:221
  1388.6 3.8 convert_element_type.209
  (289 shorter events, 97.9 us)
Async XLA Ops:
  7.2 63.4 %all-gather.8.cloned.1.call-start = ((), (), s32[]{:S(2)}) async-start(), calls=%async_computation.7 | async-start | bytes 2654208 | tf_op jit(solution)/shard_map/all_gather | solution.py:89
  8.5 121.9 %all-gather.10.cloned.1.call-start = ((), (), s32[]{:S(2)}) async-start(), calls=%async_computation.8 | async-start | bytes 17915904 | tf_op jit(solution)/shard_map/all_gather | solution.py:90
  9.3 175.6 %all-gather.12.cloned.1.call-start = ((), (), s32[]{:S(2)}) async-start(), calls=%async_computation.9 | async-start | bytes 8957952 | tf_op jit(solution)/shard_map/all_gather | solution.py:92
  10.1 34.6 %copy-start.62 = (bf16[16,144]{1,0:T(8,128)(2,1)S(1)}, bf16[16,144]{1,0:T(8,128)(2,1)}, u32[]{:S(2)}) copy-start(bf16[16,144]{1,0:T(8,128)(2,1)} %param.24) | copy-start | bytes 13828
  10.1 43.8 %copy-start.68 = (s32[2,128]{1,0:T(2,128)S(1)}, s32[2,128]{1,0:T(2,128)}, u32[]{:S(2)}) copy-start(s32[2,128]{1,0:T(2,128)} %param.22) | copy-start | bytes 3076
  10.1 206.8 %all-gather.14.cloned.1.call-start = ((), (), s32[]{:S(2)}) async-start(), calls=%async_computation.10 | async-start | bytes 2985984 | tf_op jit(solution)/shard_map/all_gather | solution.py:94
  10.7 271.8 %all-gather.16.cloned.1.call-start = ((), (), s32[]{:S(2)}) async-start(), calls=%async_computation.11 | async-start | bytes 11943936 | tf_op jit(solution)/shard_map/all_gather | solution.py:96
  11.3 336.8 %all-gather.18.cloned.1.call-start = ((), (), s32[]{:S(2)}) async-start(), calls=%async_computation.12 | async-start | bytes 11943936 | tf_op jit(solution)/shard_map/all_gather | solution.py:98
  11.8 454.0 %reduce-scatter.10.cloned.1.call-start = ((), (), s32[]{:S(2)}) async-start(), calls=%async_computation.13 | async-start | bytes 5308416 | tf_op jit(solution)/shard_map/reduce_scatter | solution.py:207
  66.3 295.9 %copy-start.44 = (pred[2,128]{1,0:T(4,128)(4,1)}, pred[2,128]{1,0:T(4,128)(4,1)S(1)}, u32[]{:S(2)}) copy-start(pred[2,128]{1,0:T(4,128)(4,1)S(1)} %compare_and_fusion) | copy-start | bytes 772
  66.3 64.1 %copy-start.39 = (f32[6912]{0:T(1024)S(1)}, f32[6912]{0:T(1024)}, u32[]{:S(2)}) copy-start(f32[6912]{0:T(1024)} %convert_element_type.181) | copy-start | bytes 82948
  69.6 115.3 %copy-start.46 = (f32[2,128]{1,0:T(2,128)}, f32[2,128]{1,0:T(2,128)S(1)}, u32[]{:S(2)}) copy-start(f32[2,128]{1,0:T(2,128)S(1)} %fusion.68) | copy-start | bytes 3076
  73.0 111.9 %copy-start.6 = (bf16[256,1152]{1,0:T(8,128)(2,1)S(1)}, bf16[256,1152]{1,0:T(8,128)(2,1)}, u32[]{:S(2)}) copy-start(bf16[256,1152]{1,0:T(8,128)(2,1)} %gather_fusion) | copy-start | bytes 1769476
  140.2 44.8 %copy-start.35 = (f32[2,1152]{1,0:T(2,128)}, f32[2,1152]{1,0:T(2,128)S(1)}, u32[]{:S(2)}) copy-start(f32[2,1152]{1,0:T(2,128)S(1)} %get-tuple-element.59) | copy-start | bytes 27652
  140.2 50.8 %copy-start.50 = (f32[2,1152]{1,0:T(2,128)}, f32[2,1152]{1,0:T(2,128)S(1)}, u32[]{:S(2)}) copy-start(f32[2,1152]{1,0:T(2,128)S(1)} %get-tuple-element.58) | copy-start | bytes 27652
  140.2 76.7 %copy-start.40 = (f32[2,1152]{1,0:T(2,128)}, f32[2,1152]{1,0:T(2,128)S(1)}, u32[]{:S(2)}) copy-start(f32[2,1152]{1,0:T(2,128)S(1)} %get-tuple-element.55) | copy-start | bytes 27652
  140.2 142.3 %copy-start.51 = (f32[2,1152]{1,0:T(2,128)}, f32[2,1152]{1,0:T(2,128)S(1)}, u32[]{:S(2)}) copy-start(f32[2,1152]{1,0:T(2,128)S(1)} %get-tuple-element.56) | copy-start | bytes 27652
  140.2 222.0 %copy-start.37 = (f32[2,1152]{1,0:T(2,128)}, f32[2,1152]{1,0:T(2,128)S(1)}, u32[]{:S(2)}) copy-start(f32[2,1152]{1,0:T(2,128)S(1)} %get-tuple-element.57) | copy-start | bytes 27652
  223.9 138.3 %copy-start.48 = (f32[2,128]{1,0:T(2,128)}, f32[2,128]{1,0:T(2,128)S(1)}, u32[]{:S(2)}) copy-start(f32[2,128]{1,0:T(2,128)S(1)} %broadcast_multiply_fusion) | copy-start | bytes 3076
  225.6 136.6 %copy-start.53 = (f32[2,128]{1,0:T(2,128)}, f32[2,128]{1,0:T(2,128)S(1)}, u32[]{:S(2)}) copy-start(f32[2,128]{1,0:T(2,128)S(1)} %fusion.69) | copy-start | bytes 3076
  378.1 20.1 %slice-start = ((s8[15925248]{0:T(1024)(128)(4,1)}), s8[4194304]{0:T(1024)(128)(4,1)S(1)}, s32[]{:S(2)}) async-start(s8[15925248]{0:T(1024)(128)(4,1)} %bitcast.127), calls=%async_computation.21 | async-start | bytes 8388608
  378.1 20.1 %slice-start.1 = ((s8[15925248]{0:T(1024)(128)(4,1)}), s8[4194304]{0:T(1024)(128)(4,1)S(1)}, s32[]{:S(2)}) async-start(s8[15925248]{0:T(1024)(128)(4,1)} %bitcast.127), calls=%async_computation.22 | async-start | bytes 8388608
  384.5 13.7 slice-start.2
  404.7 114.8 %reduce-scatter.16.cloned.1.call-start = ((), (), s32[]{:S(2)}) async-start(), calls=%async_computation.16 | async-start | bytes 5971968 | tf_op jit(solution)/shard_map/reduce_scatter | solution.py:212
  410.2 225.9 %reduce-scatter.14.cloned.1.call-start = ((), (), s32[]{:S(2)}) async-start(), calls=%async_computation.15 | async-start | bytes 17915904 | tf_op jit(solution)/shard_map/reduce_scatter | solution.py:210
  421.5 355.6 %reduce-scatter.18.cloned.1.call-start = ((), (), s32[]{:S(2)}) async-start(), calls=%async_computation.17 | async-start | bytes 23887872 | tf_op jit(solution)/shard_map/reduce_scatter | solution.py:214
  434.7 483.6 %reduce-scatter.20.cloned.1.call-start = ((), (), s32[]{:S(2)}) async-start(), calls=%async_computation.18 | async-start | bytes 23887872 | tf_op jit(solution)/shard_map/reduce_scatter | solution.py:216
  449.8 671.1 %reduce-scatter.12.cloned.1.call-start = ((), (), s32[]{:S(2)}) async-start(), calls=%async_computation.14 | async-start | bytes 35831808 | tf_op jit(solution)/shard_map/reduce_scatter | solution.py:208
  463.3 745.6 %reduce-scatter.22.cloned.1.call-start = ((), (), s32[]{:S(2)}) async-start(), calls=%async_computation.19 | async-start | bytes 663552
  465.5 921.3 %all-reduce.16.cloned.1.call-start = ((), (), s32[]{:S(2)}) async-start(), calls=%async_computation.20 | async-start | bytes 12533760 | tf_op jit(solution)/shard_map/psum | solution.py:221
  1126.8 26.9 %copy-start.1 = (f32[2,256,1152]{2,1,0:T(8,128)S(1)}, f32[2,256,1152]{2,1,0:T(8,128)}, u32[]{:S(2)}) copy-start(f32[2,256,1152]{2,1,0:T(8,128)} %copy-done) | copy-start | bytes 7077892
  1153.8 26.3 %copy-start.2 = (bf16[2,256,1152]{2,1,0:T(8,128)(2,1)}, bf16[2,256,1152]{2,1,0:T(8,128)(2,1)S(1)}, u32[]{:S(2)}) copy-start(bf16[2,256,1152]{2,1,0:T(8,128)(2,1)S(1)} %scatter_fusion) | copy-start | bytes 3538948
  (60 other events, 207.0 us)
Sparse Core Ops, SparseCore 0:
  9.9 32.2 all-gather.7
  44.0 86.2 all-gather.9
  132.3 52.5 all-gather.11
  186.6 30.2 all-gather.13
  218.7 63.8 all-gather.15
  284.3 63.8 all-gather.17
  404.9 53.8 reduce-scatter.9
  462.6 56.9 reduce-scatter.15
  523.2 112.8 reduce-scatter.13
  640.0 137.1 reduce-scatter.17
  781.2 137.1 reduce-scatter.19
  922.3 198.5 reduce-scatter.11
  1124.0 34.3 reduce-scatter.21
  1162.2 224.5 all-reduce.15
where the time goes:
time: 1410 us
  waiting for transfers between devices  1030 us (73%)
  matrix products  136 us (10%)
  blocking collectives  85.4 us (6%)
  local copies, waits for them, and re-layouts  83.5 us (6%)
  other arithmetic  50.5 us (4%)
  between operations  20.6 us (1%)
    reduce_scatter x1, waiting for transfers between devices, body(): lax.psum_scatter(ada_grad, 'grp', scatter_dimension=1, tiled=True)  200 us
    psum x1, waiting for transfers between devices, body(): lax.psum(shares[1].astype(jnp.bfloat16), 'dp').astype(jnp.float32)  149 us
    reduce_scatter x1, waiting for transfers between devices, body(): lax.psum_scatter(fc1_grad, 'grp', scatter_dimension=1, tiled=True)  138 us
    reduce_scatter x1, waiting for transfers between devices, body(): lax.psum_scatter(fc2_grad, 'grp', scatter_dimension=0, tiled=True)  138 us
    reduce_scatter x1, waiting for transfers between devices, body(): lax.psum_scatter(qkv_grad, 'grp', scatter_dimension=1, tiled=True)  115 us
    all_gather x1, waiting for transfers between devices, body(): lax.all_gather(w_ada, 'grp', axis=1, tiled=True)  57.4 us
    all_gather x1, waiting for transfers between devices, body(): lax.all_gather(w_fc1, 'grp', axis=1, tiled=True)  57 us
    all_gather x1, waiting for transfers between devices, body(): lax.all_gather(w_fc2, 'grp', axis=0, tiled=True)  55.6 us
  transfers between devices with their start and end apart: 14, of which 11 were waited for; matrix products, arithmetic and copies ran while one was open for 14% of the time, Pallas kernels for 0%

commit v1 on v0

--- a/solution.py
+++ b/solution.py
@@ -1,6 +1,10 @@
+import functools
+
 import jax
 import jax.numpy as jnp
 from jax import lax
+from jax.experimental import pallas as pl
+from jax.experimental.pallas import tpu as pltpu
 from jax.sharding import PartitionSpec as P
 
 HEADS = 16
@@ -248,9 +252,1014 @@
     )
 
 
+MESH = pl.DeviceIdType.MESH
+F32 = jnp.float32
+BF16 = jnp.bfloat16
+GELU_A = 0.7978845608028654
+GELU_B = 0.044715
+
+
+def dot(left, right, dims):
+    return lax.dot_general(left, right, ((dims[:1], dims[1:]), ((), ())), preferred_element_type=F32)
+
+
+class Place:
+    def __init__(self):
+        self.g = lax.axis_index("grp")
+        self.z = lax.axis_index("dp")
+        self.c = self.g % 2
+        self.x = (self.g // 2) % 2
+        self.y = self.g // 4
+
+    def block(self, dc, dx, dy):
+        c = 1 - self.c if dc else self.c
+        x = 1 - self.x if dx else self.x
+        y = 1 - self.y if dy else self.y
+        return y * 4 + x * 2 + c
+
+    def device(self, dc, dx, dy):
+        return (self.block(dc, dx, dy), self.z)
+
+
+RELATIVE = [(r & 1, (r >> 1) & 1, r >> 2) for r in range(8)]
+
+
+class Wire:
+    def __init__(self, send, recv):
+        self.send, self.recv, self.used = send, recv, 0
+
+    def take(self, count):
+        first = self.used
+        self.used += count
+        return first
+
+    def copy(self, number, src, dst, device):
+        return pltpu.make_async_remote_copy(
+            src_ref=src,
+            dst_ref=dst,
+            send_sem=self.send.at[number],
+            recv_sem=self.recv.at[number],
+            device_id=device,
+            device_id_type=MESH,
+        )
+
+
+def halves(rows):
+    cut = rows // 32 * 16
+    return pl.ds(0, cut), pl.ds(cut, rows - cut)
+
+
+def greet(devices):
+    barrier = pltpu.get_barrier_semaphore()
+    for device in devices:
+        pl.semaphore_signal(barrier, inc=1, device_id=device, device_id_type=MESH)
+    pl.semaphore_wait(barrier, len(devices))
+
+
+def plane(place):
+    return [place.device(*rel) for rel in RELATIVE[1:]]
+
+
+class Gather:
+    def __init__(self, place, wire, buf):
+        self.p, self.w, self.buf = place, wire, buf
+        self.first = wire.take(8)
+        self.parts = halves(buf.shape[1])
+        self.c = self.copies()
+
+    def make(self, number, block, device, part=None):
+        ref = self.buf.at[block]
+        if part is not None:
+            ref = self.buf.at[block, self.parts[part]]
+        return self.w.copy(self.first + number, ref, ref, device)
+
+    def copies(self):
+        p = self.p
+        own, xb, yb, db = p.g, p.block(0, 1, 0), p.block(0, 0, 1), p.block(0, 1, 1)
+        xd, yd, sd = p.device(0, 1, 0), p.device(0, 0, 1), p.device(1, 0, 0)
+        return [
+            self.make(0, own, xd),
+            self.make(1, own, yd),
+            self.make(2, own, sd),
+            self.make(3, xb, yd, 0),
+            self.make(4, xb, sd),
+            self.make(5, yb, xd, 1),
+            self.make(6, yb, sd),
+            self.make(7, db, sd),
+        ]
+
+    def start(self):
+        for number in (0, 1, 2):
+            self.c[number].start()
+
+    def neighbours(self):
+        self.c[0].wait_recv()
+        self.c[3].start()
+        self.c[4].start()
+        self.c[1].wait_recv()
+        self.c[5].start()
+        self.c[6].start()
+
+    def far(self):
+        self.c[3].wait_recv()
+        self.c[5].wait_recv()
+        self.c[7].start()
+
+    def wait_sib(self):
+        self.c[2].wait_recv()
+
+    def wait_sib_neighbours(self):
+        self.c[4].wait_recv()
+        self.c[6].wait_recv()
+
+    def wait_sib_far(self):
+        self.c[7].wait_recv()
+
+    def finish(self):
+        for copy in self.c:
+            copy.wait_send()
+
+
+class Scatter:
+    def __init__(self, place, wire, buf, r1, r2, r3, rows=None):
+        self.p, self.w, self.buf = place, wire, buf
+        self.r1, self.r2, self.r3 = r1, r2, r3
+        self.rows = rows or buf.shape[1]
+        self.parts = halves(self.rows)
+        self.first = wire.take(10)
+        p = place
+        self.sib = [p.block(1, q & 1, q >> 1) for q in range(4)]
+        self.mine = [p.block(0, q & 1, q >> 1) for q in range(4)]
+        xd, yd, sd = p.device(0, 1, 0), p.device(0, 0, 1), p.device(1, 0, 0)
+        f, w = self.first, wire
+        lo, hi = self.parts
+        whole = pl.ds(0, self.rows)
+        self.s1 = [w.copy(f + q, buf.at[self.sib[q], whole], r1.at[q], sd) for q in range(4)]
+        self.s2 = [
+            w.copy(f + 4, buf.at[self.mine[3], lo], r2.at[0, pl.ds(0, lo.size)], xd),
+            w.copy(f + 5, buf.at[self.mine[3], hi], r2.at[1, pl.ds(0, hi.size)], yd),
+        ]
+        self.s3 = [
+            w.copy(f + 6, buf.at[self.mine[1], lo], r3.at[0, lo], xd),
+            w.copy(f + 7, buf.at[self.mine[1], hi], r3.at[0, hi], xd),
+            w.copy(f + 8, buf.at[self.mine[2], lo], r3.at[1, lo], yd),
+            w.copy(f + 9, buf.at[self.mine[2], hi], r3.at[1, hi], yd),
+        ]
+
+    def send_sib(self, q):
+        self.s1[q].start()
+
+    def add_sib(self, q):
+        self.s1[q].wait_recv()
+        add_into(self.buf.at[self.mine[q], pl.ds(0, self.rows)], self.r1.at[q])
+
+    def send_far(self):
+        self.add_sib(3)
+        self.s2[0].start()
+        self.s2[1].start()
+
+    def send_near(self):
+        self.add_sib(1)
+        self.s3[0].start()
+        self.add_sib(2)
+        self.s3[3].start()
+
+    def relay(self):
+        lo, hi = self.parts
+        self.s2[1].wait_recv()
+        add_into(self.buf.at[self.mine[1], hi], self.r2.at[1, pl.ds(0, hi.size)])
+        self.s3[1].start()
+        self.s2[0].wait_recv()
+        add_into(self.buf.at[self.mine[2], lo], self.r2.at[0, pl.ds(0, lo.size)])
+        self.s3[2].start()
+        self.add_sib(0)
+
+    def result(self, out):
+        for copy in self.s3:
+            copy.wait_recv()
+        rows = self.rows
+        step = 16
+
+        @pl.loop(0, rows // step)
+        def _(i):
+            at = pl.ds(pl.multiple_of(i * step, step), step)
+            total = self.buf[self.mine[0], at].astype(F32) + self.r3[0, at].astype(F32) + self.r3[1, at].astype(F32)
+            out[at] = total.astype(out.dtype)
+
+    def finish(self):
+        for copy in self.s1 + self.s2 + self.s3:
+            copy.wait_send()
+
+
+def add_into(ref, other):
+    step = 16
+
+    @pl.loop(0, ref.shape[0] // step)
+    def _(i):
+        at = pl.ds(pl.multiple_of(i * step, step), step)
+        ref[at] = (ref[at].astype(F32) + other[at].astype(F32)).astype(ref.dtype)
+
+
+def scatter_scratch(rows, width):
+    return [
+        pltpu.VMEM((4, rows, width), BF16),
+        pltpu.VMEM((2, halves(rows)[1].size, width), BF16),
+        pltpu.VMEM((2, rows, width), BF16),
+    ]
+
+
+def to_all(place, wire, make):
+    first = wire.take(7)
+    copies = []
+    for number, rel in enumerate(RELATIVE[1:]):
+        src, dst = make(rel)
+        copies.append(wire.copy(first + number, src, dst, place.device(*rel)))
+        copies[-1].start()
+    return copies
+
+
+def wait_recv(copies):
+    for copy in copies:
+        copy.wait_recv()
+
+
+def wait_send(copies):
+    for copy in copies:
+        copy.wait_send()
+
+
+def params(collective_id):
+    return pltpu.CompilerParams(
+        collective_id=collective_id, has_side_effects=True, vmem_limit_bytes=62 * 2**20
+    )
+
+
+VMEM = pl.BlockSpec(memory_space=pltpu.VMEM)
+
+def gelu_parts(pre):
+    square = pre * pre
+    inner = jnp.tanh(GELU_A * pre * (1.0 + GELU_B * square))
+    act = 0.5 * pre * (1.0 + inner)
+    slope = 0.5 * (1.0 + inner) + 0.5 * pre * (1.0 - inner * inner) * (GELU_A * (1.0 + 3.0 * GELU_B * square))
+    return act, slope
+
+
+def local(src, dst, sem):
+    return pltpu.make_async_copy(src, dst, sem)
+
+
+def own_tokens(kept_ref, length, s):
+    rows = lax.broadcasted_iota(jnp.int32, (length, kept_ref.shape[1]), 0)
+    return jnp.where(rows == kept_ref[s : s + 1, :], 1.0, 0.0).astype(BF16)
+
+
+def normed(v):
+    cent = v - jnp.mean(v, -1, keepdims=True)
+    inv = lax.rsqrt(jnp.mean(cent * cent, -1, keepdims=True) + EPS)
+    return cent * inv, inv
+
+
+def norm_back(grad, hat, inv):
+    return inv * (grad - jnp.mean(grad, -1, keepdims=True) - hat * jnp.mean(grad * hat, -1, keepdims=True))
+
+
+STEP = 32
+
+
+def by_rows(samples, keep, fn):
+    @pl.loop(0, samples * keep // STEP)
+    def _(i):
+        fn(lax.div(i, keep // STEP), pl.ds(pl.multiple_of(i * STEP, STEP), STEP))
+
+
+SCALE = HEAD_DIM ** (-0.5)
+
+
+def probabilities(q, k):
+    scores = dot(q, k, (0, 0)) * SCALE
+    exps = jnp.exp(scores - jnp.max(scores, -1, keepdims=True))
+    return exps / jnp.sum(exps, -1, keepdims=True)
+
+
+def arrival(p, t):
+    dc = jnp.where((t == 1) | (t == 4) | (t == 5) | (t == 7), 1, 0)
+    dx = jnp.where((t == 2) | (t == 4) | (t >= 6), 1, 0)
+    dy = jnp.where((t == 3) | (t >= 5), 1, 0)
+    c, x, y = lax.rem(p.c + dc, 2), lax.rem(p.x + dx, 2), lax.rem(p.y + dy, 2)
+    return y * 4 + x * 2 + c
+
+
+MSG_PROJ, MSG_FC2, MSG_QV, MSG_ROWS = 8, 16, 24, 40
+
+
+def sample_weight(place, counts_ref, samples, s):
+    count = jnp.full((1, 128), counts_ref[0], jnp.int32)
+    used = count > place.z * samples + s
+    return (jnp.where(used, 1.0, 0.0) / count.astype(F32))[:, 0:1]
+
+
+def forward_kernel(samples, labels_ref, bands_ref, counts_ref, wq_ref, wp_ref, bias_ref, kept_ref, lat_ref, cot_ref, class_ref,
+                   time_ref, ada_ref, bada_ref, w1_ref, b1_ref, w2_ref,
+                   w_out, act_out, units_out, att_out, h1_out, mixed_out, proj_out, g1_out, g2_out, gb1_out, dh2_out, mod_out,
+                   cond_out, vec_out, ids_out,
+                   w_all, msg_all, cond_all, mod_in, mod_send, mod, h1, units, att, proj, mixed, vec, h2_all, dm_all, act, dpre,
+                   pbuf, p1, p2, p3, acc, send, recv, sems):
+    p = Place()
+    wire = Wire(send, recv)
+    greet(plane(p))
+    g = p.g
+    length = lat_ref.shape[1]
+    keep = kept_ref.shape[1]
+    rows, width = h1.shape
+    pair = 2 * HEAD_DIM
+    lanes = lax.broadcasted_iota(jnp.int32, (1, msg_all.shape[2]), 1)
+    msg_all[g, 0:8] = jnp.zeros((8, msg_all.shape[2]), F32)
+    for s in range(samples):
+        line = jnp.where(lanes == 0, labels_ref[s], 0) + jnp.where(lanes == 1, bands_ref[s], 0)
+        msg_all[g, s : s + 1, :] = line.astype(F32)
+    msg_all[g, 8:MSG_ROWS] = jnp.zeros((MSG_ROWS - 8, msg_all.shape[2]), F32)
+    for row in range(4):
+        at = MSG_PROJ + 8 * row
+        msg_all[g, at : at + 1, :] = bias_ref[row : row + 1, :]
+    msgs = to_all(p, wire, lambda rel: (msg_all.at[g], msg_all.at[g]))
+    w_all[g, 0 : 3 * pair] = wq_ref[...]
+    w_all[g, 3 * pair : 4 * pair] = wp_ref[...]
+    weights = Gather(p, wire, w_all)
+    weights.start()
+    main = Gather(p, wire, h2_all)
+    back = Gather(p, wire, dm_all)
+    sums = Scatter(p, wire, pbuf, p1, p2, p3)
+
+    for s in range(samples):
+        hot = own_tokens(kept_ref, length, s)
+        at = pl.ds(s * keep, keep)
+        mixed[at] = dot(hot, lat_ref[s], (0, 0))
+        proj[at] = dot(hot, cot_ref[s], (0, 0)) * sample_weight(p, counts_ref, samples, s)
+
+    wait_recv(msgs)
+    labels = jnp.concatenate([msg_all[j, 0:samples, 0:1] for j in range(8)], 0)
+    bands = jnp.concatenate([msg_all[j, 0:samples, 1:2] for j in range(8)], 0)
+
+    def one_hot(ids, size):
+        lanes = lax.broadcasted_iota(jnp.int32, (ids.shape[0], size), 1).astype(F32)
+        return jnp.where(lanes == ids, 1.0, 0.0).astype(BF16)
+
+    of_band = dot(one_hot(bands, time_ref.shape[0]), time_ref[...], (1, 0))
+    cond_all[g] = of_band + dot(one_hot(labels, class_ref.shape[1]), class_ref[...], (1, 1))
+    ids_out[...] = jnp.zeros_like(ids_out)
+    ids_out[:, 0:1] = labels
+    ids_out[:, 1:2] = bands
+    conds = to_all(p, wire, lambda rel: (cond_all.at[g], cond_all.at[g]))
+    wait_recv(conds)
+    value = jnp.concatenate([cond_all[j] for j in range(8)], 1)
+    value = (value * jax.nn.sigmoid(value)).astype(BF16)
+    mods = dot(value, ada_ref[...], (1, 1)) + bada_ref[...]
+    mod_send[...] = jnp.zeros_like(mod_send)
+    for j in range(8):
+        mod_send[j, 0:samples, :] = mods[samples * j : samples * (j + 1), :]
+    mod_in[g] = mod_send[g]
+    modc = to_all(p, wire, lambda rel: (mod_send.at[p.block(*rel)], mod_in.at[g]))
+    vec[...] = jnp.zeros_like(vec)
+    for row, at in ((0, MSG_PROJ), (1, MSG_FC2)):
+        vec[row : row + 1, :] = jnp.concatenate([msg_all[j, at : at + 1, :] for j in range(8)], 1)
+    wait_recv(modc)
+    mod[...] = jnp.zeros_like(mod)
+    for s in range(samples):
+        line = jnp.concatenate([mod_in[j, s : s + 1, :] for j in range(8)], 1)
+        for v in range(6):
+            mod[s, v : v + 1, :] = line[:, v * width : (v + 1) * width]
+
+    def first(s, at):
+        hat, inv = normed(mixed[at])
+        h1[at] = (hat * (1.0 + mod[s, 1:2, :]) + mod[s, 0:1, :]).astype(BF16)
+        dm_all[g, at] = (mod[s, 5:6, :] * proj[at]).astype(BF16)
+
+    by_rows(samples, keep, first)
+
+    ones = jnp.ones((8, rows), BF16)
+
+    @pl.loop(0, 8)
+    def _(t):
+        @pl.when(t == 1)
+        def _():
+            weights.wait_sib()
+
+        @pl.when(t == 2)
+        def _():
+            weights.neighbours()
+            back.start()
+
+        @pl.when(t == 4)
+        def _():
+            weights.wait_sib_neighbours()
+
+        @pl.when(t == 6)
+        def _():
+            weights.far()
+
+        @pl.when(t == 7)
+        def _():
+            weights.wait_sib_far()
+
+        block = arrival(p, t)
+        for i in range(3):
+            chunk = block * 3 + i
+            bias_at = jnp.where(chunk >= 16, chunk - 8, chunk)
+            keys = (chunk >= 8) & (chunk < 16)
+            line = msg_all[lax.div(bias_at, 2), pl.ds(pl.multiple_of(MSG_QV + 8 * lax.rem(bias_at, 2), 8), 8), :]
+            line = line * jnp.where(keys, 0.0, 1.0)
+            value = dot(w_all[block, i * pair : (i + 1) * pair, :], h1[...], (1, 1))
+            value = value + dot(line.astype(BF16), ones, (0, 0))
+            units[2 * chunk] = value[:HEAD_DIM].astype(BF16)
+            units[2 * chunk + 1] = value[HEAD_DIM:].astype(BF16)
+
+    outs = [
+        local(w_all, w_out, sems.at[0]),
+        local(units, units_out, sems.at[1]),
+        local(h1, h1_out, sems.at[2]),
+        local(mod, mod_out, sems.at[3]),
+        local(cond_all, cond_out, sems.at[4]),
+        local(vec, vec_out, sems.at[5]),
+        local(att, att_out, sems.at[6]),
+        local(proj, proj_out, sems.at[7]),
+        local(mixed, mixed_out, sems.at[8]),
+        local(act, act_out, sems.at[9]),
+    ]
+    for copy in outs[:6]:
+        copy.start()
+    proj[...] = jnp.zeros_like(proj)
+
+    @pl.loop(0, 8)
+    def _(u):
+        @pl.when(u == 6)
+        def _():
+            back.neighbours()
+
+        for s in range(samples):
+            lanes = pl.ds(s * keep, keep)
+            pieces = []
+            for e in range(2):
+                probs = probabilities(units[2 * u + e, :, lanes], units[16 + 2 * u + e, :, lanes])
+                pieces.append(dot(units[32 + 2 * u + e, :, lanes], probs.astype(BF16), (1, 1)))
+            att[u, :, lanes] = jnp.concatenate(pieces, 0).astype(BF16)
+        proj[...] += dot(att[u], w_all[u, pl.ds(3 * pair, pair), :], (0, 0))
+
+    def second(s, at):
+        proj[at] = proj[at] + vec[0:1, :]
+        mixed[at] = mixed[at] + mod[s, 2:3, :] * proj[at]
+        hat, inv = normed(mixed[at])
+        h2_all[g, at] = (hat * (1.0 + mod[s, 4:5, :]) + mod[s, 3:4, :]).astype(BF16)
+
+    by_rows(samples, keep, second)
+    main.start()
+    back.far()
+    for copy in outs[6:9]:
+        copy.start()
+
+    gb1_out[...] = jnp.zeros_like(gb1_out)
+
+    def hidden(block):
+        pre = dot(h2_all[block], w1_ref[...], (1, 1)) + b1_ref[...]
+        value, slope = gelu_parts(pre)
+        act[block] = value.astype(BF16)
+        low = (dot(dm_all[block], w2_ref[...], (1, 1)) * slope).astype(BF16)
+        dpre[block] = low
+        gb1_out[...] += jnp.sum(low.astype(F32), 0, keepdims=True)
+        pbuf[block] = dot(low, w1_ref[...], (1, 0)).astype(BF16)
+
+    @pl.loop(0, 8)
+    def _(t):
+        @pl.when(t == 1)
+        def _():
+            main.wait_sib()
+            back.wait_sib()
+
+        @pl.when(t == 2)
+        def _():
+            main.neighbours()
+            back.wait_sib_neighbours()
+            back.wait_sib_far()
+
+        @pl.when(t == 4)
+        def _():
+            main.wait_sib_neighbours()
+
+        @pl.when(t == 6)
+        def _():
+            main.far()
+
+        @pl.when(t == 7)
+        def _():
+            main.wait_sib_far()
+
+        hidden(arrival(p, t))
+        for at, q in ((1, 0), (4, 1), (5, 2), (7, 3)):
+
+            @pl.when(t == at)
+            def _(q=q):
+                sums.send_sib(q)
+
+    outs[9].start()
+    sums.send_far()
+    sums.send_near()
+
+    tile = acc.shape[1]
+    for left, right, out in ((dpre, h2_all, g1_out), (act, dm_all, g2_out)):
+        for n in range(width // tile):
+            at = pl.ds(n * tile, tile)
+            acc[...] = jnp.zeros_like(acc)
+
+            @pl.loop(0, 8)
+            def _(block, left=left, right=right, at=at):
+                acc[...] += dot(left[block], right[block, :, at], (0, 0))
+
+            out[:, at] = acc[...].astype(BF16)
+        if left is dpre:
+            sums.relay()
+    sums.result(dh2_out)
+    for piece in (weights, main, back, sums):
+        piece.finish()
+    for copies in (msgs, conds, modc):
+        wait_send(copies)
+    for copy in outs:
+        copy.wait()
+
+
+ANY = pl.BlockSpec(memory_space=pl.ANY)
+
+
+SMEM = pl.BlockSpec(memory_space=pltpu.SMEM)
+
+
+def forward(samples, labels, bands, counts, wq, wp, bias, kept, lat, cot, class_table, time_table, w_ada, b_ada, w1, b1, w2):
+    keep, width = kept.shape[1], wq.shape[1]
+    rows, hidden, count = samples * keep, w1.shape[0], 8 * samples
+    shape = jax.ShapeDtypeStruct
+    mods = (8, 8, w_ada.shape[0])
+    cond = (8, count, class_table.shape[0])
+    w = (8, wq.shape[0] + wp.shape[0], width)
+    return pl.pallas_call(
+        functools.partial(forward_kernel, samples),
+        out_shape=[
+            shape(w, BF16),
+            shape((8, rows, hidden), BF16),
+            shape((48, HEAD_DIM, rows), BF16),
+            shape((8, 2 * HEAD_DIM, rows), BF16),
+            shape((rows, width), BF16),
+            shape((rows, width), F32),
+            shape((rows, width), F32),
+            shape((hidden, width), BF16),
+            shape((hidden, width), BF16),
+            shape((1, hidden), F32),
+            shape((rows, width), F32),
+            shape((samples, 8, width), F32),
+            shape(cond, F32),
+            shape((8, width), F32),
+            shape((count, 128), F32),
+        ],
+        in_specs=[SMEM] * 3 + [VMEM] * 13,
+        out_specs=[ANY] * 7 + [VMEM] * 4 + [ANY] * 3 + [VMEM],
+        scratch_shapes=[
+            pltpu.VMEM(w, BF16),
+            pltpu.VMEM((8, MSG_ROWS, wp.shape[0]), F32),
+            pltpu.VMEM(cond, F32),
+            pltpu.VMEM(mods, F32),
+            pltpu.VMEM(mods, F32),
+            pltpu.VMEM((samples, 8, width), F32),
+            pltpu.VMEM((rows, width), BF16),
+            pltpu.VMEM((48, HEAD_DIM, rows), BF16),
+            pltpu.VMEM((8, 2 * HEAD_DIM, rows), BF16),
+            pltpu.VMEM((rows, width), F32),
+            pltpu.VMEM((rows, width), F32),
+            pltpu.VMEM((8, width), F32),
+            pltpu.VMEM((8, rows, width), BF16),
+            pltpu.VMEM((8, rows, width), BF16),
+            pltpu.VMEM((8, rows, hidden), BF16),
+            pltpu.VMEM((8, rows, hidden), BF16),
+            pltpu.VMEM((8, rows, width), BF16),
+            *scatter_scratch(rows, width),
+            pltpu.VMEM((hidden, width // 3), F32),
+            pltpu.SemaphoreType.DMA((55,)),
+            pltpu.SemaphoreType.DMA((55,)),
+            pltpu.SemaphoreType.DMA((10,)),
+        ],
+        compiler_params=params(1),
+    )(labels, bands, counts, wq, wp, bias, kept, lat, cot, class_table, time_table, w_ada, b_ada, w1, b1, w2)
+
+
+CHUNK = 144
+
+
+def backward_kernel(samples, planes, counts_ref, w_hbm, act_hbm, units_hbm, att_hbm, h1_ref, mixed_ref, proj_ref, g1_ref, g2_ref, gb1_ref,
+                    dh2_ref, mod_ref, cond_ref, vec_ref, ids_ref, kept_ref, lat_ref, cot_ref, ada_ref, w2_ref,
+                    out, block_out, lat_out, dmod_z, dcond_z, cvec_z, sum_z, ids_z,
+                    wt, wp, act, units, att, h1_all, dx2, dproj, dq, dq_all, from_end, gq, gp, qr1, qr2, qr3, pr1, pr2, pr3,
+                    mlp, dh1, grad, dmod_send, dmod_in, dc_send, dc_in, bundle, bundles, send, recv, sems):
+    p = Place()
+    wire = Wire(send, recv)
+    others = [(p.g, (p.z + k) % planes) for k in range(1, planes)]
+    greet(plane(p) + others)
+    g, z = p.g, p.z
+    length = lat_ref.shape[1]
+    keep = kept_ref.shape[1]
+    rows, width = dx2.shape
+    pair = 2 * HEAD_DIM
+    loads = [
+        local(w_hbm.at[:, pl.ds(3 * pair, pair)], wp, sems.at[0]),
+        local(units_hbm, units, sems.at[1]),
+        local(att_hbm, att, sems.at[2]),
+        local(w_hbm.at[:, pl.ds(0, 3 * pair)], wt, sems.at[3]),
+        local(act_hbm, act, sems.at[4]),
+    ]
+    for copy in loads:
+        copy.start()
+
+    sources = []
+    for ref in (g1_ref, g2_ref, gp, gq):
+        for start in range(0, ref.shape[0], CHUNK):
+            sources.append(ref.at[pl.ds(start, CHUNK)])
+    count = len(sources)
+    up, across, down = wire.take(count), wire.take(count), wire.take(count)
+    inner, outer, partner = 1 + z // 3, (z - 1) * 3, 3 - z
+    at_end = (z == 0) | (z == planes - 1)
+    ups = [wire.copy(up + k, sources[k], from_end.at[k], (g, inner)) for k in range(count)]
+    acrosses = [wire.copy(across + k, from_end.at[k], out.at[k], (g, partner)) for k in range(count)]
+    downs = [wire.copy(down + k, out.at[k], out.at[k], (g, outer)) for k in range(count)]
+
+    def chain_send(*numbers):
+        @pl.when(at_end)
+        def _():
+            for k in numbers:
+                ups[k].start()
+
+    def chain(*numbers):
+        @pl.when(jnp.logical_not(at_end))
+        def _():
+            for k in numbers:
+                if k < count:
+                    ups[k].wait_recv()
+                    add_into(from_end.at[k], sources[k])
+                    acrosses[k].start()
+                if k > 0:
+                    acrosses[k - 1].wait_recv()
+                    add_into(out.at[k - 1], from_end.at[k - 1])
+                    downs[k - 1].start()
+
+    chain_send(*range(8))
+
+    tokens = Gather(p, wire, h1_all)
+    h1_all[g] = h1_ref[...]
+    tokens.start()
+
+    value = cond_ref[...]
+    cvec_z[z] = (value * jax.nn.sigmoid(value)).astype(BF16)
+    ids_z[z] = ids_ref[...]
+    first = wire.take(2 * (planes - 1))
+    cvecs = [wire.copy(first + k, cvec_z.at[z], cvec_z.at[z], device) for k, device in enumerate(others)]
+    first += planes - 1
+    cvecs += [wire.copy(first + k, ids_z.at[z], ids_z.at[z], device) for k, device in enumerate(others)]
+    for copy in cvecs:
+        copy.start()
+
+    for s in range(samples):
+        hot = own_tokens(kept_ref, length, s)
+        grad[pl.ds(s * keep, keep)] = dot(hot, cot_ref[s], (0, 0)) * sample_weight(p, counts_ref, samples, s)
+    bundle[...] = jnp.zeros_like(bundle)
+
+    def add_row(row, value):
+        bundle[pl.ds(row, 1), :] += jnp.sum(value, 0, keepdims=True)
+
+    SUM_PROJ, SUM_FC2 = 6 * samples, 6 * samples + 1
+
+    def second(s, at):
+        hat, inv = normed(mixed_ref[at])
+        up_grad = dh2_ref[at]
+        value = grad[at] + norm_back(up_grad * (1.0 + mod_ref[s, 4:5, :]), hat, inv)
+        dx2[at] = value
+        low = (mod_ref[s, 2:3, :] * value).astype(BF16)
+        dproj[at] = low
+        add_row(s * 6 + 3, up_grad)
+        add_row(s * 6 + 4, up_grad * hat)
+        add_row(s * 6 + 2, value * proj_ref[at])
+        add_row(SUM_PROJ, low.astype(F32))
+        add_row(SUM_FC2, (mod_ref[s, 5:6, :] * grad[at]).astype(BF16).astype(F32))
+
+    by_rows(samples, keep, second)
+    for copy in loads[:3]:
+        copy.wait()
+
+    @pl.loop(0, 8)
+    def _(u):
+        datt = dot(wp[u], dproj[...], (1, 1))
+        wp[u] = dot(att[u], dproj[...], (1, 0)).astype(BF16)
+        lists = ([], [], [])
+        for s in range(samples):
+            lanes = pl.ds(s * keep, keep)
+            parts = ([], [], [])
+            for e in range(2):
+                q, k, v = (units[16 * i + 2 * u + e, :, lanes] for i in range(3))
+                da = datt[e * HEAD_DIM : (e + 1) * HEAD_DIM, s * keep : (s + 1) * keep].astype(BF16)
+                probs = probabilities(q, k)
+                dprobs = dot(da, v, (0, 0))
+                dscores = probs * (dprobs - jnp.sum(dprobs * probs, -1, keepdims=True))
+                dscores = dscores.astype(BF16)
+                parts[0].append(dot(k, dscores, (1, 1)) * SCALE)
+                parts[1].append(dot(q, dscores, (1, 0)) * SCALE)
+                parts[2].append(dot(da, probs.astype(BF16), (1, 0)))
+            for i in range(3):
+                lists[i].append(jnp.concatenate(parts[i], 0).astype(BF16))
+        for i in range(3):
+            chunk = 8 * i + u
+            at = pl.ds(pl.multiple_of(lax.rem(chunk, 3) * pair, 16), pair)
+            for s in range(samples):
+                dq[lax.div(chunk, 3), at, pl.ds(s * keep, keep)] = lists[i][s]
+
+        @pl.when(u == 3)
+        def _():
+            tokens.neighbours()
+            chain(0)
+
+        @pl.when(u == 7)
+        def _():
+            tokens.far()
+            chain(1)
+
+    dq_all[g] = dq[g]
+    moves = to_all(p, wire, lambda rel: (dq.at[p.block(*rel)], dq_all.at[g]))
+    projs = Scatter(p, wire, wp, pr1, pr2, pr3)
+    for q in (3, 1, 2, 0):
+        projs.send_sib(q)
+    chain(2)
+
+    loads[3].wait()
+    dh1[...] = jnp.zeros_like(dh1)
+
+    @pl.loop(0, 8)
+    def _(j):
+        dh1[...] += dot(dq[j], wt[j], (0, 0))
+
+    projs.send_far()
+    projs.send_near()
+    chain(3)
+
+    loads[4].wait()
+    outs = Scatter(p, wire, wt, qr1, qr2, qr3, rows)
+
+    @pl.loop(0, 8)
+    def _(t):
+        block = arrival(p, 7 - t)
+        wt[block, pl.ds(0, rows)] = jnp.dot(act[block], w2_ref[...], preferred_element_type=F32).astype(BF16)
+        for at, q in ((1, 0), (4, 1), (5, 2), (7, 3)):
+
+            @pl.when(t == 7 - at)
+            def _(q=q):
+                outs.send_sib(q)
+
+    projs.relay()
+    outs.send_far()
+    outs.send_near()
+    chain(4)
+    projs.result(gp)
+    chain_send(8)
+
+    for s in range(samples):
+        hot = own_tokens(kept_ref, length, s)
+        mlp[pl.ds(s * keep, keep)] = dot(hot, lat_ref[s], (0, 0))
+
+    def back_first(s, at):
+        hat, inv = normed(mlp[at])
+        up_grad = dh1[at]
+        dx = dx2[at] + norm_back(up_grad * (1.0 + mod_ref[s, 1:2, :]), hat, inv)
+        add_row(s * 6, up_grad)
+        add_row(s * 6 + 1, up_grad * hat)
+        dproj[at] = dx.astype(BF16)
+
+    by_rows(samples, keep, back_first)
+    for s in range(samples):
+        hot = own_tokens(kept_ref, length, s)
+        is_kept = jnp.sum(hot.astype(F32), 1, keepdims=True) > 0.5
+        spread = dot(hot, dproj[pl.ds(s * keep, keep)], (1, 0))
+        weighted = cot_ref[s].astype(F32) * sample_weight(p, counts_ref, samples, s)
+        lat_out[s] = jnp.where(is_kept, spread, weighted).astype(BF16)
+    chain(5)
+
+    tokens.wait_sib()
+    tokens.wait_sib_neighbours()
+    tokens.wait_sib_far()
+    wait_recv(moves)
+    for i in range(3):
+        at = pl.ds(i * pair, pair)
+        dh1[0:pair] = jnp.zeros((pair, width), F32)
+
+        @pl.loop(0, 8)
+        def _(j, at=at):
+            dh1[0:pair] += dot(dq_all[j, at, :], h1_all[j], (1, 0))
+
+        gq[at] = dh1[0:pair].astype(BF16)
+        chain_send(9 + i)
+    chain(6)
+
+    outs.relay()
+    outs.result(mlp)
+
+    def end(s, at):
+        value = mlp[at] + vec_ref[1:2, :]
+        add_row(s * 6 + 5, grad[at] * value)
+        dproj[at] = (mixed_ref[at] + mod_ref[s, 5:6, :] * value).astype(BF16)
+
+    by_rows(samples, keep, end)
+    chain(7)
+
+    cols = ada_ref.shape[0]
+    dmod_send[...] = jnp.zeros_like(dmod_send)
+    for s in range(samples):
+        line = jnp.concatenate([bundle[s * 6 + v : s * 6 + v + 1, :] for v in range(6)], 1)
+        line = line.astype(BF16).astype(F32)
+        for j in range(8):
+            dmod_send[j, s : s + 1, :] = line[:, j * cols : (j + 1) * cols]
+    dmod_in[g] = dmod_send[g]
+    dmods = to_all(p, wire, lambda rel: (dmod_send.at[p.block(*rel)], dmod_in.at[g]))
+    bundles[g, 0:8, :] = jnp.zeros((8, width), F32)
+    bundles[g, 0:2, :] = bundle[SUM_PROJ : SUM_PROJ + 2, :]
+    ones = jnp.ones((8, rows), BF16)
+    for j in range(8):
+        line = dot(ones, dq[j], (1, 1))
+        bundles[g, 8 + j : 9 + j, 0 : 3 * pair] = line[0:1, :]
+    sums = to_all(p, wire, lambda rel: (bundles.at[g], bundles.at[g]))
+
+    for s in range(samples):
+        hot = own_tokens(kept_ref, length, s)
+        is_kept = jnp.sum(hot.astype(F32), 1, keepdims=True) > 0.5
+        spread = dot(hot, dproj[pl.ds(s * keep, keep)], (1, 0))
+        block_out[s] = jnp.where(is_kept, spread, lat_ref[s].astype(F32)).astype(BF16)
+
+    wait_recv(dmods)
+    part = jnp.concatenate([dmod_in[j, 0:samples, :] for j in range(8)], 0)
+    dmod_z[z] = part
+    first = wire.take(planes - 1)
+    dmodz = [wire.copy(first + k, dmod_z.at[z], dmod_z.at[z], device) for k, device in enumerate(others)]
+    for copy in dmodz:
+        copy.start()
+    dcvec = dot(part.astype(BF16), ada_ref[...], (1, 0))
+    depth = cond_ref.shape[2]
+    for j in range(8):
+        dc_send[j] = dcvec[:, j * depth : (j + 1) * depth]
+    dc_in[g] = dc_send[g]
+    dcs = to_all(p, wire, lambda rel: (dc_send.at[p.block(*rel)], dc_in.at[g]))
+    wait_recv(sums)
+    sum_z[z] = sum(bundles[j] for j in range(8))
+    sum_z[z, 2:3, 0 : gb1_ref.shape[1]] = gb1_ref[...]
+    first = wire.take(planes - 1)
+    sumz = [wire.copy(first + k, sum_z.at[z], sum_z.at[z], device) for k, device in enumerate(others)]
+    for copy in sumz:
+        copy.start()
+    wait_recv(dcs)
+    cond = cond_ref[g]
+    gate = jax.nn.sigmoid(cond)
+    dcond_z[z] = sum(dc_in[j] for j in range(8)) * (gate * (1.0 + cond * (1.0 - gate)))
+    first = wire.take(planes - 1)
+    dconds = [wire.copy(first + k, dcond_z.at[z], dcond_z.at[z], device) for k, device in enumerate(others)]
+    for copy in dconds:
+        copy.start()
+
+    chain(*range(8, count + 1))
+
+    @pl.when(jnp.logical_not(at_end))
+    def _():
+        for k in range(count):
+            acrosses[k].wait_send()
+            downs[k].wait_send()
+
+    @pl.when(at_end)
+    def _():
+        for k in range(count):
+            downs[k].wait_recv()
+            ups[k].wait_send()
+
+    for copies in (cvecs, dmodz, sumz, dconds):
+        wait_recv(copies)
+    for copies in (moves, dmods, sums, dcs, cvecs, dmodz, sumz, dconds):
+        wait_send(copies)
+    for piece in (tokens, projs, outs):
+        piece.finish()
+
+
+def backward(samples, planes, counts, w, act, units, att, h1, mixed, proj, g1, g2, gb1, dh2, mod, cond, vec, ids, kept, lat, cot,
+             w_ada, w2):
+    keep, width = kept.shape[1], h1.shape[1]
+    rows, per = samples * keep, 8 * samples
+    pair = 2 * HEAD_DIM
+    wq, wp = 3 * pair, pair
+    count = (g1.shape[0] + g2.shape[0] + wq + wp) // CHUNK
+    shape = jax.ShapeDtypeStruct
+    cols, depth = w_ada.shape[0], cond.shape[2]
+    sems = 3 * count + 8 + 5 * (planes - 1) + 7 + 10 + 10 + 7 + 7 + 7
+    return pl.pallas_call(
+        functools.partial(backward_kernel, samples, planes),
+        out_shape=[
+            shape((count, CHUNK, width), BF16),
+            shape(lat.shape, BF16),
+            shape(lat.shape, BF16),
+            shape((planes, per, cols), F32),
+            shape((planes, per, depth), F32),
+            shape((planes, 8, per, depth), BF16),
+            shape((planes, 16, width), F32),
+            shape((planes,) + ids.shape, F32),
+        ],
+        in_specs=[SMEM] + [ANY] * 4 + [VMEM] * 16,
+        out_specs=[VMEM] * 8,
+        scratch_shapes=[
+            pltpu.VMEM((8, wq, width), BF16),
+            pltpu.VMEM((8, wp, width), BF16),
+            pltpu.VMEM(act.shape, BF16),
+            pltpu.VMEM(units.shape, BF16),
+            pltpu.VMEM(att.shape, BF16),
+            pltpu.VMEM((8, rows, width), BF16),
+            pltpu.VMEM((rows, width), F32),
+            pltpu.VMEM((rows, width), BF16),
+            pltpu.VMEM((8, wq, rows), BF16),
+            pltpu.VMEM((8, wq, rows), BF16),
+            pltpu.VMEM((count, CHUNK, width), BF16),
+            pltpu.VMEM((wq, width), BF16),
+            pltpu.VMEM((wp, width), BF16),
+            *scatter_scratch(rows, width),
+            *scatter_scratch(wp, width),
+            pltpu.VMEM((rows, width), F32),
+            pltpu.VMEM((rows, width), F32),
+            pltpu.VMEM((rows, width), F32),
+            pltpu.VMEM((8, 8, cols), F32),
+            pltpu.VMEM((8, 8, cols), F32),
+            pltpu.VMEM((8, per, depth), F32),
+            pltpu.VMEM((8, per, depth), F32),
+            pltpu.VMEM((16, width), F32),
+            pltpu.VMEM((8, 16, width), F32),
+            pltpu.SemaphoreType.DMA((sems,)),
+            pltpu.SemaphoreType.DMA((sems,)),
+            pltpu.SemaphoreType.DMA((5,)),
+        ],
+        compiler_params=params(2),
+    )(counts, w, act, units, att, h1, mixed, proj, g1, g2, gb1, dh2, mod, cond, vec, ids, kept, lat, cot, w_ada, w2)
+
+
+def plane_body(planes, latents, cotangent, bands, labels, kept, band_counts, time_table, class_table, w_ada, b_ada, w_qkv,
+               qv_bias, w_proj, b_proj, w_fc1, b_fc1, w_fc2, b_fc2):
+    samples, length, width = latents.shape
+    g = lax.axis_index("grp")
+    wq = w_qkv.shape[1]
+    wp = w_proj.shape[0]
+    hidden = w_fc1.shape[1]
+    per = 8 * samples
+
+    bias = jnp.concatenate([b_proj, b_fc2, qv_bias]).astype(F32).reshape(4, wp)
+    (w, act, units, att, h1, mixed, proj, g1, g2, gb1, dh2, mod, cond, vec, ids) = forward(
+        samples, labels, bands, band_counts, w_qkv.T, w_proj, bias, kept, latents, cotangent, class_table.T, time_table, w_ada.T,
+        b_ada.astype(F32)[None], w_fc1.T, b_fc1.astype(F32)[None], w_fc2
+    )
+    totals, block_out, latents_grad, dmod_z, dcond_z, cvec_z, sum_z, ids_z = backward(
+        samples, planes, band_counts, w, act, units, att, h1, mixed, proj, g1, g2, gb1, dh2, mod, cond, vec, ids, kept, latents,
+        cotangent, w_ada.T, w_fc2
+    )
+    totals = totals.reshape(-1, width)
+    at = 0
+    pieces = []
+    for size in (hidden, hidden, wp, wq):
+        pieces.append(totals[at : at + size].astype(F32))
+        at += size
+    cvec_z = cvec_z.transpose(0, 2, 1, 3).reshape(planes * per, width)
+    mod_z = dmod_z.reshape(planes * per, -1).astype(BF16)
+    ada_grad = jnp.einsum("se,sd->ed", mod_z, cvec_z, preferred_element_type=F32).T
+    ada_bias_grad = jnp.sum(mod_z.astype(F32), 0)
+    sums = jnp.sum(sum_z, 0)
+    part = lambda v, size: lax.dynamic_slice_in_dim(v, g * size, size, 0)
+    qkv_sums = sums[8:, :wq].reshape(-1)
+    qv_grad = part(jnp.concatenate([qkv_sums[:width], qkv_sums[2 * width :]]), qv_bias.shape[0])
+    dcond = dcond_z.reshape(planes * per, -1)
+    ids_z = ids_z.reshape(planes * per, -1)
+    hot_class = (jnp.arange(class_table.shape[0], dtype=F32)[None, :] == ids_z[:, 0:1]).astype(F32)
+    hot_time = (jnp.arange(time_table.shape[0], dtype=F32)[:, None] == ids_z[:, 1][None, :]).astype(F32)
+    return (
+        block_out,
+        latents_grad,
+        jnp.dot(hot_time, dcond, precision=HIGH),
+        jnp.einsum("se,sc->ec", dcond, hot_class, precision=HIGH).T,
+        ada_grad,
+        ada_bias_grad,
+        pieces[3].T,
+        qv_grad,
+        pieces[2],
+        part(sums[0], b_proj.shape[0]),
+        pieces[0].T,
+        sums[2, :hidden],
+        pieces[1],
+        part(sums[1], b_fc2.shape[0]),
+    )
+
+
 def solution(mesh):
+    planes = mesh.shape["dp"]
+    small = mesh.shape["grp"] == 8 and planes == 4
     return jax.shard_map(
-        body,
+        functools.partial(plane_body, planes) if small else body,
         mesh=mesh,
         in_specs=(
             P(("grp", "dp"), None, None),

time: 1410 us -> 315 us (0.22)
  waiting for transfers between devices: 1030 us -> 0 us
  Pallas kernels: 0 us -> 289 us
  matrix products: 136 us -> 4.73 us
  blocking collectives: 85.4 us -> 0 us
  local copies, waits for them, and re-layouts: 83.5 us -> 10.4 us
  other arithmetic: 50.5 us -> 8.34 us
  between operations: 20.6 us -> 1.41 us
    reduce_scatter x6 -> x0, waiting for transfers between devices: 643 us -> none  [the longest x1 200 us: body(): lax.psum_scatter(ada_grad, 'grp', scatter_dimension=1, tiled=True)]
    pallas_call x0 -> x2, Pallas kernels: none -> 289 us  [the longest x1 150 us: backward(): pl.pallas_call(functools.partial(backward_kernel, samples, planes), out_s...]
    all_gather x6 -> x0, waiting for transfers between devices: 233 us -> none  [the longest x1 57.4 us: body(): lax.all_gather(w_ada, 'grp', axis=1, tiled=True)]
    psum x1 -> x0, waiting for transfers between devices: 149 us -> none  [body(): lax.psum(shares[1].astype(jnp.bfloat16), 'dp').astype(jnp.float32)]
    dot_general x24 -> x3, matrix products: 135 us -> 4.73 us  [the longest x1 2.67 us: plane_body(): jnp.einsum('se,sd->ed', mod_z, cvec_z, preferred_element_type=F32)]
    scatter x2 -> x0, local copies, waits for them, and re-layouts: 53.2 us -> none  [the longest x1 26.9 us: body(): block_out = latents.at[rows, kept].set(result.astype(jnp.bfloat16))]
    unnamed x2 -> x0, blocking collectives: 52.6 us -> none
    convert_element_type x25 -> x2, other arithmetic: 35 us -> 2.63 us  [the longest x1 1.86 us: plane_body(): pieces.append(totals[at:at + size].astype(F32))]
  transfers between devices with their start and end apart: 14 -> 0, of which waited for: 11 -> 0; matrix products, arithmetic and copies ran while one was open for 14% -> 0% of each run, Pallas kernels for 0% -> 0%
where the time goes in v1:
time: 315 us; the launch traced here: 314 us
  Pallas kernels  289 us (92%)
  local copies, waits for them, and re-layouts  10.4 us (3%)
  other arithmetic  8.34 us (3%)
  matrix products  4.73 us (2%)
    pallas_call x1, Pallas kernels, backward(): pl.pallas_call(functools.partial(backward_kernel, samples, planes), out_s...  150 us
    pallas_call x1, Pallas kernels, forward(): pl.pallas_call(functools.partial(forward_kernel, samples), out_shape=[sha...  139 us

profile of v1, /device:TPU:0, one launch (start us, length us, event | category | flops | bytes accessed | tf_op | source)
XLA Modules:
  0.0 314.3 jit_solution(8094507304134053495)
XLA Ops:
  1.3 0.8 maximum_convert_fusion
  2.1 0.7 reshape.66.bias_ref
  2.7 1.3 reshape.67.bada_ref
  4.0 1.3 reshape.68.b1_ref
  5.3 139.2 %shard_map.281 = (bf16[8,576,1152]{2,1,0:T(8,128)(2,1)}, bf16[8,256,576]{2,1,0:T(8,128)(2,1)}, bf16[48,72,256]{2,1,0:T(8,128)(2,1)}, bf16[8,144,256]{2,1,0:T(8,1...) custom-call(s32[2]{0:T(128)} %labels_ref.1, ...), custom_call_target="tpu_custom_call" | custom-call | tf_op jit(solution)/shard_map/pallas_call | solution.py:801
  144.5 150.3 %shard_map.282 = (bf16[12,144,1152]{2,1,0:T(8,128)(2,1)}, bf16[2,256,1152]{2,1,0:T(8,128)(2,1)}, bf16[2,256,1152]{2,1,0:T(8,128)(2,1)}, f32[4,16,864]{2,1,0:T(8,...) custom-call(s32[1]{0:T(128)S(6)} %copy.41.counts_ref, ...), custom_call_target="tpu_custom_call" | custom-call | tf_op jit(solution)/shard_map/pallas_call | solution.py:1157
  294.7 1.9 fusion.5
  296.7 0.0 copy-start.2
  296.7 0.0 copy-start.4
  296.7 2.9 convert_bitcast_fusion
  299.6 0.0 copy-done.2
  299.7 0.6 constant_dynamic-slice_fusion
  300.3 0.1 reshape.65
  300.4 0.7 fusion.4
  301.1 0.0 copy-done.4
  301.1 0.1 copy.36
  301.2 0.3 reshape.64
  301.4 0.0 copy-done.5
  301.4 0.6 convert_reduce_fusion
  302.1 2.7 fusion.9
  304.7 0.0 copy-done.6
  304.7 0.1 fusion.7
  304.8 0.1 copy.38
  304.9 1.3 fusion
  306.2 1.3 slice.42
  307.5 1.5 convert_bitcast_fusion.1
  309.0 0.1 copy.37
  309.0 0.8 fusion.2
  309.8 1.9 bitcast_convert_fusion.1
  311.7 0.6 slice_reduce_fusion
  312.3 1.0 copy.42
  313.3 1.0 copy.43
  (12 shorter events, 0.0 us)
Async XLA Ops:
  296.7 2.9 copy-start.2
  296.7 4.4 %copy-start.4 = (bf16[4,8,16,144]{3,2,1,0:T(8,128)(2,1)S(1)}, bf16[4,8,16,144]{3,2,1,0:T(8,128)(2,1)}, u32[]{:S(2)}) copy-start(bf16[4,8,16,144]{3,2,1,0:T(8,128)(2,1)} %get-tuple-element.56) | copy-start | bytes 442372
  299.6 1.8 copy-start.5
  302.1 2.7 copy-start.6
  302.1 2.8 copy-start.3
  307.5 4.8 %copy-start.1 = (bf16[2,256,1152]{2,1,0:T(8,128)(2,1)S(1)}, bf16[2,256,1152]{2,1,0:T(8,128)(2,1)}, u32[]{:S(2)}) copy-start(bf16[2,256,1152]{2,1,0:T(8,128)(2,1)} %get-tuple-element.88) | copy-start | bytes 3538948
  311.7 1.6 copy-start

commit v2 on v1

--- a/solution.py
+++ b/solution.py
@@ -321,44 +321,48 @@
 
 
 class Gather:
-    def __init__(self, place, wire, buf):
-        self.p, self.w, self.buf = place, wire, buf
-        self.first = wire.take(8)
-        self.parts = halves(buf.shape[1])
-        self.c = self.copies()
-
-    def make(self, number, block, device, part=None):
-        ref = self.buf.at[block]
-        if part is not None:
-            ref = self.buf.at[block, self.parts[part]]
-        return self.w.copy(self.first + number, ref, ref, device)
-
-    def copies(self):
-        p = self.p
+    def __init__(self, place, wire, buf, start=0, rows=None, origin=None):
+        p = place
+        rows = rows or buf.shape[1]
+        lo, hi = halves(rows)
+        parts = (pl.ds(start, rows), pl.ds(start, lo.size), pl.ds(start + lo.size, hi.size))
+        first = wire.take(8)
+
+        def make(number, block, device, part=0):
+            ref = buf.at[block, parts[part]]
+            src = origin if number < 3 and origin is not None else ref
+            return wire.copy(first + number, src, ref, device)
+
         own, xb, yb, db = p.g, p.block(0, 1, 0), p.block(0, 0, 1), p.block(0, 1, 1)
         xd, yd, sd = p.device(0, 1, 0), p.device(0, 0, 1), p.device(1, 0, 0)
-        return [
-            self.make(0, own, xd),
-            self.make(1, own, yd),
-            self.make(2, own, sd),
-            self.make(3, xb, yd, 0),
-            self.make(4, xb, sd),
-            self.make(5, yb, xd, 1),
-            self.make(6, yb, sd),
-            self.make(7, db, sd),
+        self.c = [
+            make(0, own, xd),
+            make(1, own, yd),
+            make(2, own, sd),
+            make(3, xb, yd, 1),
+            make(4, xb, sd),
+            make(5, yb, xd, 2),
+            make(6, yb, sd),
+            make(7, db, sd),
         ]
 
     def start(self):
         for number in (0, 1, 2):
             self.c[number].start()
 
+    def arrived(self):
+        self.c[0].wait_recv()
+        self.c[1].wait_recv()
+        self.c[4].start()
+        self.c[6].start()
+
+    def forward(self):
+        self.c[3].start()
+        self.c[5].start()
+
     def neighbours(self):
-        self.c[0].wait_recv()
-        self.c[3].start()
-        self.c[4].start()
-        self.c[1].wait_recv()
-        self.c[5].start()
-        self.c[6].start()
+        self.arrived()
+        self.forward()
 
     def far(self):
         self.c[3].wait_recv()
@@ -394,7 +398,7 @@
         f, w = self.first, wire
         lo, hi = self.parts
         whole = pl.ds(0, self.rows)
-        self.s1 = [w.copy(f + q, buf.at[self.sib[q], whole], r1.at[q], sd) for q in range(4)]
+        self.s1 = [w.copy(f + q, buf.at[self.sib[q], whole], r1.at[q, whole], sd) for q in range(4)]
         self.s2 = [
             w.copy(f + 4, buf.at[self.mine[3], lo], r2.at[0, pl.ds(0, lo.size)], xd),
             w.copy(f + 5, buf.at[self.mine[3], hi], r2.at[1, pl.ds(0, hi.size)], yd),
@@ -411,7 +415,7 @@
 
     def add_sib(self, q):
         self.s1[q].wait_recv()
-        add_into(self.buf.at[self.mine[q], pl.ds(0, self.rows)], self.r1.at[q])
+        add_into(self.buf.at[self.mine[q], pl.ds(0, self.rows)], self.r1.at[q, pl.ds(0, self.rows)])
 
     def send_far(self):
         self.add_sib(3)
@@ -490,7 +494,7 @@
 
 def params(collective_id):
     return pltpu.CompilerParams(
-        collective_id=collective_id, has_side_effects=True, vmem_limit_bytes=62 * 2**20
+        collective_id=collective_id, has_side_effects=True, vmem_limit_bytes=63 * 2**20
     )
 
 
@@ -549,7 +553,7 @@
     return y * 4 + x * 2 + c
 
 
-MSG_PROJ, MSG_FC2, MSG_QV, MSG_ROWS = 8, 16, 24, 40
+MSG_PROJ, MSG_FC2, MSG_QV, MSG_ROWS = 0, 8, 16, 32
 
 
 def sample_weight(place, counts_ref, samples, s):
@@ -558,326 +562,68 @@
     return (jnp.where(used, 1.0, 0.0) / count.astype(F32))[:, 0:1]
 
 
-def forward_kernel(samples, labels_ref, bands_ref, counts_ref, wq_ref, wp_ref, bias_ref, kept_ref, lat_ref, cot_ref, class_ref,
-                   time_ref, ada_ref, bada_ref, w1_ref, b1_ref, w2_ref,
-                   w_out, act_out, units_out, att_out, h1_out, mixed_out, proj_out, g1_out, g2_out, gb1_out, dh2_out, mod_out,
-                   cond_out, vec_out, ids_out,
-                   w_all, msg_all, cond_all, mod_in, mod_send, mod, h1, units, att, proj, mixed, vec, h2_all, dm_all, act, dpre,
-                   pbuf, p1, p2, p3, acc, send, recv, sems):
+ANY = pl.BlockSpec(memory_space=pl.ANY)
+SMEM = pl.BlockSpec(memory_space=pltpu.SMEM)
+CHUNK = 144
+
+
+def block_kernel(samples, planes, labels_ref, bands_ref, counts_ref, wq_hbm, wp_hbm, w1_hbm, w2_hbm, ada_hbm, lat_hbm, cot_hbm,
+                 bias_ref, kept_ref, class_ref, time_ref, bada_ref, b1_ref,
+                 out_hbm, block_hbm, latg_hbm, wq_keep, dmod_z, dcond_z, cvec_z, sum_z, ids_z,
+                 wq, wp, w1, w2, h1_all, h2_all, dm_all, act, dpre, p1, p2, p3, units, att, mixed, proj, grad, dx2, tmp, rest,
+                 dproj, dq, dq_all, from_end, out, g1, g2, gq, gp, gb1, ids_all, msg_all, cond_all, mod_in, mod_send, mod, vec,
+                 dc_send, dc_in, bundle, bundles, send, recv, credits, sems, out_sems):
     p = Place()
     wire = Wire(send, recv)
-    greet(plane(p))
-    g = p.g
-    length = lat_ref.shape[1]
+    g, z = p.g, p.z
+    others = [(g, (z + k) % planes) for k in range(1, planes)]
+    greet(plane(p) + others)
+    length = lat_hbm.shape[1]
     keep = kept_ref.shape[1]
-    rows, width = h1.shape
+    rows, width = mixed.shape
     pair = 2 * HEAD_DIM
-    lanes = lax.broadcasted_iota(jnp.int32, (1, msg_all.shape[2]), 1)
-    msg_all[g, 0:8] = jnp.zeros((8, msg_all.shape[2]), F32)
-    for s in range(samples):
-        line = jnp.where(lanes == 0, labels_ref[s], 0) + jnp.where(lanes == 1, bands_ref[s], 0)
-        msg_all[g, s : s + 1, :] = line.astype(F32)
-    msg_all[g, 8:MSG_ROWS] = jnp.zeros((MSG_ROWS - 8, msg_all.shape[2]), F32)
-    for row in range(4):
-        at = MSG_PROJ + 8 * row
-        msg_all[g, at : at + 1, :] = bias_ref[row : row + 1, :]
-    msgs = to_all(p, wire, lambda rel: (msg_all.at[g], msg_all.at[g]))
-    w_all[g, 0 : 3 * pair] = wq_ref[...]
-    w_all[g, 3 * pair : 4 * pair] = wp_ref[...]
-    weights = Gather(p, wire, w_all)
-    weights.start()
+    hidden_units = act.shape[2]
+    ada_rest = ada_hbm.shape[0] - hidden_units
+
+    loads = {}
+    for number, (name, src, dst) in enumerate((
+        ("wq", wq_hbm, wq.at[g]),
+        ("wp", wp_hbm, wp.at[g]),
+        ("lat", lat_hbm, h2_all.at[pl.ds(0, samples)]),
+        ("cot", cot_hbm, h2_all.at[pl.ds(samples, samples)]),
+        ("ada1", ada_hbm.at[pl.ds(0, hidden_units)], w1),
+        ("ada2", ada_hbm.at[pl.ds(hidden_units, ada_rest)], w2.at[pl.ds(0, ada_rest)]),
+        ("w1", w1_hbm, w1),
+        ("w2", w2_hbm, w2),
+        ("keep", wq, wq_keep),
+        ("again", wq_keep, wq),
+        ("ada1b", ada_hbm.at[pl.ds(0, hidden_units)], w1),
+        ("ada2b", ada_hbm.at[pl.ds(hidden_units, ada_rest)], w2.at[pl.ds(0, ada_rest)]),
+        ("latb", lat_hbm, wq.at[pl.ds(0, samples), pl.ds(0, length)]),
+        ("cotb", cot_hbm, wq.at[pl.ds(samples, samples), pl.ds(0, length)]),
+        ("block", wq.at[pl.ds(0, samples), pl.ds(0, length)], block_hbm),
+        ("latg", wq.at[pl.ds(samples, samples), pl.ds(0, length)], latg_hbm),
+    )):
+        loads[name] = local(src, dst, sems.at[number])
+    odd = z % 2
+    there = (g, z + 1 - 2 * odd)
+    ahead, behind = 2 * pair * odd, 2 * pair * (1 - odd)
+    gather_a = Gather(p, wire, wq, ahead, pair, wq_hbm.at[pl.ds(ahead, pair)])
+    gather_m = Gather(p, wire, wq, pair, pair, wq_hbm.at[pl.ds(pair, pair)])
+    first = wire.take(7)
+    near = [p.block(0, 1, 0), p.block(0, 0, 1), p.block(0, 1, 1)]
+    sd = p.device(1, 0, 0)
+    across_z = [wire.copy(first + i, wq.at[b, pl.ds(ahead, pair)], wq.at[b, pl.ds(ahead, pair)], there) for i, b in enumerate(near)]
+    own_sib = wire.copy(first + 3, wq_hbm.at[pl.ds(behind, pair)], wq.at[g, pl.ds(behind, pair)], sd)
+    from_z = [wire.copy(first + 4 + i, wq.at[b, pl.ds(behind, pair)], wq.at[b, pl.ds(behind, pair)], sd) for i, b in enumerate(near)]
+    outward = Gather(p, wire, wp, origin=wp_hbm)
     main = Gather(p, wire, h2_all)
     back = Gather(p, wire, dm_all)
-    sums = Scatter(p, wire, pbuf, p1, p2, p3)
-
-    for s in range(samples):
-        hot = own_tokens(kept_ref, length, s)
-        at = pl.ds(s * keep, keep)
-        mixed[at] = dot(hot, lat_ref[s], (0, 0))
-        proj[at] = dot(hot, cot_ref[s], (0, 0)) * sample_weight(p, counts_ref, samples, s)
-
-    wait_recv(msgs)
-    labels = jnp.concatenate([msg_all[j, 0:samples, 0:1] for j in range(8)], 0)
-    bands = jnp.concatenate([msg_all[j, 0:samples, 1:2] for j in range(8)], 0)
-
-    def one_hot(ids, size):
-        lanes = lax.broadcasted_iota(jnp.int32, (ids.shape[0], size), 1).astype(F32)
-        return jnp.where(lanes == ids, 1.0, 0.0).astype(BF16)
-
-    of_band = dot(one_hot(bands, time_ref.shape[0]), time_ref[...], (1, 0))
-    cond_all[g] = of_band + dot(one_hot(labels, class_ref.shape[1]), class_ref[...], (1, 1))
-    ids_out[...] = jnp.zeros_like(ids_out)
-    ids_out[:, 0:1] = labels
-    ids_out[:, 1:2] = bands
-    conds = to_all(p, wire, lambda rel: (cond_all.at[g], cond_all.at[g]))
-    wait_recv(conds)
-    value = jnp.concatenate([cond_all[j] for j in range(8)], 1)
-    value = (value * jax.nn.sigmoid(value)).astype(BF16)
-    mods = dot(value, ada_ref[...], (1, 1)) + bada_ref[...]
-    mod_send[...] = jnp.zeros_like(mod_send)
-    for j in range(8):
-        mod_send[j, 0:samples, :] = mods[samples * j : samples * (j + 1), :]
-    mod_in[g] = mod_send[g]
-    modc = to_all(p, wire, lambda rel: (mod_send.at[p.block(*rel)], mod_in.at[g]))
-    vec[...] = jnp.zeros_like(vec)
-    for row, at in ((0, MSG_PROJ), (1, MSG_FC2)):
-        vec[row : row + 1, :] = jnp.concatenate([msg_all[j, at : at + 1, :] for j in range(8)], 1)
-    wait_recv(modc)
-    mod[...] = jnp.zeros_like(mod)
-    for s in range(samples):
-        line = jnp.concatenate([mod_in[j, s : s + 1, :] for j in range(8)], 1)
-        for v in range(6):
-            mod[s, v : v + 1, :] = line[:, v * width : (v + 1) * width]
-
-    def first(s, at):
-        hat, inv = normed(mixed[at])
-        h1[at] = (hat * (1.0 + mod[s, 1:2, :]) + mod[s, 0:1, :]).astype(BF16)
-        dm_all[g, at] = (mod[s, 5:6, :] * proj[at]).astype(BF16)
-
-    by_rows(samples, keep, first)
-
-    ones = jnp.ones((8, rows), BF16)
-
-    @pl.loop(0, 8)
-    def _(t):
-        @pl.when(t == 1)
-        def _():
-            weights.wait_sib()
-
-        @pl.when(t == 2)
-        def _():
-            weights.neighbours()
-            back.start()
-
-        @pl.when(t == 4)
-        def _():
-            weights.wait_sib_neighbours()
-
-        @pl.when(t == 6)
-        def _():
-            weights.far()
-
-        @pl.when(t == 7)
-        def _():
-            weights.wait_sib_far()
-
-        block = arrival(p, t)
-        for i in range(3):
-            chunk = block * 3 + i
-            bias_at = jnp.where(chunk >= 16, chunk - 8, chunk)
-            keys = (chunk >= 8) & (chunk < 16)
-            line = msg_all[lax.div(bias_at, 2), pl.ds(pl.multiple_of(MSG_QV + 8 * lax.rem(bias_at, 2), 8), 8), :]
-            line = line * jnp.where(keys, 0.0, 1.0)
-            value = dot(w_all[block, i * pair : (i + 1) * pair, :], h1[...], (1, 1))
-            value = value + dot(line.astype(BF16), ones, (0, 0))
-            units[2 * chunk] = value[:HEAD_DIM].astype(BF16)
-            units[2 * chunk + 1] = value[HEAD_DIM:].astype(BF16)
-
-    outs = [
-        local(w_all, w_out, sems.at[0]),
-        local(units, units_out, sems.at[1]),
-        local(h1, h1_out, sems.at[2]),
-        local(mod, mod_out, sems.at[3]),
-        local(cond_all, cond_out, sems.at[4]),
-        local(vec, vec_out, sems.at[5]),
-        local(att, att_out, sems.at[6]),
-        local(proj, proj_out, sems.at[7]),
-        local(mixed, mixed_out, sems.at[8]),
-        local(act, act_out, sems.at[9]),
-    ]
-    for copy in outs[:6]:
-        copy.start()
-    proj[...] = jnp.zeros_like(proj)
-
-    @pl.loop(0, 8)
-    def _(u):
-        @pl.when(u == 6)
-        def _():
-            back.neighbours()
-
-        for s in range(samples):
-            lanes = pl.ds(s * keep, keep)
-            pieces = []
-            for e in range(2):
-                probs = probabilities(units[2 * u + e, :, lanes], units[16 + 2 * u + e, :, lanes])
-                pieces.append(dot(units[32 + 2 * u + e, :, lanes], probs.astype(BF16), (1, 1)))
-            att[u, :, lanes] = jnp.concatenate(pieces, 0).astype(BF16)
-        proj[...] += dot(att[u], w_all[u, pl.ds(3 * pair, pair), :], (0, 0))
-
-    def second(s, at):
-        proj[at] = proj[at] + vec[0:1, :]
-        mixed[at] = mixed[at] + mod[s, 2:3, :] * proj[at]
-        hat, inv = normed(mixed[at])
-        h2_all[g, at] = (hat * (1.0 + mod[s, 4:5, :]) + mod[s, 3:4, :]).astype(BF16)
-
-    by_rows(samples, keep, second)
-    main.start()
-    back.far()
-    for copy in outs[6:9]:
-        copy.start()
-
-    gb1_out[...] = jnp.zeros_like(gb1_out)
-
-    def hidden(block):
-        pre = dot(h2_all[block], w1_ref[...], (1, 1)) + b1_ref[...]
-        value, slope = gelu_parts(pre)
-        act[block] = value.astype(BF16)
-        low = (dot(dm_all[block], w2_ref[...], (1, 1)) * slope).astype(BF16)
-        dpre[block] = low
-        gb1_out[...] += jnp.sum(low.astype(F32), 0, keepdims=True)
-        pbuf[block] = dot(low, w1_ref[...], (1, 0)).astype(BF16)
-
-    @pl.loop(0, 8)
-    def _(t):
-        @pl.when(t == 1)
-        def _():
-            main.wait_sib()
-            back.wait_sib()
-
-        @pl.when(t == 2)
-        def _():
-            main.neighbours()
-            back.wait_sib_neighbours()
-            back.wait_sib_far()
-
-        @pl.when(t == 4)
-        def _():
-            main.wait_sib_neighbours()
-
-        @pl.when(t == 6)
-        def _():
-            main.far()
-
-        @pl.when(t == 7)
-        def _():
-            main.wait_sib_far()
-
-        hidden(arrival(p, t))
-        for at, q in ((1, 0), (4, 1), (5, 2), (7, 3)):
-
-            @pl.when(t == at)
-            def _(q=q):
-                sums.send_sib(q)
-
-    outs[9].start()
-    sums.send_far()
-    sums.send_near()
-
-    tile = acc.shape[1]
-    for left, right, out in ((dpre, h2_all, g1_out), (act, dm_all, g2_out)):
-        for n in range(width // tile):
-            at = pl.ds(n * tile, tile)
-            acc[...] = jnp.zeros_like(acc)
-
-            @pl.loop(0, 8)
-            def _(block, left=left, right=right, at=at):
-                acc[...] += dot(left[block], right[block, :, at], (0, 0))
-
-            out[:, at] = acc[...].astype(BF16)
-        if left is dpre:
-            sums.relay()
-    sums.result(dh2_out)
-    for piece in (weights, main, back, sums):
-        piece.finish()
-    for copies in (msgs, conds, modc):
-        wait_send(copies)
-    for copy in outs:
-        copy.wait()
-
-
-ANY = pl.BlockSpec(memory_space=pl.ANY)
-
-
-SMEM = pl.BlockSpec(memory_space=pltpu.SMEM)
-
-
-def forward(samples, labels, bands, counts, wq, wp, bias, kept, lat, cot, class_table, time_table, w_ada, b_ada, w1, b1, w2):
-    keep, width = kept.shape[1], wq.shape[1]
-    rows, hidden, count = samples * keep, w1.shape[0], 8 * samples
-    shape = jax.ShapeDtypeStruct
-    mods = (8, 8, w_ada.shape[0])
-    cond = (8, count, class_table.shape[0])
-    w = (8, wq.shape[0] + wp.shape[0], width)
-    return pl.pallas_call(
-        functools.partial(forward_kernel, samples),
-        out_shape=[
-            shape(w, BF16),
-            shape((8, rows, hidden), BF16),
-            shape((48, HEAD_DIM, rows), BF16),
-            shape((8, 2 * HEAD_DIM, rows), BF16),
-            shape((rows, width), BF16),
-            shape((rows, width), F32),
-            shape((rows, width), F32),
-            shape((hidden, width), BF16),
-            shape((hidden, width), BF16),
-            shape((1, hidden), F32),
-            shape((rows, width), F32),
-            shape((samples, 8, width), F32),
-            shape(cond, F32),
-            shape((8, width), F32),
-            shape((count, 128), F32),
-        ],
-        in_specs=[SMEM] * 3 + [VMEM] * 13,
-        out_specs=[ANY] * 7 + [VMEM] * 4 + [ANY] * 3 + [VMEM],
-        scratch_shapes=[
-            pltpu.VMEM(w, BF16),
-            pltpu.VMEM((8, MSG_ROWS, wp.shape[0]), F32),
-            pltpu.VMEM(cond, F32),
-            pltpu.VMEM(mods, F32),
-            pltpu.VMEM(mods, F32),
-            pltpu.VMEM((samples, 8, width), F32),
-            pltpu.VMEM((rows, width), BF16),
-            pltpu.VMEM((48, HEAD_DIM, rows), BF16),
-            pltpu.VMEM((8, 2 * HEAD_DIM, rows), BF16),
-            pltpu.VMEM((rows, width), F32),
-            pltpu.VMEM((rows, width), F32),
-            pltpu.VMEM((8, width), F32),
-            pltpu.VMEM((8, rows, width), BF16),
-            pltpu.VMEM((8, rows, width), BF16),
-            pltpu.VMEM((8, rows, hidden), BF16),
-            pltpu.VMEM((8, rows, hidden), BF16),
-            pltpu.VMEM((8, rows, width), BF16),
-            *scatter_scratch(rows, width),
-            pltpu.VMEM((hidden, width // 3), F32),
-            pltpu.SemaphoreType.DMA((55,)),
-            pltpu.SemaphoreType.DMA((55,)),
-            pltpu.SemaphoreType.DMA((10,)),
-        ],
-        compiler_params=params(1),
-    )(labels, bands, counts, wq, wp, bias, kept, lat, cot, class_table, time_table, w_ada, b_ada, w1, b1, w2)
-
-
-CHUNK = 144
-
-
-def backward_kernel(samples, planes, counts_ref, w_hbm, act_hbm, units_hbm, att_hbm, h1_ref, mixed_ref, proj_ref, g1_ref, g2_ref, gb1_ref,
-                    dh2_ref, mod_ref, cond_ref, vec_ref, ids_ref, kept_ref, lat_ref, cot_ref, ada_ref, w2_ref,
-                    out, block_out, lat_out, dmod_z, dcond_z, cvec_z, sum_z, ids_z,
-                    wt, wp, act, units, att, h1_all, dx2, dproj, dq, dq_all, from_end, gq, gp, qr1, qr2, qr3, pr1, pr2, pr3,
-                    mlp, dh1, grad, dmod_send, dmod_in, dc_send, dc_in, bundle, bundles, send, recv, sems):
-    p = Place()
-    wire = Wire(send, recv)
-    others = [(p.g, (p.z + k) % planes) for k in range(1, planes)]
-    greet(plane(p) + others)
-    g, z = p.g, p.z
-    length = lat_ref.shape[1]
-    keep = kept_ref.shape[1]
-    rows, width = dx2.shape
-    pair = 2 * HEAD_DIM
-    loads = [
-        local(w_hbm.at[:, pl.ds(3 * pair, pair)], wp, sems.at[0]),
-        local(units_hbm, units, sems.at[1]),
-        local(att_hbm, att, sems.at[2]),
-        local(w_hbm.at[:, pl.ds(0, 3 * pair)], wt, sems.at[3]),
-        local(act_hbm, act, sems.at[4]),
-    ]
-    for copy in loads:
-        copy.start()
-
-    sources = []
-    for ref in (g1_ref, g2_ref, gp, gq):
-        for start in range(0, ref.shape[0], CHUNK):
-            sources.append(ref.at[pl.ds(start, CHUNK)])
+    tokens = Gather(p, wire, h1_all)
+    sums = Scatter(p, wire, wq, p1, p2, p3, rows)
+    outs = Scatter(p, wire, h2_all, dm_all.at[pl.ds(0, 4)], dm_all.at[pl.ds(4, 2)], dm_all.at[pl.ds(6, 2)])
+    projs = Scatter(p, wire, wp, p1, p2, p3)
+    sources = [ref.at[pl.ds(start, CHUNK)] for ref in (g1, g2, gq, gp) for start in range(0, ref.shape[0], CHUNK)]
     count = len(sources)
     up, across, down = wire.take(count), wire.take(count), wire.take(count)
     inner, outer, partner = 1 + z // 3, (z - 1) * 3, 3 - z
@@ -885,6 +631,7 @@
     ups = [wire.copy(up + k, sources[k], from_end.at[k], (g, inner)) for k in range(count)]
     acrosses = [wire.copy(across + k, from_end.at[k], out.at[k], (g, partner)) for k in range(count)]
     downs = [wire.copy(down + k, out.at[k], out.at[k], (g, outer)) for k in range(count)]
+    results = [local(out.at[k], out_hbm.at[k], out_sems.at[k]) for k in range(count)]
 
     def chain_send(*numbers):
         @pl.when(at_end)
@@ -904,26 +651,290 @@
                     acrosses[k - 1].wait_recv()
                     add_into(out.at[k - 1], from_end.at[k - 1])
                     downs[k - 1].start()
-
-    chain_send(*range(8))
-
-    tokens = Gather(p, wire, h1_all)
-    h1_all[g] = h1_ref[...]
-    tokens.start()
-
-    value = cond_ref[...]
-    cvec_z[z] = (value * jax.nn.sigmoid(value)).astype(BF16)
-    ids_z[z] = ids_ref[...]
-    first = wire.take(2 * (planes - 1))
-    cvecs = [wire.copy(first + k, cvec_z.at[z], cvec_z.at[z], device) for k, device in enumerate(others)]
-    first += planes - 1
-    cvecs += [wire.copy(first + k, ids_z.at[z], ids_z.at[z], device) for k, device in enumerate(others)]
-    for copy in cvecs:
-        copy.start()
-
+                    results[k - 1].start()
+
+    def to_planes(ref):
+        first = wire.take(planes - 1)
+        copies = [wire.copy(first + k, ref.at[z], ref.at[z], device) for k, device in enumerate(others)]
+        for copy in copies:
+            copy.start()
+        return copies
+
+    neighbours = [p.device(1, 0, 0), p.device(0, 1, 0), p.device(0, 0, 1)]
+
+    def grant(number):
+        for i, device in enumerate(neighbours):
+            pl.semaphore_signal(credits.at[number, i], inc=1, device_id=device, device_id_type=MESH)
+
+    def granted(number):
+        for i in range(3):
+            pl.semaphore_wait(credits.at[number, i], 1)
+
+    lanes = lax.broadcasted_iota(jnp.int32, (1, 128), 1)
+    ids_all[g] = jnp.zeros((8, 128), F32)
+    for s in range(samples):
+        line = jnp.where(lanes == 0, labels_ref[s], 0) + jnp.where(lanes == 1, bands_ref[s], 0)
+        ids_all[g, s : s + 1, :] = line.astype(F32)
+    idc = to_all(p, wire, lambda rel: (ids_all.at[g], ids_all.at[g]))
+    gather_a.start()
+    for name in ("lat", "cot", "ada1", "ada2", "wq", "wp"):
+        loads[name].start()
+    msg_all[g] = jnp.zeros(msg_all.shape[1:], F32)
+    for row in range(4):
+        at = MSG_PROJ + 8 * row
+        msg_all[g, at : at + 1, :] = bias_ref[row : row + 1, :]
+
+    wait_recv(idc)
+    labels = jnp.concatenate([ids_all[j, 0:samples, 0:1] for j in range(8)], 0)
+    bands = jnp.concatenate([ids_all[j, 0:samples, 1:2] for j in range(8)], 0)
+
+    def one_hot(ids, size):
+        lanes = lax.broadcasted_iota(jnp.int32, (ids.shape[0], size), 1).astype(F32)
+        return jnp.where(lanes == ids, 1.0, 0.0).astype(BF16)
+
+    of_band = dot(one_hot(bands, time_ref.shape[0]), time_ref[...], (1, 0))
+    cond_all[g] = of_band + dot(one_hot(labels, class_ref.shape[1]), class_ref[...], (1, 1))
+    conds = to_all(p, wire, lambda rel: (cond_all.at[g], cond_all.at[g]))
+    ids_z[z] = jnp.zeros(ids_z.shape[1:], F32)
+    ids_z[z, :, 0:1] = labels
+    ids_z[z, :, 1:2] = bands
+    gather_m.start()
+    own_sib.start()
+
+    loads["lat"].wait()
+    loads["cot"].wait()
     for s in range(samples):
         hot = own_tokens(kept_ref, length, s)
-        grad[pl.ds(s * keep, keep)] = dot(hot, cot_ref[s], (0, 0)) * sample_weight(p, counts_ref, samples, s)
+        at = pl.ds(s * keep, keep)
+        mixed[at] = dot(hot, h2_all[s], (0, 0))
+        grad[at] = dot(hot, h2_all[samples + s], (0, 0)) * sample_weight(p, counts_ref, samples, s)
+
+    gather_a.arrived()
+    across_z[0].start()
+    across_z[1].start()
+    zs = [to_planes(ids_z)]
+    wait_recv(conds)
+    value = cond_all[...]
+    value = value * jax.nn.sigmoid(value)
+    cvec_z[z] = value.astype(BF16)
+    zs.append(to_planes(cvec_z))
+    value = jnp.concatenate([value[j] for j in range(8)], 1).astype(BF16)
+    loads["ada1"].wait()
+    loads["ada2"].wait()
+    mods = [dot(value, w1[...], (1, 1)), dot(value, w2[0:ada_rest], (1, 1))]
+    mods = jnp.concatenate(mods, 1) + bada_ref[...]
+    mod_send[...] = jnp.zeros_like(mod_send)
+    for j in range(8):
+        mod_send[j, 0:samples, :] = mods[samples * j : samples * (j + 1), :]
+    mod_in[g] = mod_send[g]
+    modc = to_all(p, wire, lambda rel: (mod_send.at[p.block(*rel)], mod_in.at[g]))
+    msgs = to_all(p, wire, lambda rel: (msg_all.at[g], msg_all.at[g]))
+    gather_a.forward()
+    loads["w1"].start()
+    loads["w2"].start()
+    wait_recv(modc)
+    mod[...] = jnp.zeros_like(mod)
+    for s in range(samples):
+        line = jnp.concatenate([mod_in[j, s : s + 1, :] for j in range(8)], 1)
+        for v in range(6):
+            mod[s, v : v + 1, :] = line[:, v * width : (v + 1) * width]
+
+    def first_norm(s, at):
+        hat, inv = normed(mixed[at])
+        h1_all[g, at] = (hat * (1.0 + mod[s, 1:2, :]) + mod[s, 0:1, :]).astype(BF16)
+        dm_all[g, at] = (mod[s, 5:6, :] * grad[at]).astype(BF16)
+
+    gather_m.neighbours()
+    outward.start()
+    by_rows(samples, keep, first_norm)
+    wait_recv(msgs)
+    vec[...] = jnp.zeros_like(vec)
+    for row, at in ((0, MSG_PROJ), (1, MSG_FC2)):
+        vec[row : row + 1, :] = jnp.concatenate([msg_all[j, at : at + 1, :] for j in range(8)], 1)
+
+    ones = jnp.ones((8, rows), BF16)
+    loads["wq"].wait()
+
+    @pl.loop(0, 24)
+    def _(n):
+        for base, gather in ((0, gather_a), (8, gather_m)):
+
+            @pl.when(n == base + 1)
+            def _(gather=gather):
+                gather.wait_sib()
+
+            @pl.when(n == base + 4)
+            def _(gather=gather):
+                gather.wait_sib_neighbours()
+
+            @pl.when(n == base + 6)
+            def _(gather=gather, base=base):
+                gather.far()
+                if base == 0:
+                    across_z[2].start()
+
+            @pl.when(n == base + 7)
+            def _(gather=gather):
+                gather.wait_sib_far()
+
+        @pl.when(n == 17)
+        def _():
+            own_sib.wait_recv()
+
+        @pl.when(n == 18)
+        def _():
+            for i in range(2):
+                across_z[i].wait_recv()
+                from_z[i].start()
+
+        @pl.when(n == 20)
+        def _():
+            for i in range(2):
+                from_z[i].wait_recv()
+            outward.neighbours()
+            back.start()
+
+        @pl.when(n == 22)
+        def _():
+            across_z[2].wait_recv()
+            from_z[2].start()
+
+        @pl.when(n == 23)
+        def _():
+            from_z[2].wait_recv()
+
+        phase = lax.div(n, 8)
+        block = arrival(p, lax.rem(n, 8))
+        third = jnp.where(phase == 0, 2 * odd, jnp.where(phase == 1, 1, 2 - 2 * odd))
+        chunk = block * 3 + third
+        bias_at = jnp.where(chunk >= 16, chunk - 8, chunk)
+        keys = (chunk >= 8) & (chunk < 16)
+        line = msg_all[lax.div(bias_at, 2), pl.ds(pl.multiple_of(MSG_QV + 8 * lax.rem(bias_at, 2), 8), 8), :]
+        line = line * jnp.where(keys, 0.0, 1.0)
+        value = dot(wq[block, pl.ds(pl.multiple_of(third * pair, 16), pair), :], h1_all[g], (1, 1))
+        value = value + dot(line.astype(BF16), ones, (0, 0))
+        units[2 * chunk] = value[:HEAD_DIM].astype(BF16)
+        units[2 * chunk + 1] = value[HEAD_DIM:].astype(BF16)
+
+    loads["keep"].start()
+
+    @pl.loop(0, 8)
+    def _(u):
+        @pl.when(u == 1)
+        def _():
+            outward.far()
+
+        for s in range(samples):
+            lanes = pl.ds(s * keep, keep)
+            pieces = []
+            for e in range(2):
+                probs = probabilities(units[2 * u + e, :, lanes], units[16 + 2 * u + e, :, lanes])
+                pieces.append(dot(units[32 + 2 * u + e, :, lanes], probs.astype(BF16), (1, 1)))
+            att[u, :, lanes] = jnp.concatenate(pieces, 0).astype(BF16)
+
+    loads["wp"].wait()
+    outward.wait_sib()
+    outward.wait_sib_neighbours()
+    outward.wait_sib_far()
+    proj[...] = jnp.zeros_like(proj)
+
+    @pl.loop(0, 8)
+    def _(u):
+        proj[...] += dot(att[u], wp[u], (0, 0))
+
+    def second_norm(s, at):
+        proj[at] = proj[at] + vec[0:1, :]
+        mixed[at] = mixed[at] + mod[s, 2:3, :] * proj[at]
+        hat, inv = normed(mixed[at])
+        h2_all[g, at] = (hat * (1.0 + mod[s, 4:5, :]) + mod[s, 3:4, :]).astype(BF16)
+
+    back.neighbours()
+    by_rows(samples, keep, second_norm)
+    main.start()
+    back.far()
+    gb1[...] = jnp.zeros_like(gb1)
+    for piece in (gather_a, gather_m):
+        piece.finish()
+    wait_send(across_z + from_z + [own_sib])
+    loads["w1"].wait()
+    loads["w2"].wait()
+    loads["keep"].wait()
+
+    def hidden(block):
+        pre = dot(h2_all[block], w1[...], (1, 1)) + b1_ref[...]
+        value, slope = gelu_parts(pre)
+        act[block] = value.astype(BF16)
+        low = (dot(dm_all[block], w2[...], (1, 1)) * slope).astype(BF16)
+        dpre[block] = low
+        gb1[...] += jnp.sum(low.astype(F32), 0, keepdims=True)
+        wq[block, pl.ds(0, rows)] = dot(low, w1[...], (1, 0)).astype(BF16)
+
+    @pl.loop(0, 8)
+    def _(t):
+        @pl.when(t == 1)
+        def _():
+            main.wait_sib()
+            back.wait_sib()
+
+        @pl.when(t == 2)
+        def _():
+            main.neighbours()
+            back.wait_sib_neighbours()
+            back.wait_sib_far()
+
+        @pl.when(t == 4)
+        def _():
+            main.wait_sib_neighbours()
+
+        @pl.when(t == 6)
+        def _():
+            sums.send_near()
+            main.far()
+
+        @pl.when(t == 7)
+        def _():
+            main.wait_sib_far()
+
+        hidden(arrival(p, t))
+        for at, q in ((1, 0), (4, 1), (5, 2), (7, 3)):
+
+            @pl.when(t == at)
+            def _(q=q):
+                sums.send_sib(q)
+
+    sums.send_far()
+
+    def weight_grad(left, right, target):
+        pieces = [(dx2, 0, 256), (tmp, 256, 256), (rest, 512, hidden_units - 512)]
+        for ref, start, size in pieces:
+            ref[0:size] = jnp.zeros((size, width), F32)
+
+        @pl.loop(0, 4)
+        def _(i):
+            two = pl.ds(2 * i, 2)
+            values = right[two].reshape(2 * rows, width)
+            for ref, start, size in pieces:
+                part = left[two, :, pl.ds(start, size)].reshape(2 * rows, size)
+                ref[0:size] += dot(part, values, (0, 0))
+
+        for ref, start, size in pieces:
+            target[pl.ds(start, size)] = ref[0:size].astype(BF16)
+
+    weight_grad(dpre, h2_all, g1)
+    chain_send(0, 1, 2, 3)
+    sums.relay()
+    main.finish()
+    tokens.start()
+    weight_grad(act, dm_all, g2)
+    chain_send(4, 5, 6, 7)
+    back.finish()
+    grant(0)
+    sums.result(tmp)
+    sums.finish()
+    grant(1)
+    loads["again"].start()
+    chain(0)
+
     bundle[...] = jnp.zeros_like(bundle)
 
     def add_row(row, value):
@@ -931,22 +942,21 @@
 
     SUM_PROJ, SUM_FC2 = 6 * samples, 6 * samples + 1
 
-    def second(s, at):
-        hat, inv = normed(mixed_ref[at])
-        up_grad = dh2_ref[at]
-        value = grad[at] + norm_back(up_grad * (1.0 + mod_ref[s, 4:5, :]), hat, inv)
+    def second_back(s, at):
+        hat, inv = normed(mixed[at])
+        up_grad = tmp[at]
+        value = grad[at] + norm_back(up_grad * (1.0 + mod[s, 4:5, :]), hat, inv)
         dx2[at] = value
-        low = (mod_ref[s, 2:3, :] * value).astype(BF16)
+        low = (mod[s, 2:3, :] * value).astype(BF16)
         dproj[at] = low
         add_row(s * 6 + 3, up_grad)
         add_row(s * 6 + 4, up_grad * hat)
-        add_row(s * 6 + 2, value * proj_ref[at])
+        add_row(s * 6 + 2, value * proj[at])
         add_row(SUM_PROJ, low.astype(F32))
-        add_row(SUM_FC2, (mod_ref[s, 5:6, :] * grad[at]).astype(BF16).astype(F32))
-
-    by_rows(samples, keep, second)
-    for copy in loads[:3]:
-        copy.wait()
+        add_row(SUM_FC2, (mod[s, 5:6, :] * grad[at]).astype(BF16).astype(F32))
+
+    by_rows(samples, keep, second_back)
+    outward.finish()
 
     @pl.loop(0, 8)
     def _(u):
@@ -974,231 +984,262 @@
             for s in range(samples):
                 dq[lax.div(chunk, 3), at, pl.ds(s * keep, keep)] = lists[i][s]
 
-        @pl.when(u == 3)
+        @pl.when(u == 1)
+        def _():
+            chain(1)
+
+        @pl.when(u == 4)
         def _():
             tokens.neighbours()
-            chain(0)
-
-        @pl.when(u == 7)
-        def _():
-            tokens.far()
-            chain(1)
+            chain(2)
 
     dq_all[g] = dq[g]
     moves = to_all(p, wire, lambda rel: (dq.at[p.block(*rel)], dq_all.at[g]))
-    projs = Scatter(p, wire, wp, pr1, pr2, pr3)
+    granted(1)
     for q in (3, 1, 2, 0):
         projs.send_sib(q)
-    chain(2)
-
-    loads[3].wait()
-    dh1[...] = jnp.zeros_like(dh1)
+    tokens.far()
+    chain(3)
+
+    loads["again"].wait()
+    proj[...] = jnp.zeros_like(proj)
 
     @pl.loop(0, 8)
     def _(j):
-        dh1[...] += dot(dq[j], wt[j], (0, 0))
-
-    projs.send_far()
-    projs.send_near()
-    chain(3)
-
-    loads[4].wait()
-    outs = Scatter(p, wire, wt, qr1, qr2, qr3, rows)
+        proj[...] += dot(dq[j], wq[j], (0, 0))
+
+    loads["latb"].start()
+    loads["cotb"].start()
+    chain(4)
+
+    granted(0)
 
     @pl.loop(0, 8)
     def _(t):
         block = arrival(p, 7 - t)
-        wt[block, pl.ds(0, rows)] = jnp.dot(act[block], w2_ref[...], preferred_element_type=F32).astype(BF16)
+        h2_all[block] = jnp.dot(act[block], w2[...], preferred_element_type=F32).astype(BF16)
         for at, q in ((1, 0), (4, 1), (5, 2), (7, 3)):
 
             @pl.when(t == 7 - at)
             def _(q=q):
                 outs.send_sib(q)
 
+    loads["ada1b"].start()
+    loads["ada2b"].start()
+    tokens.wait_sib()
+    tokens.wait_sib_neighbours()
+    tokens.wait_sib_far()
+    chain(5)
+
+    wait_recv(moves)
+    projs.send_far()
+    projs.send_near()
+    for i in range(3):
+        at = pl.ds(i * pair, pair)
+        tmp[0:pair] = jnp.zeros((pair, width), F32)
+
+        @pl.loop(0, 8)
+        def _(j, at=at):
+            tmp[0:pair] += dot(dq_all[j, at, :], h1_all[j], (1, 0))
+
+        gq[at] = tmp[0:pair].astype(BF16)
+        chain_send(8 + i)
+        if i == 1:
+            chain(6)
     projs.relay()
     outs.send_far()
     outs.send_near()
-    chain(4)
-    projs.result(gp)
-    chain_send(8)
-
+    chain(7)
+
+    loads["latb"].wait()
+    loads["cotb"].wait()
     for s in range(samples):
         hot = own_tokens(kept_ref, length, s)
-        mlp[pl.ds(s * keep, keep)] = dot(hot, lat_ref[s], (0, 0))
-
-    def back_first(s, at):
-        hat, inv = normed(mlp[at])
-        up_grad = dh1[at]
-        dx = dx2[at] + norm_back(up_grad * (1.0 + mod_ref[s, 1:2, :]), hat, inv)
+        tmp[pl.ds(s * keep, keep)] = dot(hot, wq[s, pl.ds(0, length)], (0, 0))
+
+    def first_back(s, at):
+        hat, inv = normed(tmp[at])
+        up_grad = proj[at]
+        dx = dx2[at] + norm_back(up_grad * (1.0 + mod[s, 1:2, :]), hat, inv)
         add_row(s * 6, up_grad)
         add_row(s * 6 + 1, up_grad * hat)
         dproj[at] = dx.astype(BF16)
 
-    by_rows(samples, keep, back_first)
-    for s in range(samples):
+    by_rows(samples, keep, first_back)
+    projs.result(gp)
+    chain_send(11)
+
+    def place_tokens(s):
         hot = own_tokens(kept_ref, length, s)
         is_kept = jnp.sum(hot.astype(F32), 1, keepdims=True) > 0.5
-        spread = dot(hot, dproj[pl.ds(s * keep, keep)], (1, 0))
-        weighted = cot_ref[s].astype(F32) * sample_weight(p, counts_ref, samples, s)
-        lat_out[s] = jnp.where(is_kept, spread, weighted).astype(BF16)
-    chain(5)
-
-    tokens.wait_sib()
-    tokens.wait_sib_neighbours()
-    tokens.wait_sib_far()
-    wait_recv(moves)
-    for i in range(3):
-        at = pl.ds(i * pair, pair)
-        dh1[0:pair] = jnp.zeros((pair, width), F32)
-
-        @pl.loop(0, 8)
-        def _(j, at=at):
-            dh1[0:pair] += dot(dq_all[j, at, :], h1_all[j], (1, 0))
-
-        gq[at] = dh1[0:pair].astype(BF16)
-        chain_send(9 + i)
-    chain(6)
-
+        return is_kept, dot(hot, dproj[pl.ds(s * keep, keep)], (1, 0))
+
+    for s in range(samples):
+        is_kept, spread = place_tokens(s)
+        at = (samples + s, pl.ds(0, length))
+        weighted = wq[at].astype(F32) * sample_weight(p, counts_ref, samples, s)
+        wq[at] = jnp.where(is_kept, spread, weighted).astype(BF16)
+    loads["latg"].start()
+    chain(8)
     outs.relay()
-    outs.result(mlp)
+    chain(9)
+    chain(10)
+    outs.result(tmp)
 
     def end(s, at):
-        value = mlp[at] + vec_ref[1:2, :]
+        value = tmp[at] + vec[1:2, :]
         add_row(s * 6 + 5, grad[at] * value)
-        dproj[at] = (mixed_ref[at] + mod_ref[s, 5:6, :] * value).astype(BF16)
+        dproj[at] = (mixed[at] + mod[s, 5:6, :] * value).astype(BF16)
 
     by_rows(samples, keep, end)
-    chain(7)
-
-    cols = ada_ref.shape[0]
-    dmod_send[...] = jnp.zeros_like(dmod_send)
+
+    cols = ada_hbm.shape[0]
+    wait_send(modc)
+    mod_send[...] = jnp.zeros_like(mod_send)
     for s in range(samples):
         line = jnp.concatenate([bundle[s * 6 + v : s * 6 + v + 1, :] for v in range(6)], 1)
         line = line.astype(BF16).astype(F32)
         for j in range(8):
-            dmod_send[j, s : s + 1, :] = line[:, j * cols : (j + 1) * cols]
-    dmod_in[g] = dmod_send[g]
-    dmods = to_all(p, wire, lambda rel: (dmod_send.at[p.block(*rel)], dmod_in.at[g]))
+            mod_send[j, s : s + 1, :] = line[:, j * cols : (j + 1) * cols]
+    mod_in[g] = mod_send[g]
+    dmods = to_all(p, wire, lambda rel: (mod_send.at[p.block(*rel)], mod_in.at[g]))
     bundles[g, 0:8, :] = jnp.zeros((8, width), F32)
     bundles[g, 0:2, :] = bundle[SUM_PROJ : SUM_PROJ + 2, :]
-    ones = jnp.ones((8, rows), BF16)
     for j in range(8):
         line = dot(ones, dq[j], (1, 1))
         bundles[g, 8 + j : 9 + j, 0 : 3 * pair] = line[0:1, :]
-    sums = to_all(p, wire, lambda rel: (bundles.at[g], bundles.at[g]))
+    small = to_all(p, wire, lambda rel: (bundles.at[g], bundles.at[g]))
 
     for s in range(samples):
-        hot = own_tokens(kept_ref, length, s)
-        is_kept = jnp.sum(hot.astype(F32), 1, keepdims=True) > 0.5
-        spread = dot(hot, dproj[pl.ds(s * keep, keep)], (1, 0))
-        block_out[s] = jnp.where(is_kept, spread, lat_ref[s].astype(F32)).astype(BF16)
-
+        is_kept, spread = place_tokens(s)
+        at = (s, pl.ds(0, length))
+        wq[at] = jnp.where(is_kept, spread, wq[at].astype(F32)).astype(BF16)
+    loads["block"].start()
+    loads["ada1b"].wait()
+    loads["ada2b"].wait()
     wait_recv(dmods)
-    part = jnp.concatenate([dmod_in[j, 0:samples, :] for j in range(8)], 0)
+    part = jnp.concatenate([mod_in[j, 0:samples, :] for j in range(8)], 0)
     dmod_z[z] = part
-    first = wire.take(planes - 1)
-    dmodz = [wire.copy(first + k, dmod_z.at[z], dmod_z.at[z], device) for k, device in enumerate(others)]
-    for copy in dmodz:
-        copy.start()
-    dcvec = dot(part.astype(BF16), ada_ref[...], (1, 0))
-    depth = cond_ref.shape[2]
+    zs.append(to_planes(dmod_z))
+    part = part.astype(BF16)
+    dcvec = dot(part[:, :hidden_units], w1[...], (1, 0)) + dot(part[:, hidden_units:], w2[0:ada_rest], (1, 0))
+    depth = cond_all.shape[2]
     for j in range(8):
         dc_send[j] = dcvec[:, j * depth : (j + 1) * depth]
     dc_in[g] = dc_send[g]
     dcs = to_all(p, wire, lambda rel: (dc_send.at[p.block(*rel)], dc_in.at[g]))
-    wait_recv(sums)
+    wait_recv(small)
     sum_z[z] = sum(bundles[j] for j in range(8))
-    sum_z[z, 2:3, 0 : gb1_ref.shape[1]] = gb1_ref[...]
-    first = wire.take(planes - 1)
-    sumz = [wire.copy(first + k, sum_z.at[z], sum_z.at[z], device) for k, device in enumerate(others)]
-    for copy in sumz:
-        copy.start()
+    sum_z[z, 2:3, 0:hidden_units] = gb1[...]
+    zs.append(to_planes(sum_z))
+    chain(11)
     wait_recv(dcs)
-    cond = cond_ref[g]
+    cond = cond_all[g]
     gate = jax.nn.sigmoid(cond)
     dcond_z[z] = sum(dc_in[j] for j in range(8)) * (gate * (1.0 + cond * (1.0 - gate)))
-    first = wire.take(planes - 1)
-    dconds = [wire.copy(first + k, dcond_z.at[z], dcond_z.at[z], device) for k, device in enumerate(others)]
-    for copy in dconds:
-        copy.start()
-
-    chain(*range(8, count + 1))
+    zs.append(to_planes(dcond_z))
+    chain(12)
 
     @pl.when(jnp.logical_not(at_end))
     def _():
         for k in range(count):
             acrosses[k].wait_send()
             downs[k].wait_send()
+            results[k].wait()
 
     @pl.when(at_end)
     def _():
         for k in range(count):
             downs[k].wait_recv()
+            results[k].start()
+        for k in range(count):
             ups[k].wait_send()
-
-    for copies in (cvecs, dmodz, sumz, dconds):
+            results[k].wait()
+
+    for copies in zs:
         wait_recv(copies)
-    for copies in (moves, dmods, sums, dcs, cvecs, dmodz, sumz, dconds):
+        wait_send(copies)
+    for copies in (idc, msgs, conds, moves, dmods, small, dcs):
         wait_send(copies)
     for piece in (tokens, projs, outs):
         piece.finish()
-
-
-def backward(samples, planes, counts, w, act, units, att, h1, mixed, proj, g1, g2, gb1, dh2, mod, cond, vec, ids, kept, lat, cot,
-             w_ada, w2):
-    keep, width = kept.shape[1], h1.shape[1]
-    rows, per = samples * keep, 8 * samples
-    pair = 2 * HEAD_DIM
-    wq, wp = 3 * pair, pair
-    count = (g1.shape[0] + g2.shape[0] + wq + wp) // CHUNK
-    shape = jax.ShapeDtypeStruct
-    cols, depth = w_ada.shape[0], cond.shape[2]
-    sems = 3 * count + 8 + 5 * (planes - 1) + 7 + 10 + 10 + 7 + 7 + 7
+    loads["latg"].wait()
+    loads["block"].wait()
+
+
+def run_block(samples, planes, labels, bands, counts, wq, wp, w1, w2, w_ada, lat, cot, bias, kept, class_table, time_table, b_ada,
+              b1):
+    keep, width = kept.shape[1], wq.shape[1]
+    rows, hidden, per = samples * keep, w1.shape[0], 8 * samples
+    cols, depth = w_ada.shape[0], class_table.shape[0]
+    count = (2 * hidden + wq.shape[0] + wp.shape[0]) // CHUNK
+    shape, room = jax.ShapeDtypeStruct, pltpu.VMEM
+    blocks = room((8, rows, width), BF16)
+    plain = room((rows, width), F32)
+    copies = 8 * 6 + 7 + 3 * 10 + 3 * count + 8 * 7 + 5 * (planes - 1)
     return pl.pallas_call(
-        functools.partial(backward_kernel, samples, planes),
+        functools.partial(block_kernel, samples, planes),
         out_shape=[
             shape((count, CHUNK, width), BF16),
             shape(lat.shape, BF16),
             shape(lat.shape, BF16),
+            shape((8,) + wq.shape, BF16),
             shape((planes, per, cols), F32),
             shape((planes, per, depth), F32),
             shape((planes, 8, per, depth), BF16),
             shape((planes, 16, width), F32),
-            shape((planes,) + ids.shape, F32),
+            shape((planes, per, 128), F32),
         ],
-        in_specs=[SMEM] + [ANY] * 4 + [VMEM] * 16,
-        out_specs=[VMEM] * 8,
+        in_specs=[SMEM] * 3 + [ANY] * 7 + [VMEM] * 6,
+        out_specs=[ANY] * 4 + [VMEM] * 5,
         scratch_shapes=[
-            pltpu.VMEM((8, wq, width), BF16),
-            pltpu.VMEM((8, wp, width), BF16),
-            pltpu.VMEM(act.shape, BF16),
-            pltpu.VMEM(units.shape, BF16),
-            pltpu.VMEM(att.shape, BF16),
-            pltpu.VMEM((8, rows, width), BF16),
-            pltpu.VMEM((rows, width), F32),
-            pltpu.VMEM((rows, width), BF16),
-            pltpu.VMEM((8, wq, rows), BF16),
-            pltpu.VMEM((8, wq, rows), BF16),
-            pltpu.VMEM((count, CHUNK, width), BF16),
-            pltpu.VMEM((wq, width), BF16),
-            pltpu.VMEM((wp, width), BF16),
+            room((8,) + wq.shape, BF16),
+            room((8,) + wp.shape, BF16),
+            room(w1.shape, BF16),
+            room(w2.shape, BF16),
+            blocks,
+            blocks,
+            blocks,
+            room((8, rows, hidden), BF16),
+            room((8, rows, hidden), BF16),
             *scatter_scratch(rows, width),
-            *scatter_scratch(wp, width),
-            pltpu.VMEM((rows, width), F32),
-            pltpu.VMEM((rows, width), F32),
-            pltpu.VMEM((rows, width), F32),
-            pltpu.VMEM((8, 8, cols), F32),
-            pltpu.VMEM((8, 8, cols), F32),
-            pltpu.VMEM((8, per, depth), F32),
-            pltpu.VMEM((8, per, depth), F32),
-            pltpu.VMEM((16, width), F32),
-            pltpu.VMEM((8, 16, width), F32),
-            pltpu.SemaphoreType.DMA((sems,)),
-            pltpu.SemaphoreType.DMA((sems,)),
-            pltpu.SemaphoreType.DMA((5,)),
+            room((48, HEAD_DIM, rows), BF16),
+            room((8, 2 * HEAD_DIM, rows), BF16),
+            plain,
+            plain,
+            plain,
+            plain,
+            plain,
+            room((hidden - 512, width), F32),
+            room((rows, width), BF16),
+            room((8, wq.shape[0], rows), BF16),
+            room((8, wq.shape[0], rows), BF16),
+            room((count, CHUNK, width), BF16),
+            room((count, CHUNK, width), BF16),
+            room(w1.shape, BF16),
+            room(w1.shape, BF16),
+            room(wq.shape, BF16),
+            room(wp.shape, BF16),
+            room((1, hidden), F32),
+            room((8, 8, 128), F32),
+            room((8, MSG_ROWS, wp.shape[0]), F32),
+            room((8, per, depth), F32),
+            room((8, 8, cols), F32),
+            room((8, 8, cols), F32),
+            room((samples, 8, width), F32),
+            room((8, width), F32),
+            room((8, per, depth), F32),
+            room((8, per, depth), F32),
+            room((16, width), F32),
+            room((8, 16, width), F32),
+            pltpu.SemaphoreType.DMA((copies,)),
+            pltpu.SemaphoreType.DMA((copies,)),
+            pltpu.SemaphoreType.REGULAR((2, 3)),
+            pltpu.SemaphoreType.DMA((16,)),
+            pltpu.SemaphoreType.DMA((count,)),
         ],
-        compiler_params=params(2),
-    )(counts, w, act, units, att, h1, mixed, proj, g1, g2, gb1, dh2, mod, cond, vec, ids, kept, lat, cot, w_ada, w2)
+        compiler_params=params(1),
+    )(labels, bands, counts, wq, wp, w1, w2, w_ada, lat, cot, bias, kept, class_table, time_table, b_ada, b1)
 
 
 def plane_body(planes, latents, cotangent, bands, labels, kept, band_counts, time_table, class_table, w_ada, b_ada, w_qkv,
@@ -1211,18 +1252,14 @@
     per = 8 * samples
 
     bias = jnp.concatenate([b_proj, b_fc2, qv_bias]).astype(F32).reshape(4, wp)
-    (w, act, units, att, h1, mixed, proj, g1, g2, gb1, dh2, mod, cond, vec, ids) = forward(
-        samples, labels, bands, band_counts, w_qkv.T, w_proj, bias, kept, latents, cotangent, class_table.T, time_table, w_ada.T,
-        b_ada.astype(F32)[None], w_fc1.T, b_fc1.astype(F32)[None], w_fc2
-    )
-    totals, block_out, latents_grad, dmod_z, dcond_z, cvec_z, sum_z, ids_z = backward(
-        samples, planes, band_counts, w, act, units, att, h1, mixed, proj, g1, g2, gb1, dh2, mod, cond, vec, ids, kept, latents,
-        cotangent, w_ada.T, w_fc2
+    totals, block_out, latents_grad, unused_weights, dmod_z, dcond_z, cvec_z, sum_z, ids_z = run_block(
+        samples, planes, labels, bands, band_counts, w_qkv.T, w_proj, w_fc1.T, w_fc2, w_ada.T, latents, cotangent, bias, kept,
+        class_table.T, time_table, b_ada.astype(F32)[None], b_fc1.astype(F32)[None]
     )
     totals = totals.reshape(-1, width)
     at = 0
     pieces = []
-    for size in (hidden, hidden, wp, wq):
+    for size in (hidden, hidden, wq, wp):
         pieces.append(totals[at : at + size].astype(F32))
         at += size
     cvec_z = cvec_z.transpose(0, 2, 1, 3).reshape(planes * per, width)
@@ -1244,9 +1281,9 @@
         jnp.einsum("se,sc->ec", dcond, hot_class, precision=HIGH).T,
         ada_grad,
         ada_bias_grad,
-        pieces[3].T,
+        pieces[2].T,
         qv_grad,
-        pieces[2],
+        pieces[3],
         part(sums[0], b_proj.shape[0]),
         pieces[0].T,
         sums[2, :hidden],

time: 315 us -> 260 us (0.83)
  Pallas kernels: 289 us -> 230 us
    pallas_call x2 -> x1, Pallas kernels: 289 us -> 230 us  [run_block(): pl.pallas_call(functools.partial(block_kernel, samples, planes), out_shap...]
where the time goes in v2:
time: 260 us; the launch traced here: 259 us
  Pallas kernels  230 us (88%)
  local copies, waits for them, and re-layouts  11.9 us (5%)
  other arithmetic  10.2 us (4%)
  matrix products  5.57 us (2%)
    pallas_call x1, Pallas kernels, run_block(): pl.pallas_call(functools.partial(block_kernel, samples, planes), out_shap...  230 us

profile of v2, /device:TPU:0, one launch (start us, length us, event | category | flops | bytes accessed | tf_op | source)
XLA Modules:
  0.0 259.2 jit_solution(9952611312935014978)
XLA Ops:
  1.3 1.3 reshape.68.b1_ref
  2.6 1.3 reshape.67.bada_ref
  3.8 0.8 maximum_convert_fusion
  4.6 0.7 reshape.66.bias_ref
  5.3 230.1 %shard_map.281 = (bf16[12,144,1152]{2,1,0:T(8,128)(2,1)}, bf16[2,256,1152]{2,1,0:T(8,128)(2,1)}, bf16[2,256,1152]{2,1,0:T(8,128)(2,1)}, bf16[8,432,1152]{2,1,0:T...) custom-call(s32[2]{0:T(128)} %labels_ref.1, ...), custom_call_target="tpu_custom_call" | custom-call | tf_op jit(solution)/shard_map/pallas_call | solution.py:1180
  235.4 0.0 copy-start.3
  235.4 0.0 copy-start.2
  235.4 0.9 fusion.7
  236.3 0.1 copy.38
  236.4 0.1 copy.37
  236.5 1.6 fusion.2
  238.1 1.0 reduce_sum.19
  239.1 0.6 slice_reduce_fusion
  239.7 0.1 reshape.65
  239.8 0.6 constant_dynamic-slice_fusion
  240.4 0.7 fusion.4
  241.1 1.6 convert_reduce_fusion
  242.7 0.0 copy-done.3
  242.7 0.1 copy.36
  242.7 0.3 reshape.64
  243.0 0.0 copy-done.2
  243.0 1.3 fusion
  244.3 1.9 bitcast_convert_fusion.1
  246.2 1.3 slice.42
  247.4 1.9 fusion.5
  249.4 1.5 convert_bitcast_fusion.1
  250.9 2.9 %convert_bitcast_fusion = (f32[1152,576]{0,1:T(8,128)}, f32[576,1152]{1,0:T(8,128)}) fusion(bf16[4,144,1152]{2,1,0:T(8,128)(2,1)S(1)} %get-tuple-element.33, bf16[4,144,1152]{2,1,0:T(8,128)(2,1)S(1)} %get-tuple-element.32), kind=kLoop, calls=%fused_computation | loop fusion | flops 1327104 | bytes 7962624 | tf_op jit(solution)/shard_map/transpose | solution.py:1288
  253.8 2.7 %fusion.9 = f32[1152,864]{0,1:T(8,128)} fusion(bf16[64,1152]{1,0:T(8,128)(2,1)S(1)} %reshape.64, bf16[64,864]{1,0:T(8,128)(2,1)S(1)} %bitcast.37), kind=kOutput, calls=%fused_computation.22 | convolution fusion | flops 127401984 | bytes 4239360 | tf_op jit(solution)/shard_map/se,sd->ed/dot_general | solution.py:1267
  256.5 0.0 copy-done.1
  256.5 1.0 copy.42
  257.5 0.7 copy-done
  258.2 1.0 copy.43
  (5 shorter events, 0.0 us)
Async XLA Ops:
  235.4 7.2 %copy-start.3 = (bf16[4,8,16,144]{3,2,1,0:T(8,128)(2,1)S(1)}, bf16[4,8,16,144]{3,2,1,0:T(8,128)(2,1)}, u32[]{:S(2)}) copy-start(bf16[4,8,16,144]{3,2,1,0:T(8,128)(2,1)} %get-tuple-element.26) | copy-start | bytes 442372
  235.4 7.6 %copy-start.2 = (f32[4,16,144]{2,1,0:T(8,128)S(1)}, f32[4,16,144]{2,1,0:T(8,128)}, u32[]{:S(2)}) copy-start(f32[4,16,144]{2,1,0:T(8,128)} %get-tuple-element.25) | copy-start | bytes 110596
  253.8 2.7 %copy-start.1 = (bf16[2,256,1152]{2,1,0:T(8,128)(2,1)S(1)}, bf16[2,256,1152]{2,1,0:T(8,128)(2,1)}, u32[]{:S(2)}) copy-start(bf16[2,256,1152]{2,1,0:T(8,128)(2,1)} %get-tuple-element.58) | copy-start | bytes 3538948
  256.5 1.7 copy-start

commit v3 on v2

--- a/solution.py
+++ b/solution.py
@@ -286,19 +286,20 @@
 
 class Wire:
     def __init__(self, send, recv):
-        self.send, self.recv, self.used = send, recv, 0
-
-    def take(self, count):
-        first = self.used
-        self.used += count
+        self.send, self.recv, self.sends, self.recvs = send, recv, 0, 0
+
+    def take(self, recvs, sends=1):
+        first = (self.sends, self.recvs)
+        self.sends += sends
+        self.recvs += recvs
         return first
 
-    def copy(self, number, src, dst, device):
+    def copy(self, send, recv, src, dst, device):
         return pltpu.make_async_remote_copy(
             src_ref=src,
             dst_ref=dst,
-            send_sem=self.send.at[number],
-            recv_sem=self.recv.at[number],
+            send_sem=self.send.at[send],
+            recv_sem=self.recv.at[recv],
             device_id=device,
             device_id_type=MESH,
         )
@@ -326,12 +327,12 @@
         rows = rows or buf.shape[1]
         lo, hi = halves(rows)
         parts = (pl.ds(start, rows), pl.ds(start, lo.size), pl.ds(start + lo.size, hi.size))
-        first = wire.take(8)
+        send, recv = wire.take(8)
 
         def make(number, block, device, part=0):
             ref = buf.at[block, parts[part]]
             src = origin if number < 3 and origin is not None else ref
-            return wire.copy(first + number, src, ref, device)
+            return wire.copy(send, recv + number, src, ref, device)
 
         own, xb, yb, db = p.g, p.block(0, 1, 0), p.block(0, 0, 1), p.block(0, 1, 1)
         xd, yd, sd = p.device(0, 1, 0), p.device(0, 0, 1), p.device(1, 0, 0)
@@ -345,6 +346,8 @@
             make(6, yb, sd),
             make(7, db, sd),
         ]
+        seven = buf.at[pl.ds(0, 7), parts[0]]
+        self.sent = wire.copy(send, recv, seven, seven, sd)
 
     def start(self):
         for number in (0, 1, 2):
@@ -380,35 +383,61 @@
         self.c[7].wait_recv()
 
     def finish(self):
-        for copy in self.c:
-            copy.wait_send()
+        self.sent.wait_send()
+
+
+class OverZ:
+    def __init__(self, place, wire, buf, hbm, there, ahead, behind, rows):
+        p = place
+        near = [p.block(0, 1, 0), p.block(0, 0, 1), p.block(0, 1, 1)]
+        sd = p.device(1, 0, 0)
+        sem, recv = wire.take(7)
+        send, take = pl.ds(ahead, rows), pl.ds(behind, rows)
+        self.out = [wire.copy(sem, recv + i, buf.at[b, send], buf.at[b, send], there) for i, b in enumerate(near)]
+        self.on = [wire.copy(sem, recv + 3 + i, buf.at[b, take], buf.at[b, take], sd) for i, b in enumerate(near)]
+        self.own = wire.copy(sem, recv + 6, hbm.at[take], buf.at[p.g, take], sd)
+        seven = buf.at[pl.ds(0, 7), send]
+        self.sent = wire.copy(sem, recv, seven, seven, sd)
+
+    def pass_on(self, *numbers):
+        for i in numbers:
+            self.out[i].wait_recv()
+            self.on[i].start()
+
+    def arrived(self, *numbers):
+        for i in numbers:
+            self.on[i].wait_recv()
+
+    def finish(self):
+        self.sent.wait_send()
 
 
 class Scatter:
     def __init__(self, place, wire, buf, r1, r2, r3, rows=None):
         self.p, self.w, self.buf = place, wire, buf
         self.r1, self.r2, self.r3 = r1, r2, r3
-        self.rows = rows or buf.shape[1]
-        self.parts = halves(self.rows)
-        self.first = wire.take(10)
-        p = place
+        self.rows = rows = rows or buf.shape[1]
+        p, w = place, wire
         self.sib = [p.block(1, q & 1, q >> 1) for q in range(4)]
         self.mine = [p.block(0, q & 1, q >> 1) for q in range(4)]
         xd, yd, sd = p.device(0, 1, 0), p.device(0, 0, 1), p.device(1, 0, 0)
-        f, w = self.first, wire
-        lo, hi = self.parts
-        whole = pl.ds(0, self.rows)
-        self.s1 = [w.copy(f + q, buf.at[self.sib[q], whole], r1.at[q, whole], sd) for q in range(4)]
-        self.s2 = [
-            w.copy(f + 4, buf.at[self.mine[3], lo], r2.at[0, pl.ds(0, lo.size)], xd),
-            w.copy(f + 5, buf.at[self.mine[3], hi], r2.at[1, pl.ds(0, hi.size)], yd),
-        ]
-        self.s3 = [
-            w.copy(f + 6, buf.at[self.mine[1], lo], r3.at[0, lo], xd),
-            w.copy(f + 7, buf.at[self.mine[1], hi], r3.at[0, hi], xd),
-            w.copy(f + 8, buf.at[self.mine[2], lo], r3.at[1, lo], yd),
-            w.copy(f + 9, buf.at[self.mine[2], hi], r3.at[1, hi], yd),
-        ]
+        sem, recv = wire.take(14)
+        whole = pl.ds(0, rows)
+        lo, hi = halves(rows)
+        self.parts = [[pl.ds(half.start + cut.start, cut.size) for cut in halves(half.size)] for half in (lo, hi)]
+        self.s1 = [w.copy(sem, recv + q, buf.at[self.sib[q], whole], r1.at[q, whole], sd) for q in range(4)]
+        self.s2, self.s3 = [], []
+        for way, device in ((0, xd), (1, yd)):
+            for i, part in enumerate(self.parts[way]):
+                number = recv + 4 + 2 * way + i
+                self.s2.append(w.copy(sem, number, buf.at[self.mine[3], part], r2.at[way, pl.ds(part.start - self.parts[way][0].start, part.size)], device))
+        for way, device in ((0, xd), (1, yd)):
+            direct = (lo, hi)[way]
+            for i, part in enumerate([direct] + self.parts[1 - way]):
+                number = recv + 8 + 3 * way + i
+                self.s3.append(w.copy(sem, number, buf.at[self.mine[1 + way], part], r3.at[way, part], device))
+        seven = buf.at[pl.ds(0, 7), whole]
+        self.sent = wire.copy(sem, recv, seven, seven, sd)
 
     def send_sib(self, q):
         self.s1[q].start()
@@ -419,8 +448,8 @@
 
     def send_far(self):
         self.add_sib(3)
-        self.s2[0].start()
-        self.s2[1].start()
+        for number in (0, 2, 1, 3):
+            self.s2[number].start()
 
     def send_near(self):
         self.add_sib(1)
@@ -429,30 +458,28 @@
         self.s3[3].start()
 
     def relay(self):
-        lo, hi = self.parts
-        self.s2[1].wait_recv()
-        add_into(self.buf.at[self.mine[1], hi], self.r2.at[1, pl.ds(0, hi.size)])
-        self.s3[1].start()
-        self.s2[0].wait_recv()
-        add_into(self.buf.at[self.mine[2], lo], self.r2.at[0, pl.ds(0, lo.size)])
-        self.s3[2].start()
+        for i in range(2):
+            for way in range(2):
+                self.s2[2 * way + i].wait_recv()
+                part = self.parts[way][i]
+                came = self.r2.at[way, pl.ds(part.start - self.parts[way][0].start, part.size)]
+                add_into(self.buf.at[self.mine[2 - way], part], came)
+                self.s3[3 * (1 - way) + 1 + i].start()
         self.add_sib(0)
 
     def result(self, out):
         for copy in self.s3:
             copy.wait_recv()
-        rows = self.rows
         step = 16
 
-        @pl.loop(0, rows // step)
+        @pl.loop(0, self.rows // step)
         def _(i):
             at = pl.ds(pl.multiple_of(i * step, step), step)
             total = self.buf[self.mine[0], at].astype(F32) + self.r3[0, at].astype(F32) + self.r3[1, at].astype(F32)
             out[at] = total.astype(out.dtype)
 
     def finish(self):
-        for copy in self.s1 + self.s2 + self.s3:
-            copy.wait_send()
+        self.sent.wait_send()
 
 
 def add_into(ref, other):
@@ -472,24 +499,27 @@
     ]
 
 
-def to_all(place, wire, make):
-    first = wire.take(7)
-    copies = []
-    for number, rel in enumerate(RELATIVE[1:]):
-        src, dst = make(rel)
-        copies.append(wire.copy(first + number, src, dst, place.device(*rel)))
-        copies[-1].start()
-    return copies
+class Together:
+    def __init__(self, wire, buf, pairs, device):
+        send, recv = wire.take(1)
+        count = len(pairs)
+        for src, dst, target in pairs:
+            wire.copy(send, recv, src, dst, target).start()
+        all_blocks = buf.at[pl.ds(0, count)]
+        self.all = wire.copy(send, recv, all_blocks, all_blocks, device)
+
+
+def to_all(place, wire, buf, make):
+    pairs = [(make(rel), buf.at[place.g], place.device(*rel)) for rel in RELATIVE[1:]]
+    return Together(wire, buf, pairs, place.device(1, 0, 0))
 
 
 def wait_recv(copies):
-    for copy in copies:
-        copy.wait_recv()
+    copies.all.wait_recv()
 
 
 def wait_send(copies):
-    for copy in copies:
-        copy.wait_send()
+    copies.all.wait_send()
 
 
 def params(collective_id):
@@ -545,34 +575,32 @@
     return exps / jnp.sum(exps, -1, keepdims=True)
 
 
-def arrival(p, t):
-    dc = jnp.where((t == 1) | (t == 4) | (t == 5) | (t == 7), 1, 0)
+def arrival(p, t, last=7):
+    dc = jnp.where((t == 1) | (t == 4) | (t == 5) | (t == last), 1, 0)
     dx = jnp.where((t == 2) | (t == 4) | (t >= 6), 1, 0)
     dy = jnp.where((t == 3) | (t >= 5), 1, 0)
     c, x, y = lax.rem(p.c + dc, 2), lax.rem(p.x + dx, 2), lax.rem(p.y + dy, 2)
     return y * 4 + x * 2 + c
 
 
-MSG_PROJ, MSG_FC2, MSG_QV, MSG_ROWS = 0, 8, 16, 32
-
-
 def sample_weight(place, counts_ref, samples, s):
     count = jnp.full((1, 128), counts_ref[0], jnp.int32)
     used = count > place.z * samples + s
     return (jnp.where(used, 1.0, 0.0) / count.astype(F32))[:, 0:1]
 
 
-ANY = pl.BlockSpec(memory_space=pl.ANY)
+ANY = pl.BlockSpec(memory_space=pltpu.HBM)
 SMEM = pl.BlockSpec(memory_space=pltpu.SMEM)
-CHUNK = 144
+PIECE = 48
 
 
 def block_kernel(samples, planes, labels_ref, bands_ref, counts_ref, wq_hbm, wp_hbm, w1_hbm, w2_hbm, ada_hbm, lat_hbm, cot_hbm,
-                 bias_ref, kept_ref, class_ref, time_ref, bada_ref, b1_ref,
-                 out_hbm, block_hbm, latg_hbm, wq_keep, dmod_z, dcond_z, cvec_z, sum_z, ids_z,
+                 bp_ref, b2_ref, qv_ref, bada_ref, b1_ref, kept_ref, class_ref, time_ref,
+                 out_hbm, y_hbm, dx_hbm, wq_keep, dmod_hbm, dcond_hbm, cvec_hbm, sum_hbm, ids_hbm,
+                 dmod_z, dcond_z, cvec_z, sum_z, ids_z,
                  wq, wp, w1, w2, h1_all, h2_all, dm_all, act, dpre, p1, p2, p3, units, att, mixed, proj, grad, dx2, tmp, rest,
-                 dproj, dq, dq_all, from_end, out, g1, g2, gq, gp, gb1, ids_all, msg_all, cond_all, mod_in, mod_send, mod, vec,
-                 dc_send, dc_in, bundle, bundles, send, recv, credits, sems, out_sems):
+                 dproj, dq, dq_all, from_end, out, grads, gb1, ids_all, msg_all, cond_all, mod_in, mod_send, mod, vec,
+                 dc_send, dc_in, bundle, share_send, share_in, send, recv, credits, sems):
     p = Place()
     wire = Wire(send, recv)
     g, z = p.g, p.z
@@ -600,65 +628,70 @@
         ("ada1b", ada_hbm.at[pl.ds(0, hidden_units)], w1),
         ("ada2b", ada_hbm.at[pl.ds(hidden_units, ada_rest)], w2.at[pl.ds(0, ada_rest)]),
         ("latb", lat_hbm, wq.at[pl.ds(0, samples), pl.ds(0, length)]),
-        ("cotb", cot_hbm, wq.at[pl.ds(samples, samples), pl.ds(0, length)]),
-        ("block", wq.at[pl.ds(0, samples), pl.ds(0, length)], block_hbm),
-        ("latg", wq.at[pl.ds(samples, samples), pl.ds(0, length)], latg_hbm),
+        ("dx", dproj, dx_hbm),
+        ("y", dproj, y_hbm),
+        ("dmod", dmod_z, dmod_hbm),
+        ("dcond", dcond_z, dcond_hbm),
+        ("cvec", cvec_z, cvec_hbm),
+        ("sum", sum_z, sum_hbm),
+        ("ids", ids_z, ids_hbm),
     )):
         loads[name] = local(src, dst, sems.at[number])
     odd = z % 2
     there = (g, z + 1 - 2 * odd)
-    ahead, behind = 2 * pair * odd, 2 * pair * (1 - odd)
-    gather_a = Gather(p, wire, wq, ahead, pair, wq_hbm.at[pl.ds(ahead, pair)])
+    gather_a = Gather(p, wire, wq, 2 * pair * odd, pair, wq_hbm.at[pl.ds(2 * pair * odd, pair)])
     gather_m = Gather(p, wire, wq, pair, pair, wq_hbm.at[pl.ds(pair, pair)])
-    first = wire.take(7)
-    near = [p.block(0, 1, 0), p.block(0, 0, 1), p.block(0, 1, 1)]
-    sd = p.device(1, 0, 0)
-    across_z = [wire.copy(first + i, wq.at[b, pl.ds(ahead, pair)], wq.at[b, pl.ds(ahead, pair)], there) for i, b in enumerate(near)]
-    own_sib = wire.copy(first + 3, wq_hbm.at[pl.ds(behind, pair)], wq.at[g, pl.ds(behind, pair)], sd)
-    from_z = [wire.copy(first + 4 + i, wq.at[b, pl.ds(behind, pair)], wq.at[b, pl.ds(behind, pair)], sd) for i, b in enumerate(near)]
-    outward = Gather(p, wire, wp, origin=wp_hbm)
+    qkv_z = OverZ(p, wire, wq, wq_hbm, there, 2 * pair * odd, 2 * pair * (1 - odd), pair)
+    inside = pair // 32 * 16 + 16
+    beyond = pair - inside
+    outward = Gather(p, wire, wp, beyond * odd, inside, wp_hbm.at[pl.ds(beyond * odd, inside)])
+    proj_z = OverZ(p, wire, wp, wp_hbm, there, inside * odd, inside * (1 - odd), beyond)
     main = Gather(p, wire, h2_all)
     back = Gather(p, wire, dm_all)
     tokens = Gather(p, wire, h1_all)
     sums = Scatter(p, wire, wq, p1, p2, p3, rows)
     outs = Scatter(p, wire, h2_all, dm_all.at[pl.ds(0, 4)], dm_all.at[pl.ds(4, 2)], dm_all.at[pl.ds(6, 2)])
     projs = Scatter(p, wire, wp, p1, p2, p3)
-    sources = [ref.at[pl.ds(start, CHUNK)] for ref in (g1, g2, gq, gp) for start in range(0, ref.shape[0], CHUNK)]
-    count = len(sources)
-    up, across, down = wire.take(count), wire.take(count), wire.take(count)
+    part_of = lambda start, size: grads.at[pl.ds(start, size)]
+    g1, g2 = part_of(0, hidden_units), part_of(hidden_units, hidden_units)
+    gq, gp = part_of(2 * hidden_units, 3 * pair), part_of(2 * hidden_units + 3 * pair, pair)
+    count = grads.shape[0] // PIECE
+    (up, up_r), (across, across_r), (down, down_r) = [wire.take(count) for way in range(3)]
     inner, outer, partner = 1 + z // 3, (z - 1) * 3, 3 - z
     at_end = (z == 0) | (z == planes - 1)
-    ups = [wire.copy(up + k, sources[k], from_end.at[k], (g, inner)) for k in range(count)]
-    acrosses = [wire.copy(across + k, from_end.at[k], out.at[k], (g, partner)) for k in range(count)]
-    downs = [wire.copy(down + k, out.at[k], out.at[k], (g, outer)) for k in range(count)]
-    results = [local(out.at[k], out_hbm.at[k], out_sems.at[k]) for k in range(count)]
-
-    def chain_send(*numbers):
+    rows_of = lambda ref, k: ref.at[pl.ds(pl.multiple_of(k * PIECE, 16), PIECE)]
+    go_up = lambda k: wire.copy(up, up_r + k, rows_of(grads, k), rows_of(from_end, k), (g, inner))
+    go_across = lambda k: wire.copy(across, across_r + k, rows_of(from_end, k), rows_of(out, k), (g, partner))
+    go_down = lambda k: wire.copy(down, down_r + k, rows_of(out, k), rows_of(out, k), (g, outer))
+    to_hbm = lambda k: local(rows_of(out, k), rows_of(out_hbm, k), sems.at[20])
+
+    def chain_send(first, last):
         @pl.when(at_end)
         def _():
-            for k in numbers:
-                ups[k].start()
-
-    def chain(*numbers):
+            for k in range(first, last):
+                go_up(k).start()
+
+    def chain_up(k):
         @pl.when(jnp.logical_not(at_end))
         def _():
-            for k in numbers:
-                if k < count:
-                    ups[k].wait_recv()
-                    add_into(from_end.at[k], sources[k])
-                    acrosses[k].start()
-                if k > 0:
-                    acrosses[k - 1].wait_recv()
-                    add_into(out.at[k - 1], from_end.at[k - 1])
-                    downs[k - 1].start()
-                    results[k - 1].start()
+            go_up(k).wait_recv()
+            add_into(rows_of(from_end, k), rows_of(grads, k))
+            go_across(k).start()
+
+    def chain_down(k):
+        @pl.when(jnp.logical_not(at_end))
+        def _():
+            go_across(k).wait_recv()
+            add_into(rows_of(out, k), rows_of(from_end, k))
+            go_down(k).start()
+            to_hbm(k).start()
+
+    def chain(k, lag=3):
+        chain_up(k)
+        chain_down(k - lag)
 
     def to_planes(ref):
-        first = wire.take(planes - 1)
-        copies = [wire.copy(first + k, ref.at[z], ref.at[z], device) for k, device in enumerate(others)]
-        for copy in copies:
-            copy.start()
-        return copies
+        return Together(wire, ref, [(ref.at[z], ref.at[z], device) for device in others], others[0])
 
     neighbours = [p.device(1, 0, 0), p.device(0, 1, 0), p.device(0, 0, 1)]
 
@@ -671,18 +704,18 @@
             pl.semaphore_wait(credits.at[number, i], 1)
 
     lanes = lax.broadcasted_iota(jnp.int32, (1, 128), 1)
-    ids_all[g] = jnp.zeros((8, 128), F32)
     for s in range(samples):
         line = jnp.where(lanes == 0, labels_ref[s], 0) + jnp.where(lanes == 1, bands_ref[s], 0)
         ids_all[g, s : s + 1, :] = line.astype(F32)
-    idc = to_all(p, wire, lambda rel: (ids_all.at[g], ids_all.at[g]))
+    line_of = lambda ref: ref[...].astype(F32).reshape(1, ref.shape[0])
+    b_ada, b1, qv = line_of(bada_ref), line_of(b1_ref), line_of(qv_ref)
+    for row, line in enumerate((line_of(bp_ref), line_of(b2_ref), qv[:, :pair], qv[:, pair:])):
+        msg_all[g, row : row + 1, :] = line
+    idc = to_all(p, wire, ids_all, lambda rel: ids_all.at[g])
     gather_a.start()
+    msgs = to_all(p, wire, msg_all, lambda rel: msg_all.at[g])
     for name in ("lat", "cot", "ada1", "ada2", "wq", "wp"):
         loads[name].start()
-    msg_all[g] = jnp.zeros(msg_all.shape[1:], F32)
-    for row in range(4):
-        at = MSG_PROJ + 8 * row
-        msg_all[g, at : at + 1, :] = bias_ref[row : row + 1, :]
 
     wait_recv(idc)
     labels = jnp.concatenate([ids_all[j, 0:samples, 0:1] for j in range(8)], 0)
@@ -694,12 +727,11 @@
 
     of_band = dot(one_hot(bands, time_ref.shape[0]), time_ref[...], (1, 0))
     cond_all[g] = of_band + dot(one_hot(labels, class_ref.shape[1]), class_ref[...], (1, 1))
-    conds = to_all(p, wire, lambda rel: (cond_all.at[g], cond_all.at[g]))
+    conds = to_all(p, wire, cond_all, lambda rel: cond_all.at[g])
     ids_z[z] = jnp.zeros(ids_z.shape[1:], F32)
     ids_z[z, :, 0:1] = labels
     ids_z[z, :, 1:2] = bands
-    gather_m.start()
-    own_sib.start()
+
 
     loads["lat"].wait()
     loads["cot"].wait()
@@ -709,29 +741,27 @@
         mixed[at] = dot(hot, h2_all[s], (0, 0))
         grad[at] = dot(hot, h2_all[samples + s], (0, 0)) * sample_weight(p, counts_ref, samples, s)
 
-    gather_a.arrived()
-    across_z[0].start()
-    across_z[1].start()
-    zs = [to_planes(ids_z)]
+    gather_a.neighbours()
+    qkv_z.out[0].start()
+    qkv_z.out[1].start()
     wait_recv(conds)
-    value = cond_all[...]
-    value = value * jax.nn.sigmoid(value)
-    cvec_z[z] = value.astype(BF16)
-    zs.append(to_planes(cvec_z))
-    value = jnp.concatenate([value[j] for j in range(8)], 1).astype(BF16)
+    value = jnp.concatenate([cond_all[j] for j in range(8)], 1)
+    value = (value * jax.nn.sigmoid(value)).astype(BF16)
+    cvec_z[z] = value
     loads["ada1"].wait()
     loads["ada2"].wait()
     mods = [dot(value, w1[...], (1, 1)), dot(value, w2[0:ada_rest], (1, 1))]
-    mods = jnp.concatenate(mods, 1) + bada_ref[...]
-    mod_send[...] = jnp.zeros_like(mod_send)
+    mods = jnp.concatenate(mods, 1) + b_ada
     for j in range(8):
-        mod_send[j, 0:samples, :] = mods[samples * j : samples * (j + 1), :]
+        mod_send[j] = mods[samples * j : samples * (j + 1), :]
     mod_in[g] = mod_send[g]
-    modc = to_all(p, wire, lambda rel: (mod_send.at[p.block(*rel)], mod_in.at[g]))
-    msgs = to_all(p, wire, lambda rel: (msg_all.at[g], msg_all.at[g]))
-    gather_a.forward()
+    modc = to_all(p, wire, mod_in, lambda rel: mod_send.at[p.block(*rel)])
+    gather_m.start()
+    qkv_z.own.start()
     loads["w1"].start()
     loads["w2"].start()
+    gather_a.far()
+    qkv_z.out[2].start()
     wait_recv(modc)
     mod[...] = jnp.zeros_like(mod)
     for s in range(samples):
@@ -744,13 +774,11 @@
         h1_all[g, at] = (hat * (1.0 + mod[s, 1:2, :]) + mod[s, 0:1, :]).astype(BF16)
         dm_all[g, at] = (mod[s, 5:6, :] * grad[at]).astype(BF16)
 
-    gather_m.neighbours()
-    outward.start()
     by_rows(samples, keep, first_norm)
     wait_recv(msgs)
     vec[...] = jnp.zeros_like(vec)
-    for row, at in ((0, MSG_PROJ), (1, MSG_FC2)):
-        vec[row : row + 1, :] = jnp.concatenate([msg_all[j, at : at + 1, :] for j in range(8)], 1)
+    for row in range(2):
+        vec[row : row + 1, :] = jnp.concatenate([msg_all[j, row : row + 1, :] for j in range(8)], 1)
 
     ones = jnp.ones((8, rows), BF16)
     loads["wq"].wait()
@@ -767,41 +795,48 @@
             def _(gather=gather):
                 gather.wait_sib_neighbours()
 
-            @pl.when(n == base + 6)
-            def _(gather=gather, base=base):
-                gather.far()
-                if base == 0:
-                    across_z[2].start()
+            if base:
+
+                @pl.when(n == base + 6)
+                def _(gather=gather):
+                    gather.far()
 
             @pl.when(n == base + 7)
             def _(gather=gather):
                 gather.wait_sib_far()
 
-        @pl.when(n == 17)
-        def _():
-            own_sib.wait_recv()
-
-        @pl.when(n == 18)
-        def _():
-            for i in range(2):
-                across_z[i].wait_recv()
-                from_z[i].start()
-
-        @pl.when(n == 20)
-        def _():
-            for i in range(2):
-                from_z[i].wait_recv()
+        @pl.when(n == 6)
+        def _():
+            gather_m.neighbours()
+            outward.start()
+            proj_z.own.start()
+
+        @pl.when(n == 16)
+        def _():
             outward.neighbours()
             back.start()
+            proj_z.out[0].start()
+            proj_z.out[1].start()
+
+        @pl.when(n == 17)
+        def _():
+            qkv_z.own.wait_recv()
+
+        @pl.when(n == 18)
+        def _():
+            qkv_z.pass_on(0, 1)
+
+        @pl.when(n == 20)
+        def _():
+            qkv_z.arrived(0, 1)
 
         @pl.when(n == 22)
         def _():
-            across_z[2].wait_recv()
-            from_z[2].start()
+            qkv_z.pass_on(2)
 
         @pl.when(n == 23)
         def _():
-            from_z[2].wait_recv()
+            qkv_z.arrived(2)
 
         phase = lax.div(n, 8)
         block = arrival(p, lax.rem(n, 8))
@@ -809,20 +844,22 @@
         chunk = block * 3 + third
         bias_at = jnp.where(chunk >= 16, chunk - 8, chunk)
         keys = (chunk >= 8) & (chunk < 16)
-        line = msg_all[lax.div(bias_at, 2), pl.ds(pl.multiple_of(MSG_QV + 8 * lax.rem(bias_at, 2), 8), 8), :]
-        line = line * jnp.where(keys, 0.0, 1.0)
+        line = msg_all[lax.div(bias_at, 2), pl.ds(2 + lax.rem(bias_at, 2), 1), :] * jnp.where(keys, 0.0, 1.0)
+        line = jnp.concatenate([line, jnp.zeros((7, pair), F32)], 0)
         value = dot(wq[block, pl.ds(pl.multiple_of(third * pair, 16), pair), :], h1_all[g], (1, 1))
         value = value + dot(line.astype(BF16), ones, (0, 0))
         units[2 * chunk] = value[:HEAD_DIM].astype(BF16)
         units[2 * chunk + 1] = value[HEAD_DIM:].astype(BF16)
 
     loads["keep"].start()
+    zs = [to_planes(ids_z), to_planes(cvec_z)]
 
     @pl.loop(0, 8)
     def _(u):
-        @pl.when(u == 1)
+        @pl.when(u == 3)
         def _():
             outward.far()
+            proj_z.out[2].start()
 
         for s in range(samples):
             lanes = pl.ds(s * keep, keep)
@@ -832,10 +869,14 @@
                 pieces.append(dot(units[32 + 2 * u + e, :, lanes], probs.astype(BF16), (1, 1)))
             att[u, :, lanes] = jnp.concatenate(pieces, 0).astype(BF16)
 
+    back.neighbours()
     loads["wp"].wait()
     outward.wait_sib()
     outward.wait_sib_neighbours()
     outward.wait_sib_far()
+    proj_z.own.wait_recv()
+    proj_z.pass_on(0, 1, 2)
+    proj_z.arrived(0, 1, 2)
     proj[...] = jnp.zeros_like(proj)
 
     @pl.loop(0, 8)
@@ -848,20 +889,18 @@
         hat, inv = normed(mixed[at])
         h2_all[g, at] = (hat * (1.0 + mod[s, 4:5, :]) + mod[s, 3:4, :]).astype(BF16)
 
-    back.neighbours()
     by_rows(samples, keep, second_norm)
     main.start()
     back.far()
     gb1[...] = jnp.zeros_like(gb1)
-    for piece in (gather_a, gather_m):
+    for piece in (gather_a, gather_m, qkv_z):
         piece.finish()
-    wait_send(across_z + from_z + [own_sib])
     loads["w1"].wait()
     loads["w2"].wait()
     loads["keep"].wait()
 
     def hidden(block):
-        pre = dot(h2_all[block], w1[...], (1, 1)) + b1_ref[...]
+        pre = dot(h2_all[block], w1[...], (1, 1)) + b1
         value, slope = gelu_parts(pre)
         act[block] = value.astype(BF16)
         low = (dot(dm_all[block], w2[...], (1, 1)) * slope).astype(BF16)
@@ -888,15 +927,12 @@
 
         @pl.when(t == 6)
         def _():
+            main.far()
             sums.send_near()
-            main.far()
-
-        @pl.when(t == 7)
-        def _():
             main.wait_sib_far()
 
-        hidden(arrival(p, t))
-        for at, q in ((1, 0), (4, 1), (5, 2), (7, 3)):
+        hidden(arrival(p, t, 6))
+        for at, q in ((1, 0), (4, 1), (5, 2), (6, 3)):
 
             @pl.when(t == at)
             def _(q=q):
@@ -904,36 +940,33 @@
 
     sums.send_far()
 
-    def weight_grad(left, right, target):
-        pieces = [(dx2, 0, 256), (tmp, 256, 256), (rest, 512, hidden_units - 512)]
-        for ref, start, size in pieces:
+    def weight_grad(left, right, base, between):
+        for ref, start, size in ((dx2, 0, 256), (tmp, 256, 256), (rest, 512, hidden_units - 512)):
             ref[0:size] = jnp.zeros((size, width), F32)
 
-        @pl.loop(0, 4)
-        def _(i):
-            two = pl.ds(2 * i, 2)
-            values = right[two].reshape(2 * rows, width)
-            for ref, start, size in pieces:
+            @pl.loop(0, 4)
+            def _(i):
+                two = pl.ds(2 * i, 2)
                 part = left[two, :, pl.ds(start, size)].reshape(2 * rows, size)
-                ref[0:size] += dot(part, values, (0, 0))
-
-        for ref, start, size in pieces:
-            target[pl.ds(start, size)] = ref[0:size].astype(BF16)
-
-    weight_grad(dpre, h2_all, g1)
-    chain_send(0, 1, 2, 3)
+                ref[0:size] += dot(part, right[two].reshape(2 * rows, width), (0, 0))
+
+            grads[base + start : base + start + size] = ref[0:size].astype(BF16)
+            chain_send(-(-(base + start) // PIECE) if start == 0 else (base + start) // PIECE, (base + start + size) // PIECE)
+            between(start)
+
+    weight_grad(dpre, h2_all, 0, lambda start: None)
     sums.relay()
     main.finish()
     tokens.start()
-    weight_grad(act, dm_all, g2)
-    chain_send(4, 5, 6, 7)
+    chain_up(0)
+    weight_grad(act, dm_all, hidden_units, lambda start: chain_up(1 + start // 256))
+    chain_down(0)
     back.finish()
     grant(0)
     sums.result(tmp)
     sums.finish()
     grant(1)
     loads["again"].start()
-    chain(0)
 
     bundle[...] = jnp.zeros_like(bundle)
 
@@ -955,8 +988,13 @@
         add_row(SUM_PROJ, low.astype(F32))
         add_row(SUM_FC2, (mod[s, 5:6, :] * grad[at]).astype(BF16).astype(F32))
 
+    chain_up(4)
     by_rows(samples, keep, second_back)
+    chain_down(1)
+    chain_up(5)
+    chain_down(2)
     outward.finish()
+    proj_z.finish()
 
     @pl.loop(0, 8)
     def _(u):
@@ -984,22 +1022,18 @@
             for s in range(samples):
                 dq[lax.div(chunk, 3), at, pl.ds(s * keep, keep)] = lists[i][s]
 
-        @pl.when(u == 1)
-        def _():
-            chain(1)
-
         @pl.when(u == 4)
         def _():
             tokens.neighbours()
-            chain(2)
+
+        chain(6 + u)
 
     dq_all[g] = dq[g]
-    moves = to_all(p, wire, lambda rel: (dq.at[p.block(*rel)], dq_all.at[g]))
+    moves = to_all(p, wire, dq_all, lambda rel: dq.at[p.block(*rel)])
     granted(1)
     for q in (3, 1, 2, 0):
         projs.send_sib(q)
     tokens.far()
-    chain(3)
 
     loads["again"].wait()
     proj[...] = jnp.zeros_like(proj)
@@ -1007,10 +1041,13 @@
     @pl.loop(0, 8)
     def _(j):
         proj[...] += dot(dq[j], wq[j], (0, 0))
+        for at in range(2):
+
+            @pl.when(j == 4 * at + 3)
+            def _(at=at):
+                chain(14 + at)
 
     loads["latb"].start()
-    loads["cotb"].start()
-    chain(4)
 
     granted(0)
 
@@ -1018,6 +1055,13 @@
     def _(t):
         block = arrival(p, 7 - t)
         h2_all[block] = jnp.dot(act[block], w2[...], preferred_element_type=F32).astype(BF16)
+
+        for at in range(2):
+
+            @pl.when(t == 4 * at + 3)
+            def _(at=at):
+                chain(16 + at)
+
         for at, q in ((1, 0), (4, 1), (5, 2), (7, 3)):
 
             @pl.when(t == 7 - at)
@@ -1029,7 +1073,8 @@
     tokens.wait_sib()
     tokens.wait_sib_neighbours()
     tokens.wait_sib_far()
-    chain(5)
+    for k in range(18, 22):
+        chain(k)
 
     wait_recv(moves)
     projs.send_far()
@@ -1043,16 +1088,14 @@
             tmp[0:pair] += dot(dq_all[j, at, :], h1_all[j], (1, 0))
 
         gq[at] = tmp[0:pair].astype(BF16)
-        chain_send(8 + i)
-        if i == 1:
-            chain(6)
+        chain_send(24 + 3 * i, 27 + 3 * i)
+        chain(22 + i)
     projs.relay()
     outs.send_far()
     outs.send_near()
-    chain(7)
+    chain(25)
 
     loads["latb"].wait()
-    loads["cotb"].wait()
     for s in range(samples):
         hot = own_tokens(kept_ref, length, s)
         tmp[pl.ds(s * keep, keep)] = dot(hot, wq[s, pl.ds(0, length)], (0, 0))
@@ -1066,133 +1109,131 @@
         dproj[at] = dx.astype(BF16)
 
     by_rows(samples, keep, first_back)
+    chain(26)
     projs.result(gp)
-    chain_send(11)
-
-    def place_tokens(s):
-        hot = own_tokens(kept_ref, length, s)
-        is_kept = jnp.sum(hot.astype(F32), 1, keepdims=True) > 0.5
-        return is_kept, dot(hot, dproj[pl.ds(s * keep, keep)], (1, 0))
-
-    for s in range(samples):
-        is_kept, spread = place_tokens(s)
-        at = (samples + s, pl.ds(0, length))
-        weighted = wq[at].astype(F32) * sample_weight(p, counts_ref, samples, s)
-        wq[at] = jnp.where(is_kept, spread, weighted).astype(BF16)
-    loads["latg"].start()
-    chain(8)
+    chain_send(33, 36)
+    loads["dx"].start()
+    chain(27)
+    chain(28)
     outs.relay()
-    chain(9)
-    chain(10)
+    for k in range(29, 35):
+        chain(k)
     outs.result(tmp)
+    chain(35)
 
     def end(s, at):
         value = tmp[at] + vec[1:2, :]
         add_row(s * 6 + 5, grad[at] * value)
         dproj[at] = (mixed[at] + mod[s, 5:6, :] * value).astype(BF16)
 
+    loads["dx"].wait()
     by_rows(samples, keep, end)
+    loads["y"].start()
 
     cols = ada_hbm.shape[0]
     wait_send(modc)
-    mod_send[...] = jnp.zeros_like(mod_send)
     for s in range(samples):
         line = jnp.concatenate([bundle[s * 6 + v : s * 6 + v + 1, :] for v in range(6)], 1)
-        line = line.astype(BF16).astype(F32)
         for j in range(8):
-            mod_send[j, s : s + 1, :] = line[:, j * cols : (j + 1) * cols]
+            mod_send[j, s : s + 1, :] = line[:, j * cols : (j + 1) * cols].astype(BF16).astype(F32)
     mod_in[g] = mod_send[g]
-    dmods = to_all(p, wire, lambda rel: (mod_send.at[p.block(*rel)], mod_in.at[g]))
-    bundles[g, 0:8, :] = jnp.zeros((8, width), F32)
-    bundles[g, 0:2, :] = bundle[SUM_PROJ : SUM_PROJ + 2, :]
+    dmods = to_all(p, wire, mod_in, lambda rel: mod_send.at[p.block(*rel)])
+    lines = [dot(ones, dq[j], (1, 1))[0:1, :] for j in range(8)]
     for j in range(8):
-        line = dot(ones, dq[j], (1, 1))
-        bundles[g, 8 + j : 9 + j, 0 : 3 * pair] = line[0:1, :]
-    small = to_all(p, wire, lambda rel: (bundles.at[g], bundles.at[g]))
-
-    for s in range(samples):
-        is_kept, spread = place_tokens(s)
-        at = (s, pl.ds(0, length))
-        wq[at] = jnp.where(is_kept, spread, wq[at].astype(F32)).astype(BF16)
-    loads["block"].start()
+        for row, at in ((0, SUM_PROJ), (1, SUM_FC2)):
+            share_send[j, row : row + 1, :] = bundle[at : at + 1, j * pair : (j + 1) * pair]
+        for e in range(2):
+            u = 2 * j + e + (8 if j >= 4 else 0)
+            share_send[j, 2 + e : 3 + e, :] = lines[u // 3][:, u % 3 * pair : (u % 3 + 1) * pair]
+    share_in[g] = share_send[g]
+    small = to_all(p, wire, share_in, lambda rel: share_send.at[p.block(*rel)])
+    chain_down(33)
     loads["ada1b"].wait()
     loads["ada2b"].wait()
     wait_recv(dmods)
-    part = jnp.concatenate([mod_in[j, 0:samples, :] for j in range(8)], 0)
+    part = jnp.concatenate([mod_in[j] for j in range(8)], 0).astype(BF16)
     dmod_z[z] = part
     zs.append(to_planes(dmod_z))
-    part = part.astype(BF16)
     dcvec = dot(part[:, :hidden_units], w1[...], (1, 0)) + dot(part[:, hidden_units:], w2[0:ada_rest], (1, 0))
     depth = cond_all.shape[2]
     for j in range(8):
         dc_send[j] = dcvec[:, j * depth : (j + 1) * depth]
     dc_in[g] = dc_send[g]
-    dcs = to_all(p, wire, lambda rel: (dc_send.at[p.block(*rel)], dc_in.at[g]))
+    dcs = to_all(p, wire, dc_in, lambda rel: dc_send.at[p.block(*rel)])
+    chain_down(34)
     wait_recv(small)
-    sum_z[z] = sum(bundles[j] for j in range(8))
-    sum_z[z, 2:3, 0:hidden_units] = gb1[...]
+    sum_z[z, 0:4, :] = sum(share_in[j] for j in range(8))
+    for i in range(hidden_units // pair):
+        sum_z[z, 4 + i : 5 + i, :] = gb1[:, i * pair : (i + 1) * pair]
     zs.append(to_planes(sum_z))
-    chain(11)
+    chain_down(35)
     wait_recv(dcs)
     cond = cond_all[g]
     gate = jax.nn.sigmoid(cond)
     dcond_z[z] = sum(dc_in[j] for j in range(8)) * (gate * (1.0 + cond * (1.0 - gate)))
     zs.append(to_planes(dcond_z))
-    chain(12)
+
+    whole = lambda sem, ref: wire.copy(sem, up_r, ref, ref, (g, partner))
 
     @pl.when(jnp.logical_not(at_end))
     def _():
-        for k in range(count):
-            acrosses[k].wait_send()
-            downs[k].wait_send()
-            results[k].wait()
+        whole(across, out).wait_send()
+        whole(down, out).wait_send()
 
     @pl.when(at_end)
     def _():
-        for k in range(count):
-            downs[k].wait_recv()
-            results[k].start()
-        for k in range(count):
-            ups[k].wait_send()
-            results[k].wait()
-
+        @pl.loop(0, count)
+        def _(k):
+            go_down(k).wait_recv()
+            to_hbm(k).start()
+
+        whole(up, out).wait_send()
+
+    local(out, out_hbm, sems.at[20]).wait()
     for copies in zs:
         wait_recv(copies)
+    for name in ("ids", "cvec", "dmod", "sum", "dcond"):
+        loads[name].start()
+    for copies in zs:
         wait_send(copies)
     for copies in (idc, msgs, conds, moves, dmods, small, dcs):
         wait_send(copies)
     for piece in (tokens, projs, outs):
         piece.finish()
-    loads["latg"].wait()
-    loads["block"].wait()
-
-
-def run_block(samples, planes, labels, bands, counts, wq, wp, w1, w2, w_ada, lat, cot, bias, kept, class_table, time_table, b_ada,
-              b1):
+    for name in ("y", "ids", "cvec", "dmod", "sum", "dcond"):
+        loads[name].wait()
+
+
+def run_block(samples, planes, labels, bands, counts, wq, wp, w1, w2, w_ada, lat, cot, biases, kept, class_table, time_table):
     keep, width = kept.shape[1], wq.shape[1]
     rows, hidden, per = samples * keep, w1.shape[0], 8 * samples
     cols, depth = w_ada.shape[0], class_table.shape[0]
-    count = (2 * hidden + wq.shape[0] + wp.shape[0]) // CHUNK
+    total = 2 * hidden + wq.shape[0] + wp.shape[0]
+    count = total // PIECE
     shape, room = jax.ShapeDtypeStruct, pltpu.VMEM
     blocks = room((8, rows, width), BF16)
     plain = room((rows, width), F32)
-    copies = 8 * 6 + 7 + 3 * 10 + 3 * count + 8 * 7 + 5 * (planes - 1)
+    over_z = [
+        ((planes, per, cols), BF16),
+        ((planes, per, depth), F32),
+        ((planes, per, width), BF16),
+        ((planes, 4 + hidden // depth, depth), F32),
+        ((planes, per, 128), F32),
+    ]
+    sends, recvs = 6 + 2 + 3 + 3 + 8 + 5, 8 * 6 + 2 * 7 + 3 * 14 + 3 * count + 8 + 5
     return pl.pallas_call(
         functools.partial(block_kernel, samples, planes),
         out_shape=[
-            shape((count, CHUNK, width), BF16),
-            shape(lat.shape, BF16),
-            shape(lat.shape, BF16),
+            shape((total, width), BF16),
+            shape((rows, width), BF16),
+            shape((rows, width), BF16),
             shape((8,) + wq.shape, BF16),
-            shape((planes, per, cols), F32),
-            shape((planes, per, depth), F32),
-            shape((planes, 8, per, depth), BF16),
-            shape((planes, 16, width), F32),
-            shape((planes, per, 128), F32),
+            *[shape(dims, kind) for dims, kind in over_z],
         ],
-        in_specs=[SMEM] * 3 + [ANY] * 7 + [VMEM] * 6,
-        out_specs=[ANY] * 4 + [VMEM] * 5,
+        in_specs=[SMEM] * 3 + [ANY] * 7 + [VMEM] * 8,
+        out_specs=[ANY] * 9,
         scratch_shapes=[
+            *[room(dims, kind) for dims, kind in over_z],
             room((8,) + wq.shape, BF16),
             room((8,) + wp.shape, BF16),
             room(w1.shape, BF16),
@@ -1214,82 +1255,184 @@
             room((rows, width), BF16),
             room((8, wq.shape[0], rows), BF16),
             room((8, wq.shape[0], rows), BF16),
-            room((count, CHUNK, width), BF16),
-            room((count, CHUNK, width), BF16),
-            room(w1.shape, BF16),
-            room(w1.shape, BF16),
-            room(wq.shape, BF16),
-            room(wp.shape, BF16),
+            room((total, width), BF16),
+            room((total, width), BF16),
+            room((total, width), BF16),
             room((1, hidden), F32),
-            room((8, 8, 128), F32),
-            room((8, MSG_ROWS, wp.shape[0]), F32),
+            room((8, samples, 128), F32),
+            room((8, 4, wp.shape[0]), F32),
             room((8, per, depth), F32),
-            room((8, 8, cols), F32),
-            room((8, 8, cols), F32),
+            room((8, samples, cols), F32),
+            room((8, samples, cols), F32),
             room((samples, 8, width), F32),
             room((8, width), F32),
             room((8, per, depth), F32),
             room((8, per, depth), F32),
             room((16, width), F32),
-            room((8, 16, width), F32),
-            pltpu.SemaphoreType.DMA((copies,)),
-            pltpu.SemaphoreType.DMA((copies,)),
+            room((8, 4, wp.shape[0]), F32),
+            room((8, 4, wp.shape[0]), F32),
+            pltpu.SemaphoreType.DMA((sends,)),
+            pltpu.SemaphoreType.DMA((recvs,)),
             pltpu.SemaphoreType.REGULAR((2, 3)),
-            pltpu.SemaphoreType.DMA((16,)),
-            pltpu.SemaphoreType.DMA((count,)),
+            pltpu.SemaphoreType.DMA((21,)),
         ],
         compiler_params=params(1),
-    )(labels, bands, counts, wq, wp, w1, w2, w_ada, lat, cot, bias, kept, class_table, time_table, b_ada, b1)
+    )(labels, bands, counts, wq, wp, w1, w2, w_ada, lat, cot, *biases, kept, class_table, time_table)
+
+
+def outputs_kernel(samples, planes, counts_ref, totals_hbm, y_hbm, dx_hbm, lat_hbm, cot_hbm, kept_hbm, dmod_hbm, dcond_hbm,
+                   cvec_hbm, sum_hbm, ids_hbm,
+                   block_hbm, latg_hbm, g1_hbm, g2_hbm, gq_hbm, gp_hbm, ada_hbm, time_hbm, class_hbm, bada_hbm, qv_hbm, bp_hbm,
+                   b1_hbm, b2_hbm,
+                   kept_ref, dmod_ref, dcond_ref, cvec_ref, sum_ref, ids_ref, time_out, class_out, bada_out, qv_out, bp_out,
+                   b1_out, b2_out, totals, wide, ada, tokens, both, sems_in, sems):
+    p = Place()
+    length = lat_hbm.shape[1]
+    keep = kept_ref.shape[1]
+    chunk = 144
+    count, width = totals.shape[0] // chunk, totals.shape[1]
+    per = 8 * samples
+    chunks = [pl.ds(k * chunk, chunk) for k in range(count)]
+    ins = [local(totals_hbm.at[at], totals.at[at], sems_in.at[k]) for k, at in enumerate(chunks)]
+    ins += [
+        local(y_hbm, tokens.at[0], sems_in.at[count]),
+        local(dx_hbm, tokens.at[1], sems_in.at[count + 1]),
+        local(lat_hbm, both.at[0], sems_in.at[count + 2]),
+        local(cot_hbm, both.at[1], sems_in.at[count + 3]),
+    ]
+    pairs = ((dmod_hbm, dmod_ref), (cvec_hbm, cvec_ref), (kept_hbm, kept_ref), (dcond_hbm, dcond_ref), (sum_hbm, sum_ref), (ids_hbm, ids_ref))
+    small = [local(src, dst, sems_in.at[count + 4 + i]) for i, (src, dst) in enumerate(pairs)]
+    for copy in small + ins[count:] + ins[:count]:
+        copy.start()
+    done = []
+
+    def send(src, dst):
+        done.append(local(src, dst, sems.at[len(done)]))
+        done[-1].start()
+
+    for copy in small:
+        copy.wait()
+    cvec = jnp.concatenate([cvec_ref[k] for k in range(planes)], 0)
+    dmod = jnp.concatenate([dmod_ref[k] for k in range(planes)], 0)
+    cols = ada.shape[0]
+    for start in range(0, cols, 256):
+        size = min(256, cols - start)
+        ada[start : start + size] = dot(dmod[:, start : start + size], cvec, (0, 0))
+        send(ada.at[pl.ds(start, size)], ada_hbm.at[pl.ds(start, size)])
+    bada_out[...] = jnp.sum(dmod.astype(F32), 0)
+    send(bada_out, bada_hbm)
+
+    for copy in ins[count:]:
+        copy.wait()
+    for s in range(samples):
+        hot = own_tokens(kept_ref, length, s)
+        is_kept = jnp.sum(hot.astype(F32), 1, keepdims=True) > 0.5
+        at = pl.ds(s * keep, keep)
+        both[0, s] = jnp.where(is_kept, dot(hot, tokens[0, at], (1, 0)), both[0, s].astype(F32)).astype(BF16)
+        weighted = both[1, s].astype(F32) * sample_weight(p, counts_ref, samples, s)
+        both[1, s] = jnp.where(is_kept, dot(hot, tokens[1, at], (1, 0)), weighted).astype(BF16)
+    send(both.at[0], block_hbm)
+    send(both.at[1], latg_hbm)
+
+    k = 0
+    for out in (g1_hbm, g2_hbm, gq_hbm, gp_hbm):
+        for start in range(0, out.shape[0], chunk):
+            ins[k].wait()
+            wide[chunks[k]] = totals[chunks[k]].astype(F32)
+            send(wide.at[chunks[k]], out.at[pl.ds(start, chunk)])
+            k += 1
+
+    dcond = jnp.concatenate([dcond_ref[k] for k in range(planes)], 0)
+    ids = jnp.concatenate([ids_ref[k] for k in range(planes)], 0)
+
+    def one_hot(column, size):
+        lanes = lax.broadcasted_iota(jnp.int32, (planes * per, size), 1).astype(F32)
+        return jnp.where(lanes == ids[:, column : column + 1], 1.0, 0.0)
+
+    def exact(left, right):
+        return lax.dot_general(left, right, (((0,), (0,)), ((), ())), precision=HIGH, preferred_element_type=F32)
+
+    time_out[...] = exact(one_hot(1, time_out.shape[0]), dcond)
+    send(time_out, time_hbm)
+    class_out[...] = exact(dcond, one_hot(0, class_out.shape[1]))
+    send(class_out, class_hbm)
+    sums = sum(sum_ref[k] for k in range(planes))
+    joined = lambda start, stop: jnp.concatenate([sums[i : i + 1, :] for i in range(start, stop)], 1)
+    places = ((bp_out, bp_hbm, 0, 1), (b2_out, b2_hbm, 1, 2), (qv_out, qv_hbm, 2, 4), (b1_out, b1_hbm, 4, sums.shape[0]))
+    for out, hbm, start, stop in places:
+        out[...] = joined(start, stop).reshape(out.shape[0])
+        send(out, hbm)
+    for copy in done:
+        copy.wait()
+
+
+def place_outputs(samples, planes, counts, totals, y, dx, lat, cot, kept, dmod, dcond, cvec, sums, ids, hidden, wq, wp, classes, bands):
+    count, width = totals.shape[0] // 144, totals.shape[1]
+    cols, depth = dmod.shape[2], dcond.shape[2]
+    shape, room = jax.ShapeDtypeStruct, pltpu.VMEM
+    wide = lambda size: shape((size, width), F32)
+    return pl.pallas_call(
+        functools.partial(outputs_kernel, samples, planes),
+        out_shape=[
+            shape(lat.shape, BF16),
+            shape(lat.shape, BF16),
+            wide(hidden),
+            wide(hidden),
+            wide(wq),
+            wide(wp),
+            wide(cols),
+            shape((bands, depth), F32),
+            shape((depth, classes), F32),
+            shape((cols,), F32),
+            shape((2 * wp,), F32),
+            shape((wp,), F32),
+            shape((hidden,), F32),
+            shape((wp,), F32),
+        ],
+        in_specs=[SMEM] + [ANY] * 11,
+        out_specs=[ANY] * 14,
+        scratch_shapes=[
+            room(kept.shape, jnp.int32),
+            room(dmod.shape, BF16),
+            room(dcond.shape, F32),
+            room(cvec.shape, BF16),
+            room(sums.shape, F32),
+            room(ids.shape, F32),
+            room((bands, depth), F32),
+            room((depth, classes), F32),
+            room((cols,), F32),
+            room((2 * wp,), F32),
+            room((wp,), F32),
+            room((hidden,), F32),
+            room((wp,), F32),
+            room(totals.shape, BF16),
+            room(totals.shape, F32),
+            room((cols, width), F32),
+            room((2,) + y.shape, BF16),
+            room((2,) + lat.shape, BF16),
+            pltpu.SemaphoreType.DMA((count + 10,)),
+            pltpu.SemaphoreType.DMA((count + 9 + -(-cols // 256),)),
+        ],
+        compiler_params=pltpu.CompilerParams(vmem_limit_bytes=63 * 2**20),
+    )(counts, totals, y, dx, lat, cot, kept, dmod, dcond, cvec, sums, ids)
 
 
 def plane_body(planes, latents, cotangent, bands, labels, kept, band_counts, time_table, class_table, w_ada, b_ada, w_qkv,
                qv_bias, w_proj, b_proj, w_fc1, b_fc1, w_fc2, b_fc2):
     samples, length, width = latents.shape
-    g = lax.axis_index("grp")
     wq = w_qkv.shape[1]
     wp = w_proj.shape[0]
     hidden = w_fc1.shape[1]
-    per = 8 * samples
-
-    bias = jnp.concatenate([b_proj, b_fc2, qv_bias]).astype(F32).reshape(4, wp)
-    totals, block_out, latents_grad, unused_weights, dmod_z, dcond_z, cvec_z, sum_z, ids_z = run_block(
-        samples, planes, labels, bands, band_counts, w_qkv.T, w_proj, w_fc1.T, w_fc2, w_ada.T, latents, cotangent, bias, kept,
-        class_table.T, time_table, b_ada.astype(F32)[None], b_fc1.astype(F32)[None]
-    )
-    totals = totals.reshape(-1, width)
-    at = 0
-    pieces = []
-    for size in (hidden, hidden, wq, wp):
-        pieces.append(totals[at : at + size].astype(F32))
-        at += size
-    cvec_z = cvec_z.transpose(0, 2, 1, 3).reshape(planes * per, width)
-    mod_z = dmod_z.reshape(planes * per, -1).astype(BF16)
-    ada_grad = jnp.einsum("se,sd->ed", mod_z, cvec_z, preferred_element_type=F32).T
-    ada_bias_grad = jnp.sum(mod_z.astype(F32), 0)
-    sums = jnp.sum(sum_z, 0)
-    part = lambda v, size: lax.dynamic_slice_in_dim(v, g * size, size, 0)
-    qkv_sums = sums[8:, :wq].reshape(-1)
-    qv_grad = part(jnp.concatenate([qkv_sums[:width], qkv_sums[2 * width :]]), qv_bias.shape[0])
-    dcond = dcond_z.reshape(planes * per, -1)
-    ids_z = ids_z.reshape(planes * per, -1)
-    hot_class = (jnp.arange(class_table.shape[0], dtype=F32)[None, :] == ids_z[:, 0:1]).astype(F32)
-    hot_time = (jnp.arange(time_table.shape[0], dtype=F32)[:, None] == ids_z[:, 1][None, :]).astype(F32)
-    return (
-        block_out,
-        latents_grad,
-        jnp.dot(hot_time, dcond, precision=HIGH),
-        jnp.einsum("se,sc->ec", dcond, hot_class, precision=HIGH).T,
-        ada_grad,
-        ada_bias_grad,
-        pieces[2].T,
-        qv_grad,
-        pieces[3],
-        part(sums[0], b_proj.shape[0]),
-        pieces[0].T,
-        sums[2, :hidden],
-        pieces[1],
-        part(sums[1], b_fc2.shape[0]),
-    )
+
+    totals, y, dx, unused_weights, dmod, dcond, cvec, sums, ids = run_block(
+        samples, planes, labels, bands, band_counts, w_qkv.T, w_proj, w_fc1.T, w_fc2, w_ada.T, latents, cotangent,
+        (b_proj, b_fc2, qv_bias, b_ada, b_fc1), kept, class_table.T, time_table
+    )
+    block_out, latents_grad, g1, g2, gq, gp, ada, time, classes, bada, qv, bp, b1, b2 = place_outputs(
+        samples, planes, band_counts, totals, y, dx, latents, cotangent, kept, dmod, dcond, cvec, sums, ids, hidden, wq, wp,
+        class_table.shape[0], time_table.shape[0]
+    )
+    return (block_out, latents_grad, time, classes.T, ada.T, bada, gq.T, qv, gp, bp, g1.T, b1, g2, b2)
 
 
 def solution(mesh):

time: 260 us -> 212 us (0.82)
  Pallas kernels: 230 us -> 210 us
  local copies, waits for them, and re-layouts: 11.9 us -> 0 us
  other arithmetic: 10.2 us -> 0 us
  matrix products: 5.57 us -> 0 us
    pallas_call x1, Pallas kernels: 230 us -> 202 us  [run_block(): pl.pallas_call(functools.partial(block_kernel, samples, planes), out_shap...]
    pallas_call x0 -> x1, Pallas kernels: none -> 8.15 us  [place_outputs(): pl.pallas_call(functools.partial(outputs_kernel, samples, planes), out_sh...]
    dot_general x3 -> x0, matrix products: 5.57 us -> none  [the longest x1 2.67 us: plane_body(): jnp.einsum('se,sd->ed', mod_z, cvec_z, preferred_element_type=F32)]
    slice x7 -> x0, local copies, waits for them, and re-layouts: 4.74 us -> none  [the longest x2 3.21 us: plane_body(): pieces.append(totals[at:at + size].astype(F32))]
    transpose x2 -> x0, other arithmetic: 4.4 us -> none  [the longest x1 2.92 us: plane_body(): pieces[0]]
    unnamed x12 -> x0, local copies, waits for them, and re-layouts: 2.86 us -> none
    convert_element_type x2 -> x0, other arithmetic: 2.63 us -> none  [the longest x1 1.86 us: plane_body(): pieces.append(totals[at:at + size].astype(F32))]
where the time goes in v3:
time: 212 us
  Pallas kernels  210 us (99%)
    pallas_call x1, Pallas kernels, run_block(): pl.pallas_call(functools.partial(block_kernel, samples, planes), out_shap...  202 us
    pallas_call x1, Pallas kernels, place_outputs(): pl.pallas_call(functools.partial(outputs_kernel, samples, planes), out_sh...  8.15 us

profile of v3, /device:TPU:0, one launch (start us, length us, event | category | flops | bytes accessed | tf_op | source)
XLA Modules:
  0.0 211.7 jit_solution(4032704038262172396)
XLA Ops:
  1.3 202.1 %shard_map.281 = (bf16[1728,1152]{1,0:T(8,128)(2,1)}, bf16[256,1152]{1,0:T(8,128)(2,1)}, bf16[256,1152]{1,0:T(8,128)(2,1)}, bf16[8,432,1152]{2,1,0:T(8,128)(2,1)...) custom-call(s32[2]{0:T(128)} %labels_ref.1, ...), custom_call_target="tpu_custom_call" | custom-call | tf_op jit(solution)/shard_map/pallas_call | solution.py:1224
  203.4 8.1 %shard_map.282 = (bf16[2,256,1152]{2,1,0:T(8,128)(2,1)}, bf16[2,256,1152]{2,1,0:T(8,128)(2,1)}, f32[576,1152]{1,0:T(8,128)}, f32[576,1152]{1,0:T(8,128)}, f32[43...) custom-call(s32[1]{0:T(128)S(6)} %copy.32.counts_ref, ...), custom_call_target="tpu_custom_call" | custom-call | tf_op jit(solution)/shard_map/pallas_call | solution.py:1374

commit v4 on v3

--- a/solution.py
+++ b/solution.py
@@ -386,6 +386,37 @@
         self.sent.wait_send()
 
 
+class Halves:
+    def __init__(self, place, wire, buf):
+        self.lo, self.hi = [Gather(place, wire, buf, part.start, part.size) for part in halves(buf.shape[1])]
+
+    def start(self):
+        for number in (0, 1, 2):
+            self.lo.c[number].start()
+        for number in (0, 1, 2):
+            self.hi.c[number].start()
+
+    def far(self):
+        self.lo.far()
+        self.hi.far()
+
+    def wait_sib(self):
+        self.lo.wait_sib()
+        self.hi.wait_sib()
+
+    def wait_sib_neighbours(self):
+        self.lo.wait_sib_neighbours()
+        self.hi.wait_sib_neighbours()
+
+    def wait_sib_far(self):
+        self.lo.wait_sib_far()
+        self.hi.wait_sib_far()
+
+    def finish(self):
+        self.lo.finish()
+        self.hi.finish()
+
+
 class OverZ:
     def __init__(self, place, wire, buf, hbm, there, ahead, behind, rows):
         p = place
@@ -421,11 +452,13 @@
         self.sib = [p.block(1, q & 1, q >> 1) for q in range(4)]
         self.mine = [p.block(0, q & 1, q >> 1) for q in range(4)]
         xd, yd, sd = p.device(0, 1, 0), p.device(0, 0, 1), p.device(1, 0, 0)
-        sem, recv = wire.take(14)
+        sem, recv = wire.take(15)
         whole = pl.ds(0, rows)
         lo, hi = halves(rows)
         self.parts = [[pl.ds(half.start + cut.start, cut.size) for cut in halves(half.size)] for half in (lo, hi)]
-        self.s1 = [w.copy(sem, recv + q, buf.at[self.sib[q], whole], r1.at[q, whole], sd) for q in range(4)]
+        self.s1 = [w.copy(sem, recv + q, buf.at[self.sib[q], whole], r1.at[q, whole], sd) for q in range(3)]
+        self.far_sib = [w.copy(sem, recv + 3 + 11 * i, buf.at[self.sib[3], half], r1.at[3, half], sd) for i, half in enumerate((lo, hi))]
+        self.lo_hi = (lo, hi)
         self.s2, self.s3 = [], []
         for way, device in ((0, xd), (1, yd)):
             for i, part in enumerate(self.parts[way]):
@@ -440,9 +473,15 @@
         self.sent = wire.copy(sem, recv, seven, seven, sd)
 
     def send_sib(self, q):
-        self.s1[q].start()
+        for copy in self.far_sib if q == 3 else [self.s1[q]]:
+            copy.start()
 
     def add_sib(self, q):
+        if q == 3:
+            for copy, half in zip(self.far_sib, self.lo_hi):
+                copy.wait_recv()
+                add_into(self.buf.at[self.mine[3], half], self.r1.at[3, half])
+            return
         self.s1[q].wait_recv()
         add_into(self.buf.at[self.mine[q], pl.ds(0, self.rows)], self.r1.at[q, pl.ds(0, self.rows)])
 
@@ -457,15 +496,15 @@
         self.add_sib(2)
         self.s3[3].start()
 
-    def relay(self):
-        for i in range(2):
-            for way in range(2):
-                self.s2[2 * way + i].wait_recv()
-                part = self.parts[way][i]
-                came = self.r2.at[way, pl.ds(part.start - self.parts[way][0].start, part.size)]
-                add_into(self.buf.at[self.mine[2 - way], part], came)
-                self.s3[3 * (1 - way) + 1 + i].start()
-        self.add_sib(0)
+    def relay(self, i):
+        for way in range(2):
+            self.s2[2 * way + i].wait_recv()
+            part = self.parts[way][i]
+            came = self.r2.at[way, pl.ds(part.start - self.parts[way][0].start, part.size)]
+            add_into(self.buf.at[self.mine[2 - way], part], came)
+            self.s3[3 * (1 - way) + 1 + i].start()
+        if i == 1:
+            self.add_sib(0)
 
     def result(self, out):
         for copy in self.s3:
@@ -570,9 +609,9 @@
 
 
 def probabilities(q, k):
-    scores = dot(q, k, (0, 0)) * SCALE
-    exps = jnp.exp(scores - jnp.max(scores, -1, keepdims=True))
-    return exps / jnp.sum(exps, -1, keepdims=True)
+    scores = dot(k, q, (0, 0)) * SCALE
+    exps = jnp.exp(scores - jnp.max(scores, 0, keepdims=True))
+    return exps / jnp.sum(exps, 0, keepdims=True)
 
 
 def arrival(p, t, last=7):
@@ -646,8 +685,8 @@
     beyond = pair - inside
     outward = Gather(p, wire, wp, beyond * odd, inside, wp_hbm.at[pl.ds(beyond * odd, inside)])
     proj_z = OverZ(p, wire, wp, wp_hbm, there, inside * odd, inside * (1 - odd), beyond)
-    main = Gather(p, wire, h2_all)
-    back = Gather(p, wire, dm_all)
+    main = Halves(p, wire, h2_all)
+    back = Halves(p, wire, dm_all)
     tokens = Gather(p, wire, h1_all)
     sums = Scatter(p, wire, wq, p1, p2, p3, rows)
     outs = Scatter(p, wire, h2_all, dm_all.at[pl.ds(0, 4)], dm_all.at[pl.ds(4, 2)], dm_all.at[pl.ds(6, 2)])
@@ -686,7 +725,7 @@
             go_down(k).start()
             to_hbm(k).start()
 
-    def chain(k, lag=3):
+    def chain(k, lag):
         chain_up(k)
         chain_down(k - lag)
 
@@ -760,6 +799,8 @@
     qkv_z.own.start()
     loads["w1"].start()
     loads["w2"].start()
+    outward.start()
+    proj_z.own.start()
     gather_a.far()
     qkv_z.out[2].start()
     wait_recv(modc)
@@ -785,61 +826,67 @@
 
     @pl.loop(0, 24)
     def _(n):
-        for base, gather in ((0, gather_a), (8, gather_m)):
-
-            @pl.when(n == base + 1)
-            def _(gather=gather):
-                gather.wait_sib()
-
-            @pl.when(n == base + 4)
-            def _(gather=gather):
-                gather.wait_sib_neighbours()
-
-            if base:
-
-                @pl.when(n == base + 6)
-                def _(gather=gather):
-                    gather.far()
-
-            @pl.when(n == base + 7)
-            def _(gather=gather):
-                gather.wait_sib_far()
-
-        @pl.when(n == 6)
+        @pl.when(n == 1)
+        def _():
+            gather_a.wait_sib()
+
+        @pl.when(n == 4)
+        def _():
+            gather_a.wait_sib_neighbours()
+
+        @pl.when(n == 7)
+        def _():
+            gather_a.wait_sib_far()
+
+        @pl.when(n == 9)
+        def _():
+            gather_m.wait_sib()
+
+        @pl.when(n == 8)
         def _():
             gather_m.neighbours()
-            outward.start()
-            proj_z.own.start()
-
-        @pl.when(n == 16)
+
+        @pl.when(n == 12)
+        def _():
+            gather_m.wait_sib_neighbours()
+
+        @pl.when(n == 14)
         def _():
             outward.neighbours()
-            back.start()
             proj_z.out[0].start()
             proj_z.out[1].start()
-
-        @pl.when(n == 17)
+            back.start()
+
+        @pl.when(n == 15)
         def _():
             qkv_z.own.wait_recv()
+            qkv_z.pass_on(0, 1)
 
         @pl.when(n == 18)
         def _():
-            qkv_z.pass_on(0, 1)
+            qkv_z.arrived(0, 1)
+            gather_m.far()
 
         @pl.when(n == 20)
         def _():
-            qkv_z.arrived(0, 1)
+            qkv_z.pass_on(2)
+
+        @pl.when(n == 21)
+        def _():
+            gather_m.wait_sib_far()
 
         @pl.when(n == 22)
         def _():
-            qkv_z.pass_on(2)
+            outward.far()
+            proj_z.out[2].start()
 
         @pl.when(n == 23)
         def _():
             qkv_z.arrived(2)
 
-        phase = lax.div(n, 8)
-        block = arrival(p, lax.rem(n, 8))
+        phase = jnp.where(n < 8, 0, jnp.where((n < 14) | (n == 20) | (n == 21), 1, 2))
+        turn = jnp.where(n < 8, n, jnp.where(n < 14, n - 8, jnp.where(n < 20, n - 14, jnp.where(n < 22, n - 14, n - 16))))
+        block = arrival(p, turn)
         third = jnp.where(phase == 0, 2 * odd, jnp.where(phase == 1, 1, 2 - 2 * odd))
         chunk = block * 3 + third
         bias_at = jnp.where(chunk >= 16, chunk - 8, chunk)
@@ -854,28 +901,25 @@
     loads["keep"].start()
     zs = [to_planes(ids_z), to_planes(cvec_z)]
 
-    @pl.loop(0, 8)
-    def _(u):
-        @pl.when(u == 3)
-        def _():
-            outward.far()
-            proj_z.out[2].start()
-
-        for s in range(samples):
-            lanes = pl.ds(s * keep, keep)
-            pieces = []
-            for e in range(2):
-                probs = probabilities(units[2 * u + e, :, lanes], units[16 + 2 * u + e, :, lanes])
-                pieces.append(dot(units[32 + 2 * u + e, :, lanes], probs.astype(BF16), (1, 1)))
-            att[u, :, lanes] = jnp.concatenate(pieces, 0).astype(BF16)
-
-    back.neighbours()
+    @pl.loop(0, 4)
+    def _(i):
+        for u in (2 * i, 2 * i + 1):
+            for s in range(samples):
+                lanes = pl.ds(s * keep, keep)
+                pieces = []
+                for e in range(2):
+                    probs = probabilities(units[2 * u + e, :, lanes], units[16 + 2 * u + e, :, lanes])
+                    pieces.append(dot(units[32 + 2 * u + e, :, lanes], probs.astype(BF16), (1, 0)))
+                att[u, :, lanes] = jnp.concatenate(pieces, 0).astype(BF16)
+
+    back.lo.neighbours()
     loads["wp"].wait()
     outward.wait_sib()
     outward.wait_sib_neighbours()
     outward.wait_sib_far()
     proj_z.own.wait_recv()
     proj_z.pass_on(0, 1, 2)
+    back.hi.neighbours()
     proj_z.arrived(0, 1, 2)
     proj[...] = jnp.zeros_like(proj)
 
@@ -899,68 +943,114 @@
     loads["w2"].wait()
     loads["keep"].wait()
 
-    def hidden(block):
-        pre = dot(h2_all[block], w1[...], (1, 1)) + b1
+    half_rows = rows // 2
+
+    def hidden(places):
+        both = lambda ref: jnp.concatenate([ref[block, at] for block, at in places], 0)
+        pre = dot(both(h2_all), w1[...], (1, 1)) + b1
         value, slope = gelu_parts(pre)
-        act[block] = value.astype(BF16)
-        low = (dot(dm_all[block], w2[...], (1, 1)) * slope).astype(BF16)
-        dpre[block] = low
+        value = value.astype(BF16)
+        low = (dot(both(dm_all), w2[...], (1, 1)) * slope).astype(BF16)
         gb1[...] += jnp.sum(low.astype(F32), 0, keepdims=True)
-        wq[block, pl.ds(0, rows)] = dot(low, w1[...], (1, 0)).astype(BF16)
+        share = dot(low, w1[...], (1, 0)).astype(BF16)
+        for i, (block, at) in enumerate(places):
+            part = slice(i * half_rows, (i + 1) * half_rows)
+            act[block, at] = value[part]
+            dpre[block, at] = low[part]
+            wq[block, at] = share[part]
 
     @pl.loop(0, 8)
-    def _(t):
-        @pl.when(t == 1)
+    def _(n):
+        @pl.when(n == 1)
         def _():
             main.wait_sib()
             back.wait_sib()
 
-        @pl.when(t == 2)
-        def _():
-            main.neighbours()
+        @pl.when(n == 2)
+        def _():
+            main.lo.neighbours()
             back.wait_sib_neighbours()
             back.wait_sib_far()
 
-        @pl.when(t == 4)
-        def _():
-            main.wait_sib_neighbours()
-
-        @pl.when(t == 6)
-        def _():
-            main.far()
+        @pl.when(n == 3)
+        def _():
+            main.lo.wait_sib_neighbours()
+
+        @pl.when(n == 4)
+        def _():
+            main.hi.neighbours()
+
+        @pl.when(n == 5)
+        def _():
+            main.hi.wait_sib_neighbours()
+
+        @pl.when(n == 6)
+        def _():
+            main.lo.far()
             sums.send_near()
-            main.wait_sib_far()
-
-        hidden(arrival(p, t, 6))
-        for at, q in ((1, 0), (4, 1), (5, 2), (6, 3)):
-
-            @pl.when(t == at)
-            def _(q=q):
-                sums.send_sib(q)
+            main.lo.wait_sib_far()
+
+        @pl.when(n == 7)
+        def _():
+            main.hi.far()
+            main.hi.wait_sib_far()
+
+        upper = (n == 4) | (n == 5) | (n == 7)
+        turn = jnp.where(n < 2, n, jnp.where(n < 6, 2 + 2 * lax.rem(n, 2), 6))
+        halves_at = (jnp.where(upper, 1, 0), jnp.where(upper | (n < 2), 1, 0))
+        turns = (turn, jnp.where(n < 2, turn, turn + 1))
+        hidden([(arrival(p, t, 6), pl.ds(pl.multiple_of(h * half_rows, 16), half_rows)) for t, h in zip(turns, halves_at)])
+
+        @pl.when(n == 1)
+        def _():
+            sums.send_sib(0)
+
+        @pl.when(n == 5)
+        def _():
+            sums.send_sib(1)
+            sums.send_sib(2)
+
+        @pl.when(n == 6)
+        def _():
+            sums.far_sib[0].start()
+
+        @pl.when(n == 7)
+        def _():
+            sums.far_sib[1].start()
 
     sums.send_far()
 
     def weight_grad(left, right, base, between):
-        for ref, start, size in ((dx2, 0, 256), (tmp, 256, 256), (rest, 512, hidden_units - 512)):
-            ref[0:size] = jnp.zeros((size, width), F32)
-
-            @pl.loop(0, 4)
-            def _(i):
-                two = pl.ds(2 * i, 2)
-                part = left[two, :, pl.ds(start, size)].reshape(2 * rows, size)
-                ref[0:size] += dot(part, right[two].reshape(2 * rows, width), (0, 0))
-
-            grads[base + start : base + start + size] = ref[0:size].astype(BF16)
-            chain_send(-(-(base + start) // PIECE) if start == 0 else (base + start) // PIECE, (base + start + size) // PIECE)
-            between(start)
-
-    weight_grad(dpre, h2_all, 0, lambda start: None)
-    sums.relay()
+        for n, (start, size) in enumerate(((0, 128), (128, 256), (384, hidden_units - 384))):
+            part = left[:, :, pl.ds(start, size)].reshape(8 * rows, size)
+            grads[base + start : base + start + size] = dot(part, right[...].reshape(8 * rows, width), (0, 0)).astype(BF16)
+            chain_send(-(-base // PIECE) if n == 0 else (base + start) // PIECE, (base + start + size) // PIECE)
+            between(n)
+
+    def output_blocks(first, last):
+        @pl.loop(first, last)
+        def _(block):
+            h2_all[block] = jnp.dot(act[block], w2[...], preferred_element_type=F32).astype(BF16)
+
+    def visit(n):
+        if n == 0:
+            chain_up(0)
+            sums.relay(0)
+        elif n == 1:
+            chain_up(1)
+            sums.relay(1)
+            tokens.start()
+            chain_up(2)
+            chain_down(0)
+
+    weight_grad(dpre, h2_all, 0, lambda n: None)
+    weight_grad(act, dm_all, hidden_units, visit)
     main.finish()
-    tokens.start()
-    chain_up(0)
-    weight_grad(act, dm_all, hidden_units, lambda start: chain_up(1 + start // 256))
-    chain_down(0)
+    chain_up(3)
+    chain_down(1)
+    output_blocks(0, 3)
+    chain_up(4)
+    chain_down(2)
     back.finish()
     grant(0)
     sums.result(tmp)
@@ -976,6 +1066,11 @@
     SUM_PROJ, SUM_FC2 = 6 * samples, 6 * samples + 1
 
     def second_back(s, at):
+        @pl.when(at.start == rows // 2)
+        def _():
+            chain_up(5)
+            chain_down(3)
+
         hat, inv = normed(mixed[at])
         up_grad = tmp[at]
         value = grad[at] + norm_back(up_grad * (1.0 + mod[s, 4:5, :]), hat, inv)
@@ -988,16 +1083,12 @@
         add_row(SUM_PROJ, low.astype(F32))
         add_row(SUM_FC2, (mod[s, 5:6, :] * grad[at]).astype(BF16).astype(F32))
 
-    chain_up(4)
     by_rows(samples, keep, second_back)
-    chain_down(1)
-    chain_up(5)
-    chain_down(2)
+    chain_down(4)
     outward.finish()
     proj_z.finish()
 
-    @pl.loop(0, 8)
-    def _(u):
+    def heads_back(u):
         datt = dot(wp[u], dproj[...], (1, 1))
         wp[u] = dot(att[u], dproj[...], (1, 0)).astype(BF16)
         lists = ([], [], [])
@@ -1008,12 +1099,12 @@
                 q, k, v = (units[16 * i + 2 * u + e, :, lanes] for i in range(3))
                 da = datt[e * HEAD_DIM : (e + 1) * HEAD_DIM, s * keep : (s + 1) * keep].astype(BF16)
                 probs = probabilities(q, k)
-                dprobs = dot(da, v, (0, 0))
-                dscores = probs * (dprobs - jnp.sum(dprobs * probs, -1, keepdims=True))
+                dprobs = dot(v, da, (0, 0))
+                dscores = probs * (dprobs - jnp.sum(dprobs * probs, 0, keepdims=True))
                 dscores = dscores.astype(BF16)
-                parts[0].append(dot(k, dscores, (1, 1)) * SCALE)
-                parts[1].append(dot(q, dscores, (1, 0)) * SCALE)
-                parts[2].append(dot(da, probs.astype(BF16), (1, 0)))
+                parts[0].append(dot(k, dscores, (1, 0)) * SCALE)
+                parts[1].append(dot(q, dscores, (1, 1)) * SCALE)
+                parts[2].append(dot(da, probs.astype(BF16), (1, 1)))
             for i in range(3):
                 lists[i].append(jnp.concatenate(parts[i], 0).astype(BF16))
         for i in range(3):
@@ -1022,18 +1113,41 @@
             for s in range(samples):
                 dq[lax.div(chunk, 3), at, pl.ds(s * keep, keep)] = lists[i][s]
 
-        @pl.when(u == 4)
-        def _():
-            tokens.neighbours()
-
-        chain(6 + u)
+    visits = {
+        (0, 0): ((6,), ()),
+        (0, 1): ((7,), (5,)),
+        (1, 1): ((8,), (6,)),
+        (2, 0): ((9,), (7,)),
+        (2, 1): ((10,), ()),
+        (3, 0): ((), (8,)),
+        (3, 1): ((11,), (9,)),
+    }
+
+    @pl.loop(0, 4)
+    def _(i):
+        for e in range(2):
+            heads_back(2 * i + e)
+            if e == 0:
+
+                @pl.when(i == 2)
+                def _():
+                    tokens.neighbours()
+
+            for (at, half), (ups, downs) in visits.items():
+                if half == e:
+
+                    @pl.when(i == at)
+                    def _(ups=ups, downs=downs):
+                        for k in ups:
+                            chain_up(k)
+                        for k in downs:
+                            chain_down(k)
 
     dq_all[g] = dq[g]
     moves = to_all(p, wire, dq_all, lambda rel: dq.at[p.block(*rel)])
     granted(1)
     for q in (3, 1, 2, 0):
         projs.send_sib(q)
-    tokens.far()
 
     loads["again"].wait()
     proj[...] = jnp.zeros_like(proj)
@@ -1041,44 +1155,37 @@
     @pl.loop(0, 8)
     def _(j):
         proj[...] += dot(dq[j], wq[j], (0, 0))
-        for at in range(2):
-
-            @pl.when(j == 4 * at + 3)
-            def _(at=at):
-                chain(14 + at)
+        for at, step, k in ((1, chain_up, 12), (3, chain_down, 10), (6, chain_up, 13)):
+
+            @pl.when(j == at)
+            def _(step=step, k=k):
+                step(k)
 
     loads["latb"].start()
 
+    chain_down(11)
     granted(0)
-
-    @pl.loop(0, 8)
-    def _(t):
-        block = arrival(p, 7 - t)
-        h2_all[block] = jnp.dot(act[block], w2[...], preferred_element_type=F32).astype(BF16)
-
-        for at in range(2):
-
-            @pl.when(t == 4 * at + 3)
-            def _(at=at):
-                chain(16 + at)
-
-        for at, q in ((1, 0), (4, 1), (5, 2), (7, 3)):
-
-            @pl.when(t == 7 - at)
-            def _(q=q):
-                outs.send_sib(q)
-
+    output_blocks(3, 6)
+    chain(14, 2)
+    output_blocks(6, 8)
+    for q in (3, 1, 2, 0):
+        outs.send_sib(q)
     loads["ada1b"].start()
     loads["ada2b"].start()
+    for k in range(15, 18):
+        chain(k, 2)
+    tokens.far()
+    for k in range(18, 22):
+        chain(k, 2)
     tokens.wait_sib()
     tokens.wait_sib_neighbours()
     tokens.wait_sib_far()
-    for k in range(18, 22):
-        chain(k)
 
     wait_recv(moves)
     projs.send_far()
     projs.send_near()
+    outs.send_far()
+    chain(22, 2)
     for i in range(3):
         at = pl.ds(i * pair, pair)
         tmp[0:pair] = jnp.zeros((pair, width), F32)
@@ -1089,11 +1196,19 @@
 
         gq[at] = tmp[0:pair].astype(BF16)
         chain_send(24 + 3 * i, 27 + 3 * i)
-        chain(22 + i)
-    projs.relay()
-    outs.send_far()
-    outs.send_near()
-    chain(25)
+        if i == 0:
+            chain(23, 2)
+            projs.relay(0)
+            projs.relay(1)
+            outs.send_near()
+            chain(24, 2)
+        elif i == 1:
+            chain(25, 2)
+            chain(26, 2)
+        else:
+            chain(27, 2)
+            outs.relay(0)
+            outs.relay(1)
 
     loads["latb"].wait()
     for s in range(samples):
@@ -1101,6 +1216,10 @@
         tmp[pl.ds(s * keep, keep)] = dot(hot, wq[s, pl.ds(0, length)], (0, 0))
 
     def first_back(s, at):
+        @pl.when(at.start == rows // 2)
+        def _():
+            chain(28, 2)
+
         hat, inv = normed(tmp[at])
         up_grad = proj[at]
         dx = dx2[at] + norm_back(up_grad * (1.0 + mod[s, 1:2, :]), hat, inv)
@@ -1109,17 +1228,15 @@
         dproj[at] = dx.astype(BF16)
 
     by_rows(samples, keep, first_back)
-    chain(26)
+    loads["dx"].start()
+    chain(29, 2)
+    chain(30, 2)
+    chain(31, 2)
     projs.result(gp)
     chain_send(33, 36)
-    loads["dx"].start()
-    chain(27)
-    chain(28)
-    outs.relay()
-    for k in range(29, 35):
-        chain(k)
+    for k in range(32, 35):
+        chain(k, 2)
     outs.result(tmp)
-    chain(35)
 
     def end(s, at):
         value = tmp[at] + vec[1:2, :]
@@ -1147,7 +1264,7 @@
             share_send[j, 2 + e : 3 + e, :] = lines[u // 3][:, u % 3 * pair : (u % 3 + 1) * pair]
     share_in[g] = share_send[g]
     small = to_all(p, wire, share_in, lambda rel: share_send.at[p.block(*rel)])
-    chain_down(33)
+    chain(35, 2)
     loads["ada1b"].wait()
     loads["ada2b"].wait()
     wait_recv(dmods)
@@ -1220,7 +1337,7 @@
         ((planes, 4 + hidden // depth, depth), F32),
         ((planes, per, 128), F32),
     ]
-    sends, recvs = 6 + 2 + 3 + 3 + 8 + 5, 8 * 6 + 2 * 7 + 3 * 14 + 3 * count + 8 + 5
+    sends, recvs = 8 + 2 + 3 + 3 + 8 + 5, 8 * 8 + 2 * 7 + 3 * 15 + 3 * count + 8 + 5
     return pl.pallas_call(
         functools.partial(block_kernel, samples, planes),
         out_shape=[

time: 212 us -> 204 us (0.962)
  Pallas kernels: 210 us -> 202 us
    pallas_call x1, Pallas kernels: 202 us -> 194 us  [run_block(): pl.pallas_call(functools.partial(block_kernel, samples, planes), out_shap...]
where the time goes in v4:
time: 204 us; the launch traced here: 203 us
  Pallas kernels  202 us (99%)
    pallas_call x1, Pallas kernels, run_block(): pl.pallas_call(functools.partial(block_kernel, samples, planes), out_shap...  194 us
    pallas_call x1, Pallas kernels, place_outputs(): pl.pallas_call(functools.partial(outputs_kernel, samples, planes), out_sh...  8.15 us

profile of v4, /device:TPU:0, one launch (start us, length us, event | category | flops | bytes accessed | tf_op | source)
XLA Modules:
  0.0 203.4 jit_solution(14834141166624675070)
XLA Ops:
  1.3 193.8 %shard_map.281 = (bf16[1728,1152]{1,0:T(8,128)(2,1)}, bf16[256,1152]{1,0:T(8,128)(2,1)}, bf16[256,1152]{1,0:T(8,128)(2,1)}, bf16[8,432,1152]{2,1,0:T(8,128)(2,1)...) custom-call(s32[2]{0:T(128)} %labels_ref.1, ...), custom_call_target="tpu_custom_call" | custom-call | tf_op jit(solution)/shard_map/pallas_call | solution.py:1341
  195.1 8.1 %shard_map.282 = (bf16[2,256,1152]{2,1,0:T(8,128)(2,1)}, bf16[2,256,1152]{2,1,0:T(8,128)(2,1)}, f32[576,1152]{1,0:T(8,128)}, f32[576,1152]{1,0:T(8,128)}, f32[43...) custom-call(s32[1]{0:T(128)S(6)} %copy.32.counts_ref, ...), custom_call_target="tpu_custom_call" | custom-call | tf_op jit(solution)/shard_map/pallas_call | solution.py:1491

commit v5 on v4

--- a/solution.py
+++ b/solution.py
@@ -452,51 +452,54 @@
         self.sib = [p.block(1, q & 1, q >> 1) for q in range(4)]
         self.mine = [p.block(0, q & 1, q >> 1) for q in range(4)]
         xd, yd, sd = p.device(0, 1, 0), p.device(0, 0, 1), p.device(1, 0, 0)
-        sem, recv = wire.take(15)
+        sem, recv = wire.take(18)
         whole = pl.ds(0, rows)
         lo, hi = halves(rows)
         self.parts = [[pl.ds(half.start + cut.start, cut.size) for cut in halves(half.size)] for half in (lo, hi)]
-        self.s1 = [w.copy(sem, recv + q, buf.at[self.sib[q], whole], r1.at[q, whole], sd) for q in range(3)]
-        self.far_sib = [w.copy(sem, recv + 3 + 11 * i, buf.at[self.sib[3], half], r1.at[3, half], sd) for i, half in enumerate((lo, hi))]
         self.lo_hi = (lo, hi)
+        self.s1 = [
+            [w.copy(sem, recv + 10 + 2 * q + i, buf.at[self.sib[q], part], r1.at[q, part], sd) for i, part in enumerate((lo, hi))]
+            for q in range(4)
+        ]
         self.s2, self.s3 = [], []
         for way, device in ((0, xd), (1, yd)):
             for i, part in enumerate(self.parts[way]):
-                number = recv + 4 + 2 * way + i
+                number = recv + 2 * way + i
                 self.s2.append(w.copy(sem, number, buf.at[self.mine[3], part], r2.at[way, pl.ds(part.start - self.parts[way][0].start, part.size)], device))
         for way, device in ((0, xd), (1, yd)):
             direct = (lo, hi)[way]
             for i, part in enumerate([direct] + self.parts[1 - way]):
-                number = recv + 8 + 3 * way + i
+                number = recv + 4 + 3 * way + i
                 self.s3.append(w.copy(sem, number, buf.at[self.mine[1 + way], part], r3.at[way, part], device))
         seven = buf.at[pl.ds(0, 7), whole]
         self.sent = wire.copy(sem, recv, seven, seven, sd)
 
-    def send_sib(self, q):
-        for copy in self.far_sib if q == 3 else [self.s1[q]]:
-            copy.start()
-
-    def add_sib(self, q):
-        if q == 3:
-            for copy, half in zip(self.far_sib, self.lo_hi):
-                copy.wait_recv()
-                add_into(self.buf.at[self.mine[3], half], self.r1.at[3, half])
-            return
-        self.s1[q].wait_recv()
-        add_into(self.buf.at[self.mine[q], pl.ds(0, self.rows)], self.r1.at[q, pl.ds(0, self.rows)])
+    def send_sib(self, q, halves_of=(0, 1)):
+        for i in halves_of:
+            self.s1[q][i].start()
+
+    def add_sib(self, q, halves_of=(0, 1)):
+        for i in halves_of:
+            self.s1[q][i].wait_recv()
+            add_into(self.buf.at[self.mine[q], self.lo_hi[i]], self.r1.at[q, self.lo_hi[i]])
 
     def send_far(self):
         self.add_sib(3)
         for number in (0, 2, 1, 3):
             self.s2[number].start()
 
+    def near(self, way):
+        self.add_sib(1 + way, (way,))
+        self.s3[3 * way].start()
+
     def send_near(self):
-        self.add_sib(1)
-        self.s3[0].start()
-        self.add_sib(2)
-        self.s3[3].start()
+        self.near(0)
+        self.near(1)
 
     def relay(self, i):
+        if i == 0:
+            self.add_sib(1, (1,))
+            self.add_sib(2, (0,))
         for way in range(2):
             self.s2[2 * way + i].wait_recv()
             part = self.parts[way][i]
@@ -571,9 +574,9 @@
 
 def gelu_parts(pre):
     square = pre * pre
-    inner = jnp.tanh(GELU_A * pre * (1.0 + GELU_B * square))
-    act = 0.5 * pre * (1.0 + inner)
-    slope = 0.5 * (1.0 + inner) + 0.5 * pre * (1.0 - inner * inner) * (GELU_A * (1.0 + 3.0 * GELU_B * square))
+    half = 0.5 + 0.5 * jnp.tanh(pre * (GELU_A + GELU_A * GELU_B * square))
+    act = pre * half
+    slope = half + (act - act * half) * (2.0 * GELU_A + 6.0 * GELU_A * GELU_B * square)
     return act, slope
 
 
@@ -687,7 +690,7 @@
     proj_z = OverZ(p, wire, wp, wp_hbm, there, inside * odd, inside * (1 - odd), beyond)
     main = Halves(p, wire, h2_all)
     back = Halves(p, wire, dm_all)
-    tokens = Gather(p, wire, h1_all)
+    tokens = Halves(p, wire, h1_all)
     sums = Scatter(p, wire, wq, p1, p2, p3, rows)
     outs = Scatter(p, wire, h2_all, dm_all.at[pl.ds(0, 4)], dm_all.at[pl.ds(4, 2)], dm_all.at[pl.ds(6, 2)])
     projs = Scatter(p, wire, wp, p1, p2, p3)
@@ -695,13 +698,13 @@
     g1, g2 = part_of(0, hidden_units), part_of(hidden_units, hidden_units)
     gq, gp = part_of(2 * hidden_units, 3 * pair), part_of(2 * hidden_units + 3 * pair, pair)
     count = grads.shape[0] // PIECE
-    (up, up_r), (across, across_r), (down, down_r) = [wire.take(count) for way in range(3)]
+    (up, up_r), (across, across_r), (down, _) = [wire.take(recvs) for recvs in (count, count, 0)]
     inner, outer, partner = 1 + z // 3, (z - 1) * 3, 3 - z
     at_end = (z == 0) | (z == planes - 1)
     rows_of = lambda ref, k: ref.at[pl.ds(pl.multiple_of(k * PIECE, 16), PIECE)]
     go_up = lambda k: wire.copy(up, up_r + k, rows_of(grads, k), rows_of(from_end, k), (g, inner))
     go_across = lambda k: wire.copy(across, across_r + k, rows_of(from_end, k), rows_of(out, k), (g, partner))
-    go_down = lambda k: wire.copy(down, down_r + k, rows_of(out, k), rows_of(out, k), (g, outer))
+    go_down = lambda k: wire.copy(down, up_r + k, rows_of(out, k), rows_of(out, k), (g, outer))
     to_hbm = lambda k: local(rows_of(out, k), rows_of(out_hbm, k), sems.at[20])
 
     def chain_send(first, last):
@@ -987,12 +990,15 @@
         @pl.when(n == 6)
         def _():
             main.lo.far()
-            sums.send_near()
+            sums.send_sib(2, (1,))
+            sums.send_sib(1, (1,))
+            sums.near(0)
             main.lo.wait_sib_far()
 
         @pl.when(n == 7)
         def _():
             main.hi.far()
+            sums.near(1)
             main.hi.wait_sib_far()
 
         upper = (n == 4) | (n == 5) | (n == 7)
@@ -1005,18 +1011,18 @@
         def _():
             sums.send_sib(0)
 
-        @pl.when(n == 5)
-        def _():
-            sums.send_sib(1)
-            sums.send_sib(2)
+        @pl.when(n == 3)
+        def _():
+            sums.send_sib(1, (0,))
+            sums.send_sib(2, (0,))
 
         @pl.when(n == 6)
         def _():
-            sums.far_sib[0].start()
+            sums.send_sib(3, (0,))
 
         @pl.when(n == 7)
         def _():
-            sums.far_sib[1].start()
+            sums.send_sib(3, (1,))
 
     sums.send_far()
 
@@ -1127,11 +1133,15 @@
     def _(i):
         for e in range(2):
             heads_back(2 * i + e)
-            if e == 0:
+            if e == 1:
+
+                @pl.when(i == 1)
+                def _():
+                    tokens.lo.neighbours()
 
                 @pl.when(i == 2)
                 def _():
-                    tokens.neighbours()
+                    tokens.hi.neighbours()
 
             for (at, half), (ups, downs) in visits.items():
                 if half == e:
@@ -1163,6 +1173,8 @@
 
     loads["latb"].start()
 
+    projs.send_far()
+    projs.send_near()
     chain_down(11)
     granted(0)
     output_blocks(3, 6)
@@ -1177,14 +1189,12 @@
     tokens.far()
     for k in range(18, 22):
         chain(k, 2)
+    outs.send_far()
     tokens.wait_sib()
     tokens.wait_sib_neighbours()
     tokens.wait_sib_far()
 
     wait_recv(moves)
-    projs.send_far()
-    projs.send_near()
-    outs.send_far()
     chain(22, 2)
     for i in range(3):
         at = pl.ds(i * pair, pair)
@@ -1207,8 +1217,6 @@
             chain(26, 2)
         else:
             chain(27, 2)
-            outs.relay(0)
-            outs.relay(1)
 
     loads["latb"].wait()
     for s in range(samples):
@@ -1230,12 +1238,12 @@
     by_rows(samples, keep, first_back)
     loads["dx"].start()
     chain(29, 2)
+    outs.relay(0)
+    outs.relay(1)
     chain(30, 2)
-    chain(31, 2)
     projs.result(gp)
     chain_send(33, 36)
-    for k in range(32, 35):
-        chain(k, 2)
+    chain(31, 2)
     outs.result(tmp)
 
     def end(s, at):
@@ -1264,32 +1272,35 @@
             share_send[j, 2 + e : 3 + e, :] = lines[u // 3][:, u % 3 * pair : (u % 3 + 1) * pair]
     share_in[g] = share_send[g]
     small = to_all(p, wire, share_in, lambda rel: share_send.at[p.block(*rel)])
-    chain(35, 2)
+    chain(32, 2)
+    chain(33, 2)
     loads["ada1b"].wait()
     loads["ada2b"].wait()
     wait_recv(dmods)
     part = jnp.concatenate([mod_in[j] for j in range(8)], 0).astype(BF16)
     dmod_z[z] = part
-    zs.append(to_planes(dmod_z))
     dcvec = dot(part[:, :hidden_units], w1[...], (1, 0)) + dot(part[:, hidden_units:], w2[0:ada_rest], (1, 0))
     depth = cond_all.shape[2]
     for j in range(8):
         dc_send[j] = dcvec[:, j * depth : (j + 1) * depth]
     dc_in[g] = dc_send[g]
     dcs = to_all(p, wire, dc_in, lambda rel: dc_send.at[p.block(*rel)])
-    chain_down(34)
+    zs.append(to_planes(dmod_z))
+    chain(34, 2)
     wait_recv(small)
     sum_z[z, 0:4, :] = sum(share_in[j] for j in range(8))
     for i in range(hidden_units // pair):
         sum_z[z, 4 + i : 5 + i, :] = gb1[:, i * pair : (i + 1) * pair]
     zs.append(to_planes(sum_z))
-    chain_down(35)
+    chain(35, 2)
     wait_recv(dcs)
     cond = cond_all[g]
     gate = jax.nn.sigmoid(cond)
     dcond_z[z] = sum(dc_in[j] for j in range(8)) * (gate * (1.0 + cond * (1.0 - gate)))
     zs.append(to_planes(dcond_z))
 
+    chain_down(34)
+    chain_down(35)
     whole = lambda sem, ref: wire.copy(sem, up_r, ref, ref, (g, partner))
 
     @pl.when(jnp.logical_not(at_end))
@@ -1337,7 +1348,7 @@
         ((planes, 4 + hidden // depth, depth), F32),
         ((planes, per, 128), F32),
     ]
-    sends, recvs = 8 + 2 + 3 + 3 + 8 + 5, 8 * 8 + 2 * 7 + 3 * 15 + 3 * count + 8 + 5
+    sends, recvs = 9 + 2 + 3 + 3 + 8 + 5, 8 * 9 + 2 * 7 + 3 * 18 + 2 * count + 8 + 5
     return pl.pallas_call(
         functools.partial(block_kernel, samples, planes),
         out_shape=[
@@ -1439,6 +1450,27 @@
     bada_out[...] = jnp.sum(dmod.astype(F32), 0)
     send(bada_out, bada_hbm)
 
+    dcond = jnp.concatenate([dcond_ref[k] for k in range(planes)], 0)
+    ids = jnp.concatenate([ids_ref[k] for k in range(planes)], 0)
+
+    def one_hot(column, size):
+        lanes = lax.broadcasted_iota(jnp.int32, (planes * per, size), 1).astype(F32)
+        return jnp.where(lanes == ids[:, column : column + 1], 1.0, 0.0)
+
+    def exact(left, right):
+        return lax.dot_general(left, right, (((0,), (0,)), ((), ())), precision=HIGH, preferred_element_type=F32)
+
+    time_out[...] = exact(one_hot(1, time_out.shape[0]), dcond)
+    send(time_out, time_hbm)
+    class_out[...] = exact(dcond, one_hot(0, class_out.shape[1]))
+    send(class_out, class_hbm)
+    sums = sum(sum_ref[k] for k in range(planes))
+    joined = lambda start, stop: jnp.concatenate([sums[i : i + 1, :] for i in range(start, stop)], 1)
+    places = ((bp_out, bp_hbm, 0, 1), (b2_out, b2_hbm, 1, 2), (qv_out, qv_hbm, 2, 4), (b1_out, b1_hbm, 4, sums.shape[0]))
+    for out, hbm, start, stop in places:
+        out[...] = joined(start, stop).reshape(out.shape[0])
+        send(out, hbm)
+
     for copy in ins[count:]:
         copy.wait()
     for s in range(samples):
@@ -1459,26 +1491,6 @@
             send(wide.at[chunks[k]], out.at[pl.ds(start, chunk)])
             k += 1
 
-    dcond = jnp.concatenate([dcond_ref[k] for k in range(planes)], 0)
-    ids = jnp.concatenate([ids_ref[k] for k in range(planes)], 0)
-
-    def one_hot(column, size):
-        lanes = lax.broadcasted_iota(jnp.int32, (planes * per, size), 1).astype(F32)
-        return jnp.where(lanes == ids[:, column : column + 1], 1.0, 0.0)
-
-    def exact(left, right):
-        return lax.dot_general(left, right, (((0,), (0,)), ((), ())), precision=HIGH, preferred_element_type=F32)
-
-    time_out[...] = exact(one_hot(1, time_out.shape[0]), dcond)
-    send(time_out, time_hbm)
-    class_out[...] = exact(dcond, one_hot(0, class_out.shape[1]))
-    send(class_out, class_hbm)
-    sums = sum(sum_ref[k] for k in range(planes))
-    joined = lambda start, stop: jnp.concatenate([sums[i : i + 1, :] for i in range(start, stop)], 1)
-    places = ((bp_out, bp_hbm, 0, 1), (b2_out, b2_hbm, 1, 2), (qv_out, qv_hbm, 2, 4), (b1_out, b1_hbm, 4, sums.shape[0]))
-    for out, hbm, start, stop in places:
-        out[...] = joined(start, stop).reshape(out.shape[0])
-        send(out, hbm)
     for copy in done:
         copy.wait()
 

time: 204 us -> 202 us (level)
  no operation moved by 1% of the time
where the time goes in v5:
time: 202 us
  Pallas kernels  200 us (99%)
    pallas_call x1, Pallas kernels, run_block(): pl.pallas_call(functools.partial(block_kernel, samples, planes), out_shap...  192 us
    pallas_call x1, Pallas kernels, place_outputs(): pl.pallas_call(functools.partial(outputs_kernel, samples, planes), out_sh...  7.72 us

profile of v5, /device:TPU:0, one launch (start us, length us, event | category | flops | bytes accessed | tf_op | source)
XLA Modules:
  0.0 201.6 jit_solution(11621266531259564986)
XLA Ops:
  1.3 192.4 %shard_map.281 = (bf16[1728,1152]{1,0:T(8,128)(2,1)}, bf16[256,1152]{1,0:T(8,128)(2,1)}, bf16[256,1152]{1,0:T(8,128)(2,1)}, bf16[8,432,1152]{2,1,0:T(8,128)(2,1)...) custom-call(s32[2]{0:T(128)} %labels_ref.1, ...), custom_call_target="tpu_custom_call" | custom-call | tf_op jit(solution)/shard_map/pallas_call | solution.py:1352
  193.7 7.7 %shard_map.282 = (bf16[2,256,1152]{2,1,0:T(8,128)(2,1)}, bf16[2,256,1152]{2,1,0:T(8,128)(2,1)}, f32[576,1152]{1,0:T(8,128)}, f32[576,1152]{1,0:T(8,128)}, f32[43...) custom-call(s32[1]{0:T(128)S(6)} %copy.32.counts_ref, ...), custom_call_target="tpu_custom_call" | custom-call | tf_op jit(solution)/shard_map/pallas_call | solution.py:1503

commit v6 on v5

--- a/solution.py
+++ b/solution.py
@@ -637,8 +637,9 @@
 
 
 def block_kernel(samples, planes, labels_ref, bands_ref, counts_ref, wq_hbm, wp_hbm, w1_hbm, w2_hbm, ada_hbm, lat_hbm, cot_hbm,
+                 bp_hbm, b2_hbm, qv_hbm, bada_hbm, b1_hbm, kept_hbm, class_hbm, time_hbm,
+                 out_hbm, y_hbm, dx_hbm, wq_keep, dmod_hbm, dcond_hbm, cvec_hbm, sum_hbm, ids_hbm,
                  bp_ref, b2_ref, qv_ref, bada_ref, b1_ref, kept_ref, class_ref, time_ref,
-                 out_hbm, y_hbm, dx_hbm, wq_keep, dmod_hbm, dcond_hbm, cvec_hbm, sum_hbm, ids_hbm,
                  dmod_z, dcond_z, cvec_z, sum_z, ids_z,
                  wq, wp, w1, w2, h1_all, h2_all, dm_all, act, dpre, p1, p2, p3, units, att, mixed, proj, grad, dx2, tmp, rest,
                  dproj, dq, dq_all, from_end, out, grads, gb1, ids_all, msg_all, cond_all, mod_in, mod_send, mod, vec,
@@ -647,7 +648,22 @@
     wire = Wire(send, recv)
     g, z = p.g, p.z
     others = [(g, (z + k) % planes) for k in range(1, planes)]
+    smalls = (
+        (bp_hbm, bp_ref),
+        (b2_hbm, b2_ref),
+        (qv_hbm, qv_ref),
+        (bada_hbm, bada_ref),
+        (b1_hbm, b1_ref),
+        (kept_hbm, kept_ref),
+        (class_hbm, class_ref),
+        (time_hbm, time_ref),
+    )
+    early = [local(src, dst, sems.at[21 + i]) for i, (src, dst) in enumerate(smalls)]
+    for copy in early:
+        copy.start()
     greet(plane(p) + others)
+    for copy in early:
+        copy.wait()
     length = lat_hbm.shape[1]
     keep = kept_ref.shape[1]
     rows, width = mixed.shape
@@ -1024,8 +1040,6 @@
         def _():
             sums.send_sib(3, (1,))
 
-    sums.send_far()
-
     def weight_grad(left, right, base, between):
         for n, (start, size) in enumerate(((0, 128), (128, 256), (384, hidden_units - 384))):
             part = left[:, :, pl.ds(start, size)].reshape(8 * rows, size)
@@ -1042,18 +1056,18 @@
         if n == 0:
             chain_up(0)
             sums.relay(0)
+            chain_up(1)
         elif n == 1:
-            chain_up(1)
+            chain_down(0)
+            chain_up(2)
             sums.relay(1)
             tokens.start()
-            chain_up(2)
-            chain_down(0)
-
-    weight_grad(dpre, h2_all, 0, lambda n: None)
+
+    weight_grad(dpre, h2_all, 0, lambda n: sums.send_far() if n == 0 else None)
     weight_grad(act, dm_all, hidden_units, visit)
     main.finish()
+    chain_down(1)
     chain_up(3)
-    chain_down(1)
     output_blocks(0, 3)
     chain_up(4)
     chain_down(2)
@@ -1063,6 +1077,8 @@
     sums.finish()
     grant(1)
     loads["again"].start()
+    chain_down(3)
+    chain_up(5)
 
     bundle[...] = jnp.zeros_like(bundle)
 
@@ -1072,11 +1088,6 @@
     SUM_PROJ, SUM_FC2 = 6 * samples, 6 * samples + 1
 
     def second_back(s, at):
-        @pl.when(at.start == rows // 2)
-        def _():
-            chain_up(5)
-            chain_down(3)
-
         hat, inv = normed(mixed[at])
         up_grad = tmp[at]
         value = grad[at] + norm_back(up_grad * (1.0 + mod[s, 4:5, :]), hat, inv)
@@ -1090,6 +1101,7 @@
         add_row(SUM_FC2, (mod[s, 5:6, :] * grad[at]).astype(BF16).astype(F32))
 
     by_rows(samples, keep, second_back)
+    chain_up(6)
     chain_down(4)
     outward.finish()
     proj_z.finish()
@@ -1120,13 +1132,14 @@
                 dq[lax.div(chunk, 3), at, pl.ds(s * keep, keep)] = lists[i][s]
 
     visits = {
-        (0, 0): ((6,), ()),
-        (0, 1): ((7,), (5,)),
-        (1, 1): ((8,), (6,)),
-        (2, 0): ((9,), (7,)),
-        (2, 1): ((10,), ()),
-        (3, 0): ((), (8,)),
-        (3, 1): ((11,), (9,)),
+        (0, 0): ((), (5,)),
+        (0, 1): ((7,), ()),
+        (1, 0): ((8,), (6,)),
+        (1, 1): ((9,), ()),
+        (2, 0): ((), (7,)),
+        (2, 1): ((10,), (8,)),
+        (3, 0): ((11,), ()),
+        (3, 1): ((), (9,)),
     }
 
     @pl.loop(0, 4)
@@ -1358,9 +1371,10 @@
             shape((8,) + wq.shape, BF16),
             *[shape(dims, kind) for dims, kind in over_z],
         ],
-        in_specs=[SMEM] * 3 + [ANY] * 7 + [VMEM] * 8,
+        in_specs=[SMEM] * 3 + [ANY] * 15,
         out_specs=[ANY] * 9,
         scratch_shapes=[
+            *[room(array.shape, array.dtype) for array in (*biases, kept, class_table, time_table)],
             *[room(dims, kind) for dims, kind in over_z],
             room((8,) + wq.shape, BF16),
             room((8,) + wp.shape, BF16),
@@ -1402,7 +1416,7 @@
             pltpu.SemaphoreType.DMA((sends,)),
             pltpu.SemaphoreType.DMA((recvs,)),
             pltpu.SemaphoreType.REGULAR((2, 3)),
-            pltpu.SemaphoreType.DMA((21,)),
+            pltpu.SemaphoreType.DMA((29,)),
         ],
         compiler_params=params(1),
     )(labels, bands, counts, wq, wp, w1, w2, w_ada, lat, cot, *biases, kept, class_table, time_table)

time: 202 us -> 201 us (level)
  no operation moved by 1% of the time
where the time goes in v6:
time: 201 us
  Pallas kernels  200 us (100%)
    pallas_call x1, Pallas kernels, run_block(): pl.pallas_call(functools.partial(block_kernel, samples, planes), out_shap...  192 us
    pallas_call x1, Pallas kernels, place_outputs(): pl.pallas_call(functools.partial(outputs_kernel, samples, planes), out_sh...  7.72 us

profile of v6, /device:TPU:0, one launch (start us, length us, event | category | flops | bytes accessed | tf_op | source)
XLA Modules:
  0.0 201.3 jit_solution(3679481795177262310)
XLA Ops:
  1.3 192.1 %shard_map.281 = (bf16[1728,1152]{1,0:T(8,128)(2,1)}, bf16[256,1152]{1,0:T(8,128)(2,1)}, bf16[256,1152]{1,0:T(8,128)(2,1)}, bf16[8,432,1152]{2,1,0:T(8,128)(2,1)...) custom-call(s32[2]{0:T(128)} %labels_ref.1, ...), custom_call_target="tpu_custom_call" | custom-call | tf_op jit(solution)/shard_map/pallas_call | solution.py:1365
  193.4 7.7 %shard_map.282 = (bf16[2,256,1152]{2,1,0:T(8,128)(2,1)}, bf16[2,256,1152]{2,1,0:T(8,128)(2,1)}, f32[576,1152]{1,0:T(8,128)}, f32[576,1152]{1,0:T(8,128)}, f32[43...) custom-call(s32[1]{0:T(128)S(6)} %copy.32.counts_ref, ...), custom_call_target="tpu_custom_call" | custom-call | tf_op jit(solution)/shard_map/pallas_call | solution.py:1517
